TPU v7x, 128 devices: a whole 4x4x4 slice. The times are simulated.
128 devices in a mesh: panel: 4 (over z), front: 32 (over x, y, core).
Axes of the slice: x: 4, y: 4, z: 4, core: 2. Of those that a mesh axis runs over, the one named last changes fastest.
Arguments:
- source: float32 [2, 24, 32, 256, 512], P(None, None, 'panel', 'front'), may hold values from -6 to 6
- wave_term: float32 [32, 256, 512], P('panel', 'front'), may hold values from 0.5 to 2.5
- leaf_inverse: bfloat16 [2, 4, 32, 512, 512], P(None, 'panel', 'front'), may hold values from -0.1875 to 0.1875
- separator_inverse: bfloat16 [2, 4, 32, 4, 512, 512], P(None, 'panel', 'front'), may hold values from -0.1875 to 0.1875
- restrict_weight: float32 [32, 256], P('panel', 'front'), may hold values from 0.01 to 0.1
- prolong_weight: float32 [32, 256], P('panel', 'front'), may hold values from 0.05 to 0.5
Outputs:
- solution: float32 [2, 24, 32, 256, 512], P(None, None, 'panel', 'front')
- residual: float32 [2, 24, 32, 256, 512], P(None, None, 'panel', 'front')
All inputs are finite; a program needn't handle non-finite values.
Results may differ from a plain program's by a relative error of at most 0.0055.
Values may be sent and summed in bfloat16 or wider, within the bound.
No kernel may reach another device: no remote copies, remote signals or barrier semaphores. Data moves between devices by JAX's collectives and lax.ppermute only.
A program may use at most 128 MiB of HBM per device.

v0:
```python
import jax
import jax.numpy as jnp
from jax import lax
from jax.experimental import pallas as pl
from jax.experimental.pallas import tpu as pltpu
from jax.sharding import PartitionSpec as P

DAMPING = 0.25
PANELS = 4
FRONTS = 32
AXES = ("panel", "front")
BF = jnp.bfloat16
F32 = jnp.float32
PAIRS = {"A": ((0, 1), (2, 3)), "B": ((1, 2), (0, 3))}


def pairing(swaps):
    target = {}
    for one, two in swaps:
        target[one] = two
        target[two] = one
    for device in range(PANELS * FRONTS):
        target.setdefault(device, device ^ 1)
    return sorted(target.items())


def within(panels, even, odd):
    swaps = []
    for panel in panels:
        for front in range(FRONTS):
            other = front ^ (odd if front % 2 else even)
            swaps.append((panel * FRONTS + front, panel * FRONTS + other))
    return pairing(swaps)


def across(pairs, even, odd):
    swaps = []
    for one, two in pairs:
        for front in range(FRONTS):
            other = front ^ (odd if front % 2 else even)
            swaps.append((one * FRONTS + front, two * FRONTS + other))
    return pairing(swaps)


def moved(block, route):
    return lax.ppermute(block, AXES, route)


def other_core(block):
    return moved(block, pairing(()))


def swapped(block, which):
    return moved(block, across(PAIRS[which], 0, 0))


def product(block, matrix_real, matrix_imag, half):
    by_real = jnp.dot(block, matrix_real, preferred_element_type=F32)
    by_imag = jnp.dot(block, matrix_imag, preferred_element_type=F32)
    return by_real[:half] - by_imag[half:], by_imag[:half] + by_real[half:]


def leaf_kernel(source_ref, matrix_ref, weight_ref, leaf_ref, total_ref, first_ref, last_ref, low_ref, high_ref):
    count, planes, rows, width = source_ref.shape[1:]
    flat = count * planes * rows
    real = source_ref[0].reshape(flat, width).astype(BF)
    imag = source_ref[1].reshape(flat, width).astype(BF)
    dot = lambda a, b: jnp.dot(a, b, preferred_element_type=F32)
    out = (
        dot(real, matrix_ref[0]) - dot(imag, matrix_ref[1]),
        dot(real, matrix_ref[1]) + dot(imag, matrix_ref[0]),
    )
    for part in range(2):
        shaped = out[part].reshape(count, planes, rows, width)
        leaf_ref[part] = shaped
        first_ref[part] = shaped[:, 0].astype(BF)
        last_ref[part] = shaped[:, planes - 1].astype(BF)
        low_ref[part] = shaped[:, :, 0]
        high_ref[part] = shaped[:, :, rows - 1]
        total_ref[0, part] = jnp.sum(shaped * weight_ref[...][None], axis=(1, 2))


def leaf_solve(source, matrix, weights):
    two, sources, planes, rows, width = source.shape
    step = 4
    whole = pl.BlockSpec((two, step, planes, rows, width), lambda i: (0, i, 0, 0, 0))
    plane = pl.BlockSpec((two, step, rows, width), lambda i: (0, i, 0, 0))
    leaf, total, first, last, low, high = pl.pallas_call(
        leaf_kernel,
        grid=(sources // step,),
        in_specs=[
            whole,
            pl.BlockSpec((two, width, width), lambda i: (0, 0, 0)),
            pl.BlockSpec((planes, rows, width), lambda i: (0, 0, 0)),
        ],
        out_specs=[whole, pl.BlockSpec((1, two, step, width), lambda i: (i, 0, 0, 0)), plane, plane, plane, plane],
        out_shape=[
            jax.ShapeDtypeStruct(source.shape, F32),
            jax.ShapeDtypeStruct((sources // step, two, step, width), F32),
            jax.ShapeDtypeStruct((two, sources, rows, width), BF),
            jax.ShapeDtypeStruct((two, sources, rows, width), BF),
            jax.ShapeDtypeStruct((two, sources, planes, width), F32),
            jax.ShapeDtypeStruct((two, sources, planes, width), F32),
        ],
        compiler_params=pltpu.CompilerParams(vmem_limit_bytes=24 * 2**20),
        cost_estimate=pl.CostEstimate(flops=65000000, bytes_accessed=1600000, transcendentals=0),
        name="leaf_solve",
    )(source, matrix, weights)
    return leaf, total.transpose(1, 0, 2, 3).reshape(two, sources, width), first, last, low, high


def whole_call(kernel, shapes, cost, name, smem, *args):
    spaces = [pltpu.SMEM] * smem + [pltpu.VMEM] * (len(args) - smem)
    return pl.pallas_call(
        kernel,
        in_specs=[pl.BlockSpec(memory_space=space) for space in spaces],
        out_specs=[pl.BlockSpec(memory_space=pltpu.VMEM)] * len(shapes),
        out_shape=shapes,
        compiler_params=pltpu.CompilerParams(vmem_limit_bytes=16 * 2**20),
        cost_estimate=pl.CostEstimate(flops=cost, bytes_accessed=cost // 200, transcendentals=0),
        name=name,
    )(*args)


def near_kernel(own_ref, quad_ref, slab_ref, matrix_ref, out_ref):
    sources, width = own_ref.shape[1:]
    total = None
    for level, ref in enumerate((own_ref, quad_ref, slab_ref)):
        block = ref[...].reshape(2 * sources, width).astype(BF)
        got = product(block, matrix_ref[0, level], matrix_ref[1, level], sources)
        total = got if total is None else (total[0] + got[0], total[1] + got[1])
    out_ref[0] = total[0]
    out_ref[1] = total[1]


def near_part(own, quad, slab, separators):
    return whole_call(
        near_kernel, [jax.ShapeDtypeStruct(own.shape, F32)], 150000000, "near_part", 0, own, quad, slab, separators
    )[0]


def advance_kernel(
    flag_ref, scale_ref, near_ref, slab_ref, side_ref, opposite_ref, back_ref, before_ref, base_ref,
    root_ref, top_ref, low_ref, state_ref, *out_refs,
):
    sources, width = near_ref.shape[1:]
    even = flag_ref[0] == 1
    active = flag_ref[1] == 1
    keep = flag_ref[2] == 1
    mine = opposite_ref[...].astype(F32)
    other = back_ref[2].astype(F32)
    root = []
    for part in range(2):
        far = jnp.where(even, mine, other) if part == 0 else jnp.where(even, other, mine)
        root.append(slab_ref[part] + side_ref[part].astype(F32) + back_ref[part].astype(F32) + far)
    block = jnp.concatenate(root, axis=0).astype(BF)
    got = product(block, root_ref[0], root_ref[1], sources)
    state = []
    for part in range(2):
        new = near_ref[part] + got[part]
        old = before_ref[part]
        state.append(jnp.where(active, new + jnp.where(keep, old, 0.0), old))
        state_ref[part] = state[part]
    count = base_ref.shape[0]
    rows = [base_ref[i, part] + scale_ref[i] * state[part] for part in range(2) for i in range(count)]
    block = jnp.concatenate(rows, axis=0).astype(BF)
    half = width // 2
    one = product(block[:, :half], top_ref[0], top_ref[1], count * sources)
    two = product(block[:, half:], low_ref[0], low_ref[1], count * sources)
    for part in range(2):
        out = (one[part] + two[part]).astype(BF)
        for i in range(count):
            out_refs[i][part] = out[i * sources : (i + 1) * sources]


def advance(flags, scales, near, slab, got, before, bases, root_matrix, halves):
    side, opposite, back = got
    vector = jax.ShapeDtypeStruct(near.shape, BF)
    out = whole_call(
        advance_kernel, [jax.ShapeDtypeStruct(near.shape, F32)] + [vector] * bases.shape[0], 200000000, "advance", 2,
        flags, scales, near, slab, side, opposite, back, before, bases, root_matrix, *halves,
    )
    return out


def sums_kernel(first_ref, last_ref, table_ref, out_ref):
    for part in range(2):
        last = last_ref[part].astype(F32)
        first = first_ref[part].astype(F32)
        for i in range(3):
            out_ref[i, part] = jnp.sum(last * table_ref[i][None], axis=1)
        for i in range(3, 5):
            out_ref[i, part] = jnp.sum(first * table_ref[i][None], axis=1)


def edge_sums(first, last, tables):
    two, sources, rows, width = first.shape
    shape = jax.ShapeDtypeStruct((5, two, sources, width), F32)
    return whole_call(sums_kernel, [shape], 10000000, "edge_sums", 0, first, last, tables)[0]


def edges_kernel(
    flag_ref, scale_ref, low_ref, high_ref, prolong_ref, vector_ref, enter_ref, leave_ref, near_ref, far_ref
):
    sources, planes, width = low_ref.shape[1:]
    rows = enter_ref.shape[2]
    even = flag_ref[0] == 1
    depth = lax.broadcasted_iota(jnp.int32, (planes, width), 0)
    for part in range(2):
        for b in range(sources):
            vec = vector_ref[part, b]
            done = []
            for side, ref in ((0, low_ref), (1, high_ref)):
                x = 0 if side == 0 else rows - 1
                enter = enter_ref[part, b, x : x + 1] + scale_ref[0, x] * vec[1:2]
                leave = leave_ref[part, b, x : x + 1] + scale_ref[1, x] * vec[5:6] + scale_ref[2, x] * vec[6:7]
                tile = ref[part, b] + prolong_ref[side] * vec[0:1]
                tile = tile + jnp.where(depth == 0, enter, 0.0) + jnp.where(depth == planes - 1, leave, 0.0)
                done.append(tile)
            near_ref[part, b] = jnp.where(even, done[1], done[0]).astype(BF)
            far_ref[part, b] = jnp.where(even, done[0], done[1]).astype(BF)


def edge_rows(flags, scales, low, high, prolong, vectors, enter, leave):
    shape = jax.ShapeDtypeStruct(low.shape, BF)
    return whole_call(
        edges_kernel, [shape, shape], 20000000, "edge_rows", 2, flags, scales, low, high, prolong, vectors, enter, leave
    )


def final_kernel(
    leaf_ref, source_ref, wave_ref, prolong_ref, table_ref, vector_ref, enter_ref, leave_ref,
    xlow_ref, xhigh_ref, zlow_ref, zhigh_ref, field_ref, residual_ref,
):
    count, planes, rows, width = leaf_ref.shape[1:]
    column = lax.broadcasted_iota(jnp.int32, (rows, width), 1)
    row = lax.broadcasted_iota(jnp.int32, (rows, width), 0)
    below_last, above_first = table_ref[0], table_ref[1]
    own_last, own_first = prolong_ref[planes - 1], prolong_ref[0]
    for b in range(count):
        field, ends = [], []
        for part in range(2):
            vec = [vector_ref[part, b, i : i + 1] for i in range(9)]
            tiles = []
            for z in range(planes):
                tile = leaf_ref[part, b, z] + prolong_ref[z] * vec[0]
                if z == 0:
                    tile = tile + enter_ref[part, b] + below_last * vec[1]
                if z == planes - 1:
                    tile = tile + leave_ref[part, b] + above_first * vec[5] + own_last * vec[6]
                field_ref[part, b, z] = tile
                tiles.append(tile)
            field.append(tiles)
            below = zlow_ref[part, b] + below_last * (vec[3] + vec[8]) + own_first * vec[7]
            above = zhigh_ref[part, b] + above_first * vec[2] + own_last * vec[4]
            ends.append((below, above))
        for z in range(planes):
            diag_real = 6.0 - wave_ref[z]
            diag_imag = -DAMPING * wave_ref[z]
            for part in range(2):
                tiles = field[part]
                here = tiles[z]
                below = tiles[z - 1] if z else ends[part][0]
                above = tiles[z + 1] if z < planes - 1 else ends[part][1]
                near = below + above
                low = jnp.where(row == 0, xlow_ref[part, b, z].astype(F32)[None], pltpu.roll(here, 1, 0))
                high = jnp.where(row == rows - 1, xhigh_ref[part, b, z].astype(F32)[None], pltpu.roll(here, rows - 1, 0))
                near = near + low + high
                left = jnp.where(column == 0, 0.0, pltpu.roll(here, 1, 1))
                right = jnp.where(column == width - 1, 0.0, pltpu.roll(here, width - 1, 1))
                near = near + left + right
                cross = diag_imag * field[1 - part][z]
                applied = diag_real * here - near
                applied = applied - cross if part == 0 else applied + cross
                residual_ref[part, b, z] = source_ref[part, b, z] - applied


def finish(leaf, source, wave_term, prolong, tables, vectors, enter, leave, xlow, xhigh, zlow, zhigh):
    two, sources, planes, rows, width = source.shape
    step = 2
    whole = pl.BlockSpec((two, step, planes, rows, width), lambda i: (0, i, 0, 0, 0))
    plane = pl.BlockSpec((two, step, rows, width), lambda i: (0, i, 0, 0))
    fixed = pl.BlockSpec((planes, rows, width), lambda i: (0, 0, 0))
    return pl.pallas_call(
        final_kernel,
        grid=(sources // step,),
        in_specs=[
            whole, whole, fixed, fixed,
            pl.BlockSpec((2, rows, width), lambda i: (0, 0, 0)),
            pl.BlockSpec((two, step, 9, width), lambda i: (0, i, 0, 0)),
            plane, plane, plane, plane, plane, plane,
        ],
        out_specs=[whole, whole],
        out_shape=[jax.ShapeDtypeStruct(source.shape, F32)] * 2,
        compiler_params=pltpu.CompilerParams(vmem_limit_bytes=24 * 2**20),
        cost_estimate=pl.CostEstimate(flops=60000000, bytes_accessed=26000000, transcendentals=0),
        name="finish",
    )(leaf, source, wave_term, prolong, tables, vectors, enter, leave, xlow, xhigh, zlow, zhigh)


def times(block, matrix):
    shape = block.shape[1:-1]
    flat = block.astype(BF).reshape(-1, block.shape[-1])
    half = flat.shape[0] // 2
    out = jnp.stack(product(flat, matrix[0], matrix[1], half))
    return out.reshape((2,) + shape + (matrix.shape[-1],))


def after(value, *others):
    return lax.optimization_barrier((value, *others))[0]


def local(source, wave_term, leaf_inverse, separator_inverse, restrict_weight, prolong_weight):
    two, sources, planes, rows, width = source.shape
    panel = lax.axis_index("panel")
    front = lax.axis_index("front")
    even_core = front % 2 == 0
    even_panel = panel % 2 == 0
    leaf_matrix = leaf_inverse[:, 0, 0]
    separators = separator_inverse[:, 0, 0]
    root_matrix = separators[:, 3]
    half = width // 2

    def by_parity(even_value, odd_value):
        return jnp.where(even_panel, even_value, odd_value)

    weights = jnp.stack([restrict_weight, prolong_weight])
    traded_weights = {which: swapped(weights, which) for which in "AB"}
    leaf_a = [swapped(leaf_matrix[:, :half], "A")]
    leaf_a.append(swapped(after(leaf_matrix[:, half:], leaf_a[0]), "A"))
    leaf_b = [swapped(after(leaf_matrix[:, :half], leaf_a[1]), "B")]
    leaf_b.append(swapped(after(leaf_matrix[:, half:], leaf_b[0]), "B"))
    traded_leaf = {"A": leaf_a, "B": leaf_b}

    wide = lambda table: jnp.broadcast_to(table[..., None], table.shape + (width,))
    leaf, base_terms, first_plane, last_plane, low_rows, high_rows = leaf_solve(
        source, leaf_matrix, wide(restrict_weight)
    )

    def halves(block):
        return jnp.where(even_core, block[0], block[1])

    def inside(sent, panels, near, far, cross):
        side = moved(sent, within(panels, near, cross))
        opposite = moved(halves(sent), within(panels, far, far))
        back = other_core(jnp.concatenate([side, opposite[None]]))
        return side, opposite, back

    def pair_sum(terms):
        return terms.astype(F32) + other_core(terms).astype(F32)

    every = tuple(range(PANELS))
    pair = pair_sum(base_terms.astype(BF))
    side, opposite, back = inside(pair.astype(BF), every, 2, 4, 6)
    near_term = jnp.where(even_core, side, back[:2]).astype(F32)
    far_term = jnp.where(even_core, jnp.stack([opposite, back[2]]), jnp.stack([back[2], opposite])).astype(F32)
    quad = pair + near_term
    slab = pair + side.astype(F32) + back[:2].astype(F32) + far_term
    base_sums = (pair, quad, slab)
    nothing = jnp.zeros((two, sources, width), F32)

    def flags(active, keep):
        return jnp.stack([even_core, active, jnp.full((), keep)]).astype(jnp.int32)

    def close(sums, panels, active, keep, before, bases, scales, which):
        own, quad, slab = sums
        got = inside(slab.astype(BF), panels, 8, 16, 24)
        near = near_part(own, quad, slab, separators)
        return advance(flags(active, keep), scales, near, slab, got, before, bases, root_matrix, traded_leaf[which])

    def cross(terms, from_panel, to_panel):
        sent = pair_sum(terms).astype(BF)
        ends = ((from_panel, to_panel),)
        one = moved(sent, across(ends, 0, 2))
        two_ = moved(sent, across(ends, 4, 6))
        back = other_core(jnp.stack([one, two_])).astype(F32)
        one = one.astype(F32)
        own = jnp.where(even_core, one, back[0])
        quad = one + back[0]
        return own, quad, quad + two_.astype(F32) + back[1]

    restrict = {which: traded_weights[which][0] for which in "AB"}
    prolong = {which: traded_weights[which][1] for which in "AB"}
    tables = jnp.stack(
        [restrict["A"][0], restrict["B"][0], restrict_weight[-1], restrict["A"][-1], restrict["B"][-1]]
    )
    sums = edge_sums(first_plane, last_plane, wide(tables))
    onward = {"A": sums[0], "B": sums[1]}
    returning = {"A": sums[3], "B": sums[4]}
    own_scale = jnp.sum(restrict_weight[-1] * prolong_weight[-1])

    def forward_bases(which):
        scale = jnp.sum(restrict[which][0] * prolong_weight[-1])
        return jnp.stack([onward[which], nothing, sums[2]]), jnp.stack([scale, jnp.ones((), F32), own_scale])

    def backward_bases(which, brought):
        scale = jnp.sum(restrict[which][-1] * prolong_weight[0])
        return (returning[which] + brought)[None], scale[None]

    state, terms, carried, echo = close(
        base_sums, every, panel == 0, False, nothing, *forward_bases("A"), "A"
    )
    carried = jnp.where(panel == 0, carried, 0)
    echo = jnp.where(panel == 0, echo, 0)
    brought = {}
    for turn, which in enumerate("ABA"):
        target = turn + 1
        sums_now = cross(terms, turn, target)
        if turn > 0:
            brought[which] = swapped(jnp.stack([carried, echo]), which)
        total = tuple(a + b for a, b in zip(sums_now, base_sums))
        if turn < 2:
            following = "BA"[turn]
            state, terms, new_carried, new_echo = close(
                total, (target,), panel == target, False, state, *forward_bases(following), following
            )
            carried = jnp.where(panel == target, new_carried, carried)
            echo = jnp.where(panel == target, new_echo, echo)
        else:
            entered_echo = by_parity(brought["B"], brought["A"])
            entered = jnp.where(panel > 0, entered_echo[0], 0)
            echoed = entered_echo[1].astype(F32)
            state, terms = close(
                total, (target,), panel == target, False, state, *backward_bases("A", echoed), "A"
            )
    for turn, which in enumerate("ABA"):
        from_panel = PANELS - 1 - turn
        target = from_panel - 1
        sums_now = cross(terms, from_panel, target)
        following = "BAA"[turn]
        state, terms = close(
            sums_now, (target,), panel == target, True, state, *backward_bases(following, echoed), following
        )
        if turn == 1:
            traded_b = swapped(state.astype(BF), "B")
    correction = state

    by_a = swapped(by_parity(last_plane, first_plane), "A")
    by_b = swapped(by_parity(first_plane, last_plane), "B")
    below = jnp.where(panel > 0, by_parity(by_b, by_a), 0)
    above = jnp.where(panel < PANELS - 1, by_parity(by_a, by_b), 0)
    joined_a, joined_b = (jnp.concatenate(traded_leaf[which], axis=1) for which in "AB")
    upper_leaf, lower_leaf = by_parity(joined_a, joined_b), by_parity(joined_b, joined_a)
    enter = times(below, leaf_matrix)
    above_enter = times(last_plane, upper_leaf)
    zhigh = jnp.where(panel < PANELS - 1, above.astype(F32) + above_enter, 0)
    leave = times(zhigh, leaf_matrix)
    below_leave = times(first_plane.astype(F32) + enter, lower_leaf)
    zlow = jnp.where(panel > 0, below.astype(F32) + below_leave, 0)
    left_behind = jnp.where(panel < PANELS - 1, carried, 0)

    below_last = jnp.where(panel > 0, by_parity(prolong["B"], prolong["A"])[-1], 0)
    above_first = jnp.where(panel < PANELS - 1, by_parity(prolong["A"], prolong["B"])[0], 0)

    traded_a = swapped(correction.astype(BF), "A")
    upper = by_parity(traded_a, traded_b)
    lower = by_parity(traded_b, traded_a)
    out_up = times(jnp.concatenate([upper, left_behind], axis=1), leaf_matrix)
    out_down = times(jnp.concatenate([correction.astype(BF), entered], axis=1), lower_leaf)
    out_down = jnp.where(panel > 0, out_down, 0)
    pick = lambda block: (block[:, :sources], block[:, sources:])
    vectors = [correction, entered, upper, lower, left_behind, *pick(out_up), *pick(out_down)]
    vectors = jnp.stack([block.astype(F32) for block in vectors], axis=2)

    scales = jnp.stack([below_last, above_first, prolong_weight[-1]])
    ends = wide(jnp.stack([prolong_weight[:, 0], prolong_weight[:, -1]]))
    near_rows, far_rows = edge_rows(
        flags(True, True), scales, low_rows, high_rows, ends, vectors, enter, leave
    )
    near_front = other_core(near_rows)
    chain = [(p * FRONTS + f, p * FRONTS + (f + 1) % FRONTS) for p in range(PANELS) for f in range(1, FRONTS, 2)]
    far_front = moved(far_rows, pairing(chain))
    xlow = jnp.where(even_core, jnp.where(front > 0, far_front, 0), near_front)
    xhigh = jnp.where(even_core, near_front, jnp.where(front < FRONTS - 1, far_front, 0))
    return tuple(
        finish(
            leaf, source, wave_term, wide(prolong_weight), wide(jnp.stack([below_last, above_first])), vectors,
            enter, leave, xlow, xhigh, zlow, zhigh,
        )
    )


def solution(mesh):
    placed = (
        P(None, None, "panel", "front", None),
        P("panel", "front", None),
        P(None, "panel", "front", None, None),
        P(None, "panel", "front", None, None, None),
        P("panel", "front"),
        P("panel", "front"),
    )
    return jax.shard_map(
        local,
        mesh=mesh,
        in_specs=placed,
        out_specs=(P(None, None, "panel", "front", None), P(None, None, "panel", "front", None)),
        check_vma=False,
    )
```

profile of v0, /device:TPU:0, one launch (start us, length us, event | category | flops | bytes accessed | tf_op | source)
XLA Modules:
  0.0 227.0 jit_solution(11601132940863039581)
XLA Ops:
  1.4 2.0 collective-permute-start.1
  3.4 2.5 %collective-permute-start = (f32[2,8,8]{2,1,0:T(8,128)S(1)}, f32[2,8,8]{2,1,0:T(8,128)S(1)}, u32[]{:S(2)}, u32[]{:S(2)}) collective-permute-start(f32[2,8,8]{2,1,0:T(8,128)S(1)} %pad_maximum_fusion.23), channel_id=1, source_target_pairs={{0,96},{1,97},{2,98},{3,99},{4,100},{5,101},{6,102},{7,103},{8,104... | collective-permute-start | bytes 1544 | tf_op jit(solution)/shard_map/ppermute | solution.py:46
  5.9 2.3 fusion.98
  8.2 1.0 collective-permute-start.9
  10.0 1.2 copy-done.1
  11.2 2.8 %copy-done.3 = f32[2,24,8,8,512]{4,3,2,1,0:T(8,128)S(1)} copy-done((f32[2,24,8,8,512]{4,3,2,1,0:T(8,128)S(1)}, f32[2,24,8,8,512]{4,3,2,1,0:T(8,128)}, u32[]{:S(2)}) %copy-start.3) | copy-done | bytes 6291480
  14.0 5.7 %leaf_solve.1 = (f32[2,24,8,8,512]{4,3,2,1,0:T(8,128)S(1)}, f32[6,2,4,512]{3,2,1,0:T(4,128)S(1)}, bf16[2,24,8,512]{3,2,1,0:T(8,128)(2,1)S(1)}, bf16[2,24,8,512]{...) custom-call(f32[2,24,8,8,512]{4,3,2,1,0:T(8,128)S(1)} %copy-done.3, ...), custom_call_target="tpu_custom_call" | custom-call | flops 65000000 | bytes 1600000 | tf_op jit(solution)/shard_map/leaf_solve/pallas_call | solution.py:88
  19.7 2.7 %copy-done.8 = f32[2,24,8,8,512]{4,3,2,1,0:T(8,128)} copy-done((f32[2,24,8,8,512]{4,3,2,1,0:T(8,128)}, f32[2,24,8,8,512]{4,3,2,1,0:T(8,128)S(1)}, u32[]{:S(2)}) %copy-start.8) | copy-done | bytes 6291480
  24.4 1.0 collective-permute-start.60
  26.1 2.6 %copy.30 = bf16[2,1,1,4,512,512]{5,4,0,3,2,1:T(8,128)(2,1)S(1)} copy(bf16[2,1,1,4,512,512]{5,4,3,2,1,0:T(8,128)(2,1)} %param.9) | data formatting | bytes 8388608 | tf_op args[3]
  30.5 1.1 edge_sums.1
  31.7 1.7 collective-permute-start.3
  33.3 2.9 %collective-permute-start.4 = (bf16[24,512]{1,0:T(8,128)(2,1)S(1)}, bf16[24,512]{1,0:T(8,128)(2,1)S(1)}, u32[]{:S(2)}, u32[]{:S(2)}) collective-permute-start(bf16[24,512]{1,0:T(8,128)(2,1)S(1)} %fusion.63), channel_id=1, source_target_pairs={{0,4},{1,5},{2,6},{3,7},{4,0},{5,1},{6,2},{7,3},{8,12},{9,13},{10,... | collective-permute-start | bytes 73736 | tf_op jit(solution)/shard_map/ppermute | solution.py:46
  36.4 2.5 %collective-permute-done.4 = bf16[24,512]{1,0:T(8,128)(2,1)S(1)} collective-permute-done((bf16[24,512]{1,0:T(8,128)(2,1)S(1)}, bf16[24,512]{1,0:T(8,128)(2,1)S(1)}, u32[]{:S(2)}, u32[]{:S(2)}) %collective-permute-start.4) | collective-permute-done | bytes 24608 | tf_op jit(solution)/shard_map/ppermute | solution.py:46
  39.1 1.1 collective-permute-done.5
  40.3 1.6 collective-permute-start.6
  42.0 2.7 %collective-permute-start.7 = (bf16[24,512]{1,0:T(8,128)(2,1)S(1)}, bf16[24,512]{1,0:T(8,128)(2,1)S(1)}, u32[]{:S(2)}, u32[]{:S(2)}) collective-permute-start(bf16[24,512]{1,0:T(8,128)(2,1)S(1)} %fusion.62), channel_id=1, source_target_pairs={{0,16},{1,17},{2,18},{3,19},{4,20},{5,21},{6,22},{7,23},{8,24},{9,... | collective-permute-start | bytes 73736 | tf_op jit(solution)/shard_map/ppermute | solution.py:46
  44.7 1.4 fusion.77
  46.1 1.4 collective-permute-done.7.opposite_ref
  47.7 1.3 fusion.73.scale_ref
  49.7 7.0 %collective-permute-done.10.low_ref = bf16[2,256,512]{2,1,0:T(8,128)(2,1)S(1)} collective-permute-done((bf16[2,256,512]{2,1,0:T(8,128)(2,1)}, bf16[2,256,512]{2,1,0:T(8,128)(2,1)S(1)}, u32[]{:S(2)}, u32[]{:S(2)}) %collective-permute-start.10) | collective-permute-done | bytes 524320 | tf_op jit(solution)/shard_map/ppermute | solution.py:46
  56.7 1.1 advance.7
  58.0 2.5 %collective-permute-start.18 = (bf16[2,256,512]{2,1,0:T(8,128)(2,1)}, bf16[2,256,512]{2,1,0:T(8,128)(2,1)S(1)}, u32[]{:S(2)}, u32[]{:S(2)}) collective-permute-start(bf16[2,256,512]{2,1,0:T(8,128)(2,1)} %get-tuple-element.39), channel_id=1, source_target_pairs={{0,96},{1,97},{2,98},{3,99},{4,100},{5,101},{6,102},{7,103},{8,104... | collective-permute-start | bytes 1572872 | tf_op jit(solution)/shard_map/ppermute | solution.py:46
  60.6 2.1 collective-permute-start.13
  62.7 2.2 collective-permute-start.12
  64.9 2.4 %collective-permute-done.13 = bf16[2,24,512]{2,1,0:T(8,128)(2,1)S(1)} collective-permute-done((bf16[2,24,512]{2,1,0:T(8,128)(2,1)S(1)}, bf16[2,24,512]{2,1,0:T(8,128)(2,1)S(1)}, u32[]{:S(2)}, u32[]{:S(2)}) %collective-permute-start.13) | collective-permute-done | bytes 49184 | tf_op jit(solution)/shard_map/ppermute | solution.py:46
  67.6 1.3 collective-permute-done.14
  69.0 4.8 %collective-permute-done.18.top_ref = bf16[2,256,512]{2,1,0:T(8,128)(2,1)S(1)} collective-permute-done((bf16[2,256,512]{2,1,0:T(8,128)(2,1)}, bf16[2,256,512]{2,1,0:T(8,128)(2,1)S(1)}, u32[]{:S(2)}, u32[]{:S(2)}) %collective-permute-start.18) | collective-permute-done | bytes 524320 | tf_op jit(solution)/shard_map/ppermute | solution.py:46
  73.7 2.5 %collective-permute-start.19 = (bf16[2,256,512]{2,1,0:T(8,128)(2,1)S(1)}, bf16[2,256,512]{2,1,0:T(8,128)(2,1)S(1)}, u32[]{:S(2)}, u32[]{:S(2)}) collective-permute-start(bf16[2,256,512]{2,1,0:T(8,128)(2,1)S(1)} %copy-done.17), channel_id=1, source_target_pairs={{0,96},{1,97},{2,98},{3,99},{4,100},{5,101},{6,102},{7,103},{8,104... | collective-permute-start | bytes 1572872 | tf_op jit(solution)/shard_map/ppermute | solution.py:46
  78.0 1.3 fusion.74.scale_ref
  80.0 8.4 %collective-permute-done.19.low_ref = bf16[2,256,512]{2,1,0:T(8,128)(2,1)S(1)} collective-permute-done((bf16[2,256,512]{2,1,0:T(8,128)(2,1)S(1)}, bf16[2,256,512]{2,1,0:T(8,128)(2,1)S(1)}, u32[]{:S(2)}, u32[]{:S(2)}) %collective-permute-start.19) | collective-permute-done | bytes 524320 | tf_op jit(solution)/shard_map/ppermute | solution.py:46
  88.4 1.1 advance.8
  89.7 1.1 select_select_fusion.2
  96.9 1.1 advance.9
  100.0 11.6 %collective-permute-start.34 = (bf16[2,2,24,512]{3,2,1,0:T(8,128)(2,1)S(1)}, bf16[2,2,24,512]{3,2,1,0:T(8,128)(2,1)S(1)}, u32[]{:S(2)}, u32[]{:S(2)}) collective-permute-start(bf16[2,2,24,512]{3,2,1,0:T(8,128)(2,1)S(1)} %pad_maximum_fusion.8), channel_id=1, source_target_pairs={{0,96},{1,97},{2,98},{3,99},{4,100},{5,101},{6,102},{7,103},{8,104... | collective-permute-start | bytes 294920 | tf_op jit(solution)/shard_map/ppermute | solution.py:46
  111.7 1.5 collective-permute-start.35
  114.2 2.8 %collective-permute-done.35 = bf16[2,2,24,512]{3,2,1,0:T(8,128)(2,1)S(1)} collective-permute-done((bf16[2,2,24,512]{3,2,1,0:T(8,128)(2,1)S(1)}, bf16[2,2,24,512]{3,2,1,0:T(8,128)(2,1)S(1)}, u32[]{:S(2)}, u32[]{:S(2)}) %collective-permute-start.35) | collective-permute-done | bytes 98336 | tf_op jit(solution)/shard_map/ppermute | solution.py:46
  118.4 1.7 advance.10
  120.3 1.0 collective-permute-done.36
  127.3 1.8 advance.11
  132.3 2.1 fusion.83
  137.6 1.6 advance.12
  140.6 27.0 %collective-permute-start.52 = (bf16[2,24,512]{2,1,0:T(8,128)(2,1)S(1)}, bf16[2,24,512]{2,1,0:T(8,128)(2,1)S(1)}, u32[]{:S(2)}, u32[]{:S(2)}) collective-permute-start(bf16[2,24,512]{2,1,0:T(8,128)(2,1)S(1)} %add_convert_fusion.1), channel_id=1, source_target_pairs={{0,36},{1,39},{2,38},{3,37},{4,32},{5,35},{6,34},{7,33},{8,44},{9,... | collective-permute-start | bytes 147464 | tf_op jit(solution)/shard_map/ppermute | solution.py:46
  167.6 1.1 add_convert_fusion
  168.7 1.0 collective-permute-done.52
  169.8 2.4 %collective-permute-done.51 = bf16[2,24,512]{2,1,0:T(8,128)(2,1)S(1)} collective-permute-done((bf16[2,24,512]{2,1,0:T(8,128)(2,1)S(1)}, bf16[2,24,512]{2,1,0:T(8,128)(2,1)S(1)}, u32[]{:S(2)}, u32[]{:S(2)}) %collective-permute-start.51) | collective-permute-done | bytes 49184 | tf_op jit(solution)/shard_map/ppermute | solution.py:46
  172.3 1.3 fusion.18
  174.3 2.0 collective-permute-start.55
  176.4 1.3 fusion.16
  177.7 2.1 collective-permute-done.55.opposite_ref
  181.1 2.3 %advance.13 = (f32[2,24,512]{2,1,0:T(8,128)S(1)}, bf16[2,24,512]{2,1,0:T(8,128)(2,1)}) custom-call(s32[3]{0:T(128)S(1)} %fusion.66.flag_ref, f32[1]{0:T(128)} %bitcast.9.scale_ref, f32[2,24,512]{2,1,0:T(8,128)S(1)} %near_part.13.near_ref, f32[2,24,512]{2,1,0:T(8,128)S(1)} %get-tuple-element.78.slab_ref, ...), custom_call_target="tpu_custom_call" | custom-call | flops 200000000 | bytes 1000000 | tf_op jit(solution)/shard_map/advance/pallas_call | solution.py:114
  185.5 2.0 collective-permute-done.57
  190.4 6.5 %stack.338.vector_ref = f32[2,24,9,512]{3,2,1,0:T(8,128)} concatenate(f32[2,24,1,512]{3,2,1,0:T(1,128)S(1)} %stack.321, f32[2,24,1,512]{3,2,1,0:T(1,128)S(1)} %copy.17, f32[2,24,1,512]{3,2,1,0:T(1,128)} %copy.18, f32[2,24,1,512]{3,2,1,0:T(1,128)} %copy.19, f32[2,24,1,512]{3,2,1,0:T(1,128)S(1)} %reshape.119, f32[2,24,1,512]{3,2,1,0:T(1,128)} %copy.20, ...), dimensions={2} | concatenate | bytes 1769472 | tf_op jit(solution)/shard_map/stack | solution.py:463
  197.0 1.4 copy-done.4
  198.4 1.1 copy-done.6
  199.5 1.1 copy-done.12
  200.6 1.1 copy-done.14
  201.8 1.5 edge_rows.1
  203.3 1.3 collective-permute-start.61
  204.6 1.5 fusion.27
  206.1 1.1 fusion.1.zlow_ref
  207.2 6.7 %collective-permute-done.61 = bf16[2,24,8,512]{3,2,1,0:T(8,128)(2,1)S(1)} collective-permute-done((bf16[2,24,8,512]{3,2,1,0:T(8,128)(2,1)S(1)}, bf16[2,24,8,512]{3,2,1,0:T(8,128)(2,1)S(1)}, u32[]{:S(2)}, u32[]{:S(2)}) %collective-permute-start.61) | collective-permute-done | bytes 393248 | tf_op jit(solution)/shard_map/ppermute | solution.py:46
  214.2 2.8 %copy-done.9 = f32[2,24,8,8,512]{4,3,2,1,0:T(8,128)S(1)} copy-done((f32[2,24,8,8,512]{4,3,2,1,0:T(8,128)S(1)}, f32[2,24,8,8,512]{4,3,2,1,0:T(8,128)}, u32[]{:S(2)}) %copy-start.9) | copy-done | bytes 6291480
  216.9 10.0 %finish.1 = (f32[2,24,8,8,512]{4,3,2,1,0:T(8,128)}, f32[2,24,8,8,512]{4,3,2,1,0:T(8,128)}) custom-call(f32[2,24,8,8,512]{4,3,2,1,0:T(8,128)S(1)} %copy-done.9, f32[2,24,8,8,512]{4,3,2,1,0:T(8,128)S(1)} %bitcast.297, f32[8,8,512]{2,1,0:T(8,128)S(1)} %copy-done.15, f32[8,8,512]{2,1,0:T(8,128)S(1)} %broadcast_in_dim.100.prolong_ref, ...), custom_call_target="tpu_custom_call" | custom-call | flops 60000000 | bytes 26000000 | tf_op jit(solution)/shard_map/finish/pallas_call | solution.py:284
  (259 shorter events, 42.3 us)
Async XLA Ops:
  1.4 28.3 %collective-permute-start.1 = (f32[2,8,8]{2,1,0:T(8,128)S(1)}, f32[2,8,8]{2,1,0:T(8,128)S(1)}, u32[]{:S(2)}, u32[]{:S(2)}) collective-permute-start(f32[2,8,8]{2,1,0:T(8,128)S(1)} %pad_maximum_fusion.23), channel_id=1, source_target_pairs={{0,32},{1,33},{2,34},{3,35},{4,36},{5,37},{6,38},{7,39},{8,40},{9,... | collective-permute-start | bytes 1544 | tf_op jit(solution)/shard_map/ppermute | solution.py:46
  3.4 27.0 %collective-permute-start = (f32[2,8,8]{2,1,0:T(8,128)S(1)}, f32[2,8,8]{2,1,0:T(8,128)S(1)}, u32[]{:S(2)}, u32[]{:S(2)}) collective-permute-start(f32[2,8,8]{2,1,0:T(8,128)S(1)} %pad_maximum_fusion.23), channel_id=1, source_target_pairs={{0,96},{1,97},{2,98},{3,99},{4,100},{5,101},{6,102},{7,103},{8,104... | collective-permute-start | bytes 1544 | tf_op jit(solution)/shard_map/ppermute | solution.py:46
  8.2 33.7 %collective-permute-start.9 = (bf16[2,256,512]{2,1,0:T(8,128)(2,1)}, bf16[2,256,512]{2,1,0:T(8,128)(2,1)S(1)}, u32[]{:S(2)}, u32[]{:S(2)}) collective-permute-start(bf16[2,256,512]{2,1,0:T(8,128)(2,1)} %get-tuple-element.39), channel_id=1, source_target_pairs={{0,32},{1,33},{2,34},{3,35},{4,36},{5,37},{6,38},{7,39},{8,40},{9,... | collective-permute-start | bytes 1572872 | tf_op jit(solution)/shard_map/ppermute | solution.py:46
  23.3 8.3 %collective-permute-start.2 = (bf16[2,24,512]{2,1,0:T(8,128)(2,1)S(1)}, bf16[2,24,512]{2,1,0:T(8,128)(2,1)S(1)}, u32[]{:S(2)}, u32[]{:S(2)}) collective-permute-start(bf16[2,24,512]{2,1,0:T(8,128)(2,1)S(1)} %convert_element_type.253), channel_id=1, source_target_pairs={{0,1},{1,0},{2,3},{3,2},{4,5},{5,4},{6,7},{7,6},{8,9},{9,8},{10,11... | collective-permute-start | bytes 147464 | tf_op jit(solution)/shard_map/ppermute | solution.py:46
  24.4 65.2 %collective-permute-start.60 = (bf16[2,24,8,512]{3,2,1,0:T(8,128)(2,1)}, bf16[2,24,8,512]{3,2,1,0:T(8,128)(2,1)}, u32[]{:S(2)}, u32[]{:S(2)}) collective-permute-start(bf16[2,24,8,512]{3,2,1,0:T(8,128)(2,1)} %get-tuple-element.110), channel_id=1, source_target_pairs={{0,32},{1,33},{2,34},{3,35},{4,36},{5,37},{6,38},{7,39},{8,40},{9,... | collective-permute-start | bytes 1179656 | tf_op jit(solution)/shard_map/ppermute | solution.py:46
  29.7 60.0 %collective-permute-start.59 = (bf16[2,24,8,512]{3,2,1,0:T(8,128)(2,1)}, bf16[2,24,8,512]{3,2,1,0:T(8,128)(2,1)}, u32[]{:S(2)}, u32[]{:S(2)}) collective-permute-start(bf16[2,24,8,512]{3,2,1,0:T(8,128)(2,1)} %get-tuple-element.111), channel_id=1, source_target_pairs={{0,96},{1,97},{2,98},{3,99},{4,100},{5,101},{6,102},{7,103},{8,104... | collective-permute-start | bytes 1179656 | tf_op jit(solution)/shard_map/ppermute | solution.py:46
  30.5 43.2 %copy-start.17 = (bf16[2,256,512]{2,1,0:T(8,128)(2,1)S(1)}, bf16[2,256,512]{2,1,0:T(8,128)(2,1)}, u32[]{:S(2)}) copy-start(bf16[2,256,512]{2,1,0:T(8,128)(2,1)} %get-tuple-element.40) | copy-start | bytes 1572868
  31.7 7.2 %collective-permute-start.3 = (bf16[2,24,512]{2,1,0:T(8,128)(2,1)S(1)}, bf16[2,24,512]{2,1,0:T(8,128)(2,1)S(1)}, u32[]{:S(2)}, u32[]{:S(2)}) collective-permute-start(bf16[2,24,512]{2,1,0:T(8,128)(2,1)S(1)} %fusion.82), channel_id=1, source_target_pairs={{0,2},{1,7},{2,0},{3,5},{4,6},{5,3},{6,4},{7,1},{8,10},{9,15},{10,... | collective-permute-start | bytes 147464 | tf_op jit(solution)/shard_map/ppermute | solution.py:46
  33.3 5.5 %collective-permute-start.4 = (bf16[24,512]{1,0:T(8,128)(2,1)S(1)}, bf16[24,512]{1,0:T(8,128)(2,1)S(1)}, u32[]{:S(2)}, u32[]{:S(2)}) collective-permute-start(bf16[24,512]{1,0:T(8,128)(2,1)S(1)} %fusion.63), channel_id=1, source_target_pairs={{0,4},{1,5},{2,6},{3,7},{4,0},{5,1},{6,2},{7,3},{8,12},{9,13},{10,... | collective-permute-start | bytes 73736 | tf_op jit(solution)/shard_map/ppermute | solution.py:46
  38.9 1.3 collective-permute-start.5
  40.3 7.3 %collective-permute-start.6 = (bf16[2,24,512]{2,1,0:T(8,128)(2,1)S(1)}, bf16[2,24,512]{2,1,0:T(8,128)(2,1)S(1)}, u32[]{:S(2)}, u32[]{:S(2)}) collective-permute-start(bf16[2,24,512]{2,1,0:T(8,128)(2,1)S(1)} %get-tuple-element.92), channel_id=1, source_target_pairs={{0,8},{1,25},{2,10},{3,27},{4,12},{5,29},{6,14},{7,31},{8,0},{9,17... | collective-permute-start | bytes 147464 | tf_op jit(solution)/shard_map/ppermute | solution.py:46
  41.8 14.8 %collective-permute-start.10 = (bf16[2,256,512]{2,1,0:T(8,128)(2,1)}, bf16[2,256,512]{2,1,0:T(8,128)(2,1)S(1)}, u32[]{:S(2)}, u32[]{:S(2)}) collective-permute-start(bf16[2,256,512]{2,1,0:T(8,128)(2,1)} %get-tuple-element.40), channel_id=1, source_target_pairs={{0,32},{1,33},{2,34},{3,35},{4,36},{5,37},{6,38},{7,39},{8,40},{9,... | collective-permute-start | bytes 1572872 | tf_op jit(solution)/shard_map/ppermute | solution.py:46
  42.0 5.5 %collective-permute-start.7 = (bf16[24,512]{1,0:T(8,128)(2,1)S(1)}, bf16[24,512]{1,0:T(8,128)(2,1)S(1)}, u32[]{:S(2)}, u32[]{:S(2)}) collective-permute-start(bf16[24,512]{1,0:T(8,128)(2,1)S(1)} %fusion.62), channel_id=1, source_target_pairs={{0,16},{1,17},{2,18},{3,19},{4,20},{5,21},{6,22},{7,23},{8,24},{9,... | collective-permute-start | bytes 73736 | tf_op jit(solution)/shard_map/ppermute | solution.py:46
  47.5 2.2 collective-permute-start.8
  57.8 2.7 %collective-permute-start.11 = (bf16[2,24,512]{2,1,0:T(8,128)(2,1)S(1)}, bf16[2,24,512]{2,1,0:T(8,128)(2,1)S(1)}, u32[]{:S(2)}, u32[]{:S(2)}) collective-permute-start(bf16[2,24,512]{2,1,0:T(8,128)(2,1)S(1)} %get-tuple-element.37), channel_id=1, source_target_pairs={{0,1},{1,0},{2,3},{3,2},{4,5},{5,4},{6,7},{7,6},{8,9},{9,8},{10,11... | collective-permute-start | bytes 147464 | tf_op jit(solution)/shard_map/ppermute | solution.py:46
  58.0 15.7 %collective-permute-start.18 = (bf16[2,256,512]{2,1,0:T(8,128)(2,1)}, bf16[2,256,512]{2,1,0:T(8,128)(2,1)S(1)}, u32[]{:S(2)}, u32[]{:S(2)}) collective-permute-start(bf16[2,256,512]{2,1,0:T(8,128)(2,1)} %get-tuple-element.39), channel_id=1, source_target_pairs={{0,96},{1,97},{2,98},{3,99},{4,100},{5,101},{6,102},{7,103},{8,104... | collective-permute-start | bytes 1572872 | tf_op jit(solution)/shard_map/ppermute | solution.py:46
  60.6 6.7 %collective-permute-start.13 = (bf16[2,24,512]{2,1,0:T(8,128)(2,1)S(1)}, bf16[2,24,512]{2,1,0:T(8,128)(2,1)S(1)}, u32[]{:S(2)}, u32[]{:S(2)}) collective-permute-start(bf16[2,24,512]{2,1,0:T(8,128)(2,1)S(1)} %add_convert_fusion.6), channel_id=1, source_target_pairs={{0,36},{1,39},{2,38},{3,37},{4,32},{5,35},{6,34},{7,33},{8,44},{9,... | collective-permute-start | bytes 147464 | tf_op jit(solution)/shard_map/ppermute | solution.py:46
  62.7 4.8 %collective-permute-start.12 = (bf16[2,24,512]{2,1,0:T(8,128)(2,1)S(1)}, bf16[2,24,512]{2,1,0:T(8,128)(2,1)S(1)}, u32[]{:S(2)}, u32[]{:S(2)}) collective-permute-start(bf16[2,24,512]{2,1,0:T(8,128)(2,1)S(1)} %add_convert_fusion.6), channel_id=1, source_target_pairs={{0,32},{1,35},{2,34},{3,33},{4,36},{5,39},{6,38},{7,37},{8,40},{9,... | collective-permute-start | bytes 147464 | tf_op jit(solution)/shard_map/ppermute | solution.py:46
  67.5 1.4 collective-permute-start.14
  73.7 14.7 %collective-permute-start.19 = (bf16[2,256,512]{2,1,0:T(8,128)(2,1)S(1)}, bf16[2,256,512]{2,1,0:T(8,128)(2,1)S(1)}, u32[]{:S(2)}, u32[]{:S(2)}) collective-permute-start(bf16[2,256,512]{2,1,0:T(8,128)(2,1)S(1)} %copy-done.17), channel_id=1, source_target_pairs={{0,96},{1,97},{2,98},{3,99},{4,100},{5,101},{6,102},{7,103},{8,104... | collective-permute-start | bytes 1572872 | tf_op jit(solution)/shard_map/ppermute | solution.py:46
  76.2 1.4 collective-permute-start.15
  76.2 1.4 collective-permute-start.16
  77.6 2.4 %collective-permute-start.17 = (bf16[3,24,512]{2,1,0:T(8,128)(2,1)S(1)}, bf16[3,24,512]{2,1,0:T(8,128)(2,1)S(1)}, u32[]{:S(2)}, u32[]{:S(2)}) collective-permute-start(bf16[3,24,512]{2,1,0:T(8,128)(2,1)S(1)} %pad_maximum_fusion.17), channel_id=1, source_target_pairs={{0,1},{1,0},{2,3},{3,2},{4,5},{5,4},{6,7},{7,6},{8,9},{9,8},{10,11... | collective-permute-start | bytes 221192 | tf_op jit(solution)/shard_map/ppermute | solution.py:46
  89.5 1.3 collective-permute-start.20
  90.9 1.3 collective-permute-start.22
  91.3 1.2 collective-permute-start.21
  92.6 1.4 collective-permute-start.23
  94.0 1.6 collective-permute-start.24
  94.4 1.2 collective-permute-start.25
  95.6 1.3 collective-permute-start.26
  98.1 1.3 collective-permute-start.27
  99.4 12.2 %collective-permute-start.29 = (bf16[2,24,512]{2,1,0:T(8,128)(2,1)S(1)}, bf16[2,24,512]{2,1,0:T(8,128)(2,1)S(1)}, u32[]{:S(2)}, u32[]{:S(2)}) collective-permute-start(bf16[2,24,512]{2,1,0:T(8,128)(2,1)S(1)} %add_convert_fusion.4), channel_id=1, source_target_pairs={{0,1},{1,0},{2,3},{3,2},{4,5},{5,4},{6,7},{7,6},{8,9},{9,8},{10,11... | collective-permute-start | bytes 147464 | tf_op jit(solution)/shard_map/ppermute | solution.py:46
  99.7 11.9 %collective-permute-start.28 = (bf16[2,24,512]{2,1,0:T(8,128)(2,1)S(1)}, bf16[2,24,512]{2,1,0:T(8,128)(2,1)S(1)}, u32[]{:S(2)}, u32[]{:S(2)}) collective-permute-start(bf16[2,24,512]{2,1,0:T(8,128)(2,1)S(1)} %add_convert_fusion.4), channel_id=1, source_target_pairs={{0,1},{1,0},{2,3},{3,2},{4,5},{5,4},{6,7},{7,6},{8,9},{9,8},{10,11... | collective-permute-start | bytes 147464 | tf_op jit(solution)/shard_map/ppermute | solution.py:46
  100.0 14.2 %collective-permute-start.34 = (bf16[2,2,24,512]{3,2,1,0:T(8,128)(2,1)S(1)}, bf16[2,2,24,512]{3,2,1,0:T(8,128)(2,1)S(1)}, u32[]{:S(2)}, u32[]{:S(2)}) collective-permute-start(bf16[2,2,24,512]{3,2,1,0:T(8,128)(2,1)S(1)} %pad_maximum_fusion.8), channel_id=1, source_target_pairs={{0,96},{1,97},{2,98},{3,99},{4,100},{5,101},{6,102},{7,103},{8,104... | collective-permute-start | bytes 294920 | tf_op jit(solution)/shard_map/ppermute | solution.py:46
  111.6 1.6 collective-permute-start.30
  111.7 5.3 %collective-permute-start.35 = (bf16[2,2,24,512]{3,2,1,0:T(8,128)(2,1)S(1)}, bf16[2,2,24,512]{3,2,1,0:T(8,128)(2,1)S(1)}, u32[]{:S(2)}, u32[]{:S(2)}) collective-permute-start(bf16[2,2,24,512]{3,2,1,0:T(8,128)(2,1)S(1)} %pad_maximum_fusion.9), channel_id=1, source_target_pairs={{0,32},{1,33},{2,34},{3,35},{4,36},{5,37},{6,38},{7,39},{8,40},{9,... | collective-permute-start | bytes 294920 | tf_op jit(solution)/shard_map/ppermute | solution.py:46
  113.3 3.7 %collective-permute-start.31 = (bf16[2,24,512]{2,1,0:T(8,128)(2,1)S(1)}, bf16[2,24,512]{2,1,0:T(8,128)(2,1)S(1)}, u32[]{:S(2)}, u32[]{:S(2)}) collective-permute-start(bf16[2,24,512]{2,1,0:T(8,128)(2,1)S(1)} %get-tuple-element.86), channel_id=1, source_target_pairs={{0,1},{1,0},{2,3},{3,2},{4,5},{5,4},{6,7},{7,6},{8,9},{9,8},{10,11... | collective-permute-start | bytes 147464 | tf_op jit(solution)/shard_map/ppermute | solution.py:46
  113.6 3.4 %collective-permute-start.32 = (bf16[24,512]{1,0:T(8,128)(2,1)S(1)}, bf16[24,512]{1,0:T(8,128)(2,1)S(1)}, u32[]{:S(2)}, u32[]{:S(2)}) collective-permute-start(bf16[24,512]{1,0:T(8,128)(2,1)S(1)} %fusion.59), channel_id=1, source_target_pairs={{0,1},{1,0},{2,3},{3,2},{4,5},{5,4},{6,7},{7,6},{8,9},{9,8},{10,11... | collective-permute-start | bytes 73736 | tf_op jit(solution)/shard_map/ppermute | solution.py:46
  117.1 1.3 collective-permute-start.33
  120.1 1.3 collective-permute-start.36
  121.4 1.3 collective-permute-start.38
  121.6 1.2 collective-permute-start.37
  122.9 1.4 collective-permute-start.39
  124.3 1.6 collective-permute-start.40
  124.8 1.2 collective-permute-start.41
  126.0 1.3 collective-permute-start.42
  129.1 1.3 collective-permute-start.43
  130.4 1.3 collective-permute-start.45
  130.8 1.2 collective-permute-start.44
  132.0 2.4 %collective-permute-start.46 = (bf16[2,2,24,512]{3,2,1,0:T(8,128)(2,1)S(1)}, bf16[2,2,24,512]{3,2,1,0:T(8,128)(2,1)S(1)}, u32[]{:S(2)}, u32[]{:S(2)}) collective-permute-start(bf16[2,2,24,512]{3,2,1,0:T(8,128)(2,1)S(1)} %pad_maximum_fusion.11), channel_id=1, source_target_pairs={{0,1},{1,0},{2,3},{3,2},{4,5},{5,4},{6,7},{7,6},{8,9},{9,8},{10,11... | collective-permute-start | bytes 294920 | tf_op jit(solution)/shard_map/ppermute | solution.py:46
  134.5 1.6 collective-permute-start.47
  134.9 1.2 collective-permute-start.48
  136.1 1.6 collective-permute-start.49
  139.3 1.3 collective-permute-start.50
  140.6 29.1 %collective-permute-start.52 = (bf16[2,24,512]{2,1,0:T(8,128)(2,1)S(1)}, bf16[2,24,512]{2,1,0:T(8,128)(2,1)S(1)}, u32[]{:S(2)}, u32[]{:S(2)}) collective-permute-start(bf16[2,24,512]{2,1,0:T(8,128)(2,1)S(1)} %add_convert_fusion.1), channel_id=1, source_target_pairs={{0,36},{1,39},{2,38},{3,37},{4,32},{5,35},{6,34},{7,33},{8,44},{9,... | collective-permute-start | bytes 147464 | tf_op jit(solution)/shard_map/ppermute | solution.py:46
  167.6 4.6 %collective-permute-start.51 = (bf16[2,24,512]{2,1,0:T(8,128)(2,1)S(1)}, bf16[2,24,512]{2,1,0:T(8,128)(2,1)S(1)}, u32[]{:S(2)}, u32[]{:S(2)}) collective-permute-start(bf16[2,24,512]{2,1,0:T(8,128)(2,1)S(1)} %add_convert_fusion.1), channel_id=1, source_target_pairs={{0,32},{1,35},{2,34},{3,33},{4,36},{5,39},{6,38},{7,37},{8,40},{9,... | collective-permute-start | bytes 147464 | tf_op jit(solution)/shard_map/ppermute | solution.py:46
  172.2 1.4 collective-permute-start.53
  173.7 6.1 %collective-permute-start.54 = (bf16[2,24,512]{2,1,0:T(8,128)(2,1)S(1)}, bf16[2,24,512]{2,1,0:T(8,128)(2,1)S(1)}, u32[]{:S(2)}, u32[]{:S(2)}) collective-permute-start(bf16[2,24,512]{2,1,0:T(8,128)(2,1)S(1)} %get-tuple-element.77), channel_id=1, source_target_pairs={{0,8},{1,25},{2,10},{3,27},{4,12},{5,29},{6,14},{7,31},{8,0},{9,17... | collective-permute-start | bytes 147464 | tf_op jit(solution)/shard_map/ppermute | solution.py:46
  174.3 5.4 %collective-permute-start.55 = (bf16[24,512]{1,0:T(8,128)(2,1)S(1)}, bf16[24,512]{1,0:T(8,128)(2,1)S(1)}, u32[]{:S(2)}, u32[]{:S(2)}) collective-permute-start(bf16[24,512]{1,0:T(8,128)(2,1)S(1)} %fusion.56), channel_id=1, source_target_pairs={{0,16},{1,17},{2,18},{3,19},{4,20},{5,21},{6,22},{7,23},{8,24},{9,... | collective-permute-start | bytes 73736 | tf_op jit(solution)/shard_map/ppermute | solution.py:46
  179.7 1.3 collective-permute-start.56
  180.0 5.5 %collective-permute-start.58 = (bf16[2,24,512]{2,1,0:T(8,128)(2,1)S(1)}, bf16[2,24,512]{2,1,0:T(8,128)(2,1)S(1)}, u32[]{:S(2)}, u32[]{:S(2)}) collective-permute-start(bf16[2,24,512]{2,1,0:T(8,128)(2,1)S(1)} %convert_element_type.308), channel_id=1, source_target_pairs={{0,96},{1,97},{2,98},{3,99},{4,100},{5,101},{6,102},{7,103},{8,104... | collective-permute-start | bytes 147464 | tf_op jit(solution)/shard_map/ppermute | solution.py:46
  183.4 4.2 %collective-permute-start.57 = (bf16[2,24,512]{2,1,0:T(8,128)(2,1)S(1)}, bf16[2,24,512]{2,1,0:T(8,128)(2,1)S(1)}, u32[]{:S(2)}, u32[]{:S(2)}) collective-permute-start(bf16[2,24,512]{2,1,0:T(8,128)(2,1)S(1)} %convert_element_type.307), channel_id=1, source_target_pairs={{0,32},{1,33},{2,34},{3,35},{4,36},{5,37},{6,38},{7,39},{8,40},{9,... | collective-permute-start | bytes 147464 | tf_op jit(solution)/shard_map/ppermute | solution.py:46
  203.3 10.6 %collective-permute-start.61 = (bf16[2,24,8,512]{3,2,1,0:T(8,128)(2,1)S(1)}, bf16[2,24,8,512]{3,2,1,0:T(8,128)(2,1)S(1)}, u32[]{:S(2)}, u32[]{:S(2)}) collective-permute-start(bf16[2,24,8,512]{3,2,1,0:T(8,128)(2,1)S(1)} %get-tuple-element.60), channel_id=1, source_target_pairs={{0,31},{1,2},{2,1},{3,4},{4,3},{5,6},{6,5},{7,8},{8,7},{9,10},{10,... | collective-permute-start | bytes 1179656 | tf_op jit(solution)/shard_map/ppermute | solution.py:46
  204.6 9.3 %collective-permute-start.62 = (bf16[2,24,8,512]{3,2,1,0:T(8,128)(2,1)S(1)}, bf16[2,24,8,512]{3,2,1,0:T(8,128)(2,1)S(1)}, u32[]{:S(2)}, u32[]{:S(2)}) collective-permute-start(bf16[2,24,8,512]{3,2,1,0:T(8,128)(2,1)S(1)} %get-tuple-element.61), channel_id=1, source_target_pairs={{0,1},{1,0},{2,3},{3,2},{4,5},{5,4},{6,7},{7,6},{8,9},{9,8},{10,11... | collective-permute-start | bytes 1179656 | tf_op jit(solution)/shard_map/ppermute | solution.py:46
  (20 other events, 231.6 us)
where the time goes:
time: 228 us; the launch traced here: 227 us
  starting transfers between devices  80.2 us (35%)
  waiting for transfers between devices  58.3 us (26%)
  Pallas kernels  33.6 us (15%)
  local copies, waits for them, and re-layouts  32.9 us (14%)
  other arithmetic  14.9 us (7%)
  matrix products  5.55 us (2%)
    ppermute x63, starting transfers between devices, moved(): return lax.ppermute(block, AXES, route)  80.2 us
    ppermute x63, waiting for transfers between devices, moved(): return lax.ppermute(block, AXES, route)  58.3 us
    unnamed x45, local copies, waits for them, and re-layouts  17.9 us
    pallas_call x16, Pallas kernels, whole_call(): pl.pallas_call(kernel, in_specs=[pl.BlockSpec(memory_space=space) for spa...  17.9 us
    another operation x9, local copies, waits for them, and re-layouts, local(): vectors = jnp.stack([block.astype(F32) for block in vectors], axis=2)  10.3 us
    pallas_call x1, Pallas kernels, finish(): pl.pallas_call(final_kernel, grid=(sources // step,), in_specs=[whole, wh...  10 us
    pallas_call x1, Pallas kernels, leaf_solve(): pl.pallas_call(leaf_kernel, grid=(sources // step,), in_specs=[whole, pl....  5.68 us
  transfers between devices with their start and end apart: 63, of which 37 were waited for; matrix products, arithmetic and copies ran while one was open for 12% of the time, Pallas kernels for 7%

commit v1 on v0

v1 whole, which is shorter than its diff:
```python
import functools

import jax
import jax.numpy as jnp
from jax import lax
from jax.experimental import pallas as pl
from jax.experimental.pallas import tpu as pltpu
from jax.sharding import PartitionSpec as P

DAMPING = 0.25
PANELS = 4
FRONTS = 32
AXES = ("panel", "front")
BF = jnp.bfloat16
F32 = jnp.float32
PAIRS = {"A": ((0, 1), (2, 3)), "B": ((1, 2), (0, 3))}


def pairing(swaps):
    target = {}
    for one, two in swaps:
        target[one] = two
        target[two] = one
    for device in range(PANELS * FRONTS):
        target.setdefault(device, device ^ 1)
    return sorted(target.items())


def within(panels, even, odd):
    swaps = []
    for panel in panels:
        for front in range(FRONTS):
            other = front ^ (odd if front % 2 else even)
            swaps.append((panel * FRONTS + front, panel * FRONTS + other))
    return pairing(swaps)


def across(pairs, even, odd):
    swaps = []
    for one, two in pairs:
        for front in range(FRONTS):
            other = front ^ (odd if front % 2 else even)
            swaps.append((one * FRONTS + front, two * FRONTS + other))
    return pairing(swaps)


def moved(block, route):
    return lax.ppermute(block, AXES, route)


def other_core(block):
    return moved(block, pairing(()))


def swapped(block, which):
    return moved(block, across(PAIRS[which], 0, 0))


def product(block, matrix_real, matrix_imag, half):
    by_real = jnp.dot(block, matrix_real, preferred_element_type=F32)
    by_imag = jnp.dot(block, matrix_imag, preferred_element_type=F32)
    return by_real[:half] - by_imag[half:], by_imag[:half] + by_real[half:]


def column(scalars, width):
    row = lax.broadcasted_iota(jnp.int32, (len(scalars), 128), 0)
    tile = jnp.full((len(scalars), 128), scalars[0])
    for i in range(1, len(scalars)):
        tile = jnp.where(row == i, scalars[i], tile)
    return jnp.concatenate([tile] * (width // 128), axis=1)


def dotted(one, two):
    total = one[0] * two[0]
    for a, b in zip(one[1:], two[1:]):
        total = total + a * b
    return total


def entries(ref, kind, plane):
    return [ref[kind, plane, x] for x in range(ref.shape[2])]


def leaf_kernel(weight_ref, source_ref, matrix_ref, leaf_ref, total_ref, first_ref, last_ref, low_ref, high_ref):
    count, planes, rows, width = source_ref.shape[1:]
    flat = count * planes * rows
    real = source_ref[0].reshape(flat, width).astype(BF)
    imag = source_ref[1].reshape(flat, width).astype(BF)
    dot = lambda a, b: jnp.dot(a, b, preferred_element_type=F32)
    out = (
        dot(real, matrix_ref[0]) - dot(imag, matrix_ref[1]),
        dot(real, matrix_ref[1]) + dot(imag, matrix_ref[0]),
    )
    columns = [column(entries(weight_ref, 0, z), width) for z in range(planes)]
    for part in range(2):
        shaped = out[part].reshape(count, planes, rows, width)
        leaf_ref[part] = shaped
        first_ref[part] = shaped[:, 0].astype(BF)
        last_ref[part] = shaped[:, planes - 1].astype(BF)
        low_ref[part] = shaped[:, :, 0]
        high_ref[part] = shaped[:, :, rows - 1]
        total = shaped[:, 0] * columns[0][None]
        for z in range(1, planes):
            total = total + shaped[:, z] * columns[z][None]
        total_ref[0, part] = jnp.sum(total, axis=1)


def leaf_solve(weights, source, matrix):
    two, sources, planes, rows, width = source.shape
    step = 4
    whole = pl.BlockSpec((two, step, planes, rows, width), lambda i: (0, i, 0, 0, 0))
    plane = pl.BlockSpec((two, step, rows, width), lambda i: (0, i, 0, 0))
    leaf, total, first, last, low, high = pl.pallas_call(
        leaf_kernel,
        grid=(sources // step,),
        in_specs=[
            pl.BlockSpec(memory_space=pltpu.SMEM),
            whole,
            pl.BlockSpec((two, width, width), lambda i: (0, 0, 0)),
        ],
        out_specs=[whole, pl.BlockSpec((1, two, step, width), lambda i: (i, 0, 0, 0)), plane, plane, plane, plane],
        out_shape=[
            jax.ShapeDtypeStruct(source.shape, F32),
            jax.ShapeDtypeStruct((sources // step, two, step, width), F32),
            jax.ShapeDtypeStruct((two, sources, rows, width), BF),
            jax.ShapeDtypeStruct((two, sources, rows, width), BF),
            jax.ShapeDtypeStruct((two, sources, planes, width), F32),
            jax.ShapeDtypeStruct((two, sources, planes, width), F32),
        ],
        compiler_params=pltpu.CompilerParams(vmem_limit_bytes=58 * 2**20),
        cost_estimate=pl.CostEstimate(flops=65000000, bytes_accessed=1600000, transcendentals=0),
        name="leaf_solve",
    )(weights, source, matrix)
    return leaf, total.transpose(1, 0, 2, 3).reshape(two, sources, width), first, last, low, high


def whole_call(kernel, shapes, cost, name, smem, *args):
    spaces = [pltpu.SMEM] * smem + [pltpu.VMEM] * (len(args) - smem)
    return pl.pallas_call(
        kernel,
        in_specs=[pl.BlockSpec(memory_space=space) for space in spaces],
        out_specs=[pl.BlockSpec(memory_space=pltpu.VMEM)] * len(shapes),
        out_shape=shapes,
        compiler_params=pltpu.CompilerParams(vmem_limit_bytes=28 * 2**20),
        cost_estimate=pl.CostEstimate(flops=cost, bytes_accessed=cost // 200, transcendentals=0),
        name=name,
    )(*args)


def near_kernel(own_ref, quad_ref, slab_ref, matrix_ref, out_ref):
    sources, width = own_ref.shape[1:]
    total = None
    for level, ref in enumerate((own_ref, quad_ref, slab_ref)):
        block = ref[...].reshape(2 * sources, width).astype(BF)
        got = product(block, matrix_ref[0, level], matrix_ref[1, level], sources)
        total = got if total is None else (total[0] + got[0], total[1] + got[1])
    out_ref[0] = total[0]
    out_ref[1] = total[1]


def near_part(own, quad, slab, separators):
    return whole_call(
        near_kernel, [jax.ShapeDtypeStruct(own.shape, F32)], 150000000, "near_part", 0, own, quad, slab, separators
    )[0]


def advanced(target, keep, place_ref, near_ref, slab_ref, side_ref, opposite_ref, back_ref, before_ref, root_ref, state_ref):
    sources, width = near_ref.shape[1:]
    even = place_ref[0] == 1
    active = place_ref[1] == target
    mine = opposite_ref[...].astype(F32)
    other = back_ref[2].astype(F32)
    root = []
    for part in range(2):
        far = jnp.where(even, mine, other) if part == 0 else jnp.where(even, other, mine)
        root.append(slab_ref[part] + side_ref[part].astype(F32) + back_ref[part].astype(F32) + far)
    block = jnp.concatenate(root, axis=0).astype(BF)
    got = product(block, root_ref[0], root_ref[1], sources)
    state = []
    for part in range(2):
        old = before_ref[part]
        new = near_ref[part] + got[part]
        if keep:
            new = new + old
        state.append(jnp.where(active, new, old))
        state_ref[part] = state[part]
    return state, active


def forward_kernel(
    target, which, place_ref, own_ref, traded_ref, near_ref, slab_ref, side_ref, opposite_ref, back_ref, before_ref,
    root_ref, leaf_ref, sums_ref, parcel_ref, state_ref, terms_ref, out_ref,
):
    state, active = advanced(
        target, False, place_ref, near_ref, slab_ref, side_ref, opposite_ref, back_ref, before_ref, root_ref, state_ref
    )
    sources = near_ref.shape[1]
    end = own_ref.shape[1] - 1
    scale = dotted(entries(traded_ref, 0, 0), entries(own_ref, 1, end))
    own_scale = dotted(entries(own_ref, 0, end), entries(own_ref, 1, end))
    rows = []
    for part in range(2):
        here = state[part]
        rows += [sums_ref["AB".index(which), part] + scale * here, here, sums_ref[2, part] + own_scale * here]
    block = jnp.concatenate(rows, axis=0).astype(BF)
    got = product(block, leaf_ref[0], leaf_ref[1], 3 * sources)
    for part in range(2):
        terms_ref[part] = got[part][:sources].astype(BF)
        for i in range(2):
            new = got[part][(i + 1) * sources : (i + 2) * sources].astype(BF)
            out_ref[i, part] = jnp.where(active, new, parcel_ref[i, part])


def backward_kernel(
    target, keep, which, place_ref, own_ref, traded_ref, near_ref, slab_ref, side_ref, opposite_ref, back_ref, before_ref,
    root_ref, leaf_ref, sums_ref, by_a_ref, by_b_ref, state_ref, terms_ref,
):
    state, _ = advanced(
        target, keep, place_ref, near_ref, slab_ref, side_ref, opposite_ref, back_ref, before_ref, root_ref, state_ref
    )
    sources = near_ref.shape[1]
    end = own_ref.shape[1] - 1
    even_panel = lax.rem(place_ref[1], 2) == 0
    scale = dotted(entries(traded_ref, 0, end), entries(own_ref, 1, 0))
    rows = []
    for part in range(2):
        echo = jnp.where(even_panel, by_b_ref[1, part], by_a_ref[1, part]).astype(F32)
        rows.append(sums_ref[3 + "AB".index(which), part] + echo + scale * state[part])
    block = jnp.concatenate(rows, axis=0).astype(BF)
    got = product(block, leaf_ref[0], leaf_ref[1], sources)
    for part in range(2):
        terms_ref[part] = got[part].astype(BF)


def last_kernel(
    target, place_ref, near_ref, slab_ref, side_ref, opposite_ref, back_ref, before_ref, root_ref, state_ref
):
    advanced(
        target, True, place_ref, near_ref, slab_ref, side_ref, opposite_ref, back_ref, before_ref, root_ref, state_ref
    )


def sums_kernel(own_ref, by_a_ref, by_b_ref, first_ref, last_ref, out_ref):
    width = first_ref.shape[3]
    end = own_ref.shape[1] - 1
    tables = [
        (last_ref, column(entries(by_a_ref, 0, 0), width)),
        (last_ref, column(entries(by_b_ref, 0, 0), width)),
        (last_ref, column(entries(own_ref, 0, end), width)),
        (first_ref, column(entries(by_a_ref, 0, end), width)),
        (first_ref, column(entries(by_b_ref, 0, end), width)),
    ]
    for part in range(2):
        for i, (ref, table) in enumerate(tables):
            out_ref[i, part] = jnp.sum(ref[part].astype(F32) * table[None], axis=1)


def planes_kernel(
    place_ref, by_a_ref, by_b_ref, first_ref, last_ref, own_ref, leaf_a_ref, leaf_b_ref,
    enter_ref, leave_ref, zlow_ref, zhigh_ref,
):
    two, sources, rows, width = first_ref.shape
    flat = sources * rows
    panel = place_ref[1]
    even = lax.rem(panel, 2) == 0
    lower = panel > 0
    upper = panel < PANELS - 1

    def stacked(parts):
        return jnp.concatenate([part.reshape(flat, width) for part in parts], axis=0).astype(BF)

    def times(parts, matrix):
        return [part.reshape(sources, rows, width) for part in product(stacked(parts), matrix[0], matrix[1], flat)]

    below = [jnp.where(even, by_b_ref[part], by_a_ref[part]).astype(F32) for part in range(2)]
    below = [jnp.where(lower, part, 0.0) for part in below]
    above = [jnp.where(even, by_a_ref[part], by_b_ref[part]).astype(F32) for part in range(2)]
    upper_leaf = [jnp.where(even, leaf_a_ref[part], leaf_b_ref[part]) for part in range(2)]
    lower_leaf = [jnp.where(even, leaf_b_ref[part], leaf_a_ref[part]) for part in range(2)]
    own_leaf = [own_ref[0], own_ref[1]]
    enter = times(below, own_leaf)
    above_enter = times([last_ref[part].astype(F32) for part in range(2)], upper_leaf)
    zhigh = [jnp.where(upper, above[part] + above_enter[part], 0.0) for part in range(2)]
    leave = times(zhigh, own_leaf)
    below_leave = times([first_ref[part].astype(F32) + enter[part] for part in range(2)], lower_leaf)
    for part in range(2):
        enter_ref[part] = enter[part]
        leave_ref[part] = leave[part]
        zhigh_ref[part] = zhigh[part]
        zlow_ref[part] = jnp.where(lower, below[part] + below_leave[part], 0.0)


def neighbour_tables(place_ref, by_a_ref, by_b_ref, end):
    panel = place_ref[1]
    even = lax.rem(panel, 2) == 0
    pick = lambda one, two, there: jnp.where(there, jnp.where(even, one, two), 0.0)
    below = [
        pick(b, a, panel > 0) for a, b in zip(entries(by_a_ref, 1, end), entries(by_b_ref, 1, end))
    ]
    above = [
        pick(a, b, panel < PANELS - 1) for a, b in zip(entries(by_a_ref, 1, 0), entries(by_b_ref, 1, 0))
    ]
    return below, above


def closing_kernel(
    place_ref, own_w_ref, a_w_ref, b_w_ref, state_ref, got_a_ref, got_b_ref, parcel_a_ref, parcel_b_ref, parcel_ref,
    own_ref, leaf_a_ref, leaf_b_ref, low_ref, high_ref, enter_ref, leave_ref, vector_ref, near_ref, far_ref,
):
    sources, planes, width = low_ref.shape[1:]
    rows = enter_ref.shape[2]
    panel = place_ref[1]
    even_core = place_ref[0] == 1
    even = lax.rem(panel, 2) == 0
    lower = panel > 0
    upper = panel < PANELS - 1
    below_last, above_first = neighbour_tables(place_ref, a_w_ref, b_w_ref, planes - 1)
    own_last = entries(own_w_ref, 1, planes - 1)
    own_leaf = [own_ref[0], own_ref[1]]
    lower_leaf = [jnp.where(even, leaf_b_ref[part], leaf_a_ref[part]) for part in range(2)]
    here, entered, above, below, behind = [], [], [], [], []
    for part in range(2):
        here.append(state_ref[part])
        entered.append(jnp.where(lower, jnp.where(even, parcel_b_ref[0, part], parcel_a_ref[0, part]).astype(F32), 0.0))
        above.append(jnp.where(even, got_a_ref[part], got_b_ref[part]).astype(F32))
        below.append(jnp.where(even, got_b_ref[part], got_a_ref[part]).astype(F32))
        behind.append(jnp.where(upper, parcel_ref[0, part].astype(F32), 0.0))
    stacked = lambda one, two: jnp.concatenate([one[0], two[0], one[1], two[1]], axis=0).astype(BF)
    out_up = product(stacked(above, behind), own_leaf[0], own_leaf[1], 2 * sources)
    out_down = product(stacked(here, entered), lower_leaf[0], lower_leaf[1], 2 * sources)
    depth = lax.broadcasted_iota(jnp.int32, (planes, width), 0)
    ends = [column([own_w_ref[1, z, x] for z in range(planes)], width) for x in (0, rows - 1)]
    for part in range(2):
        down = jnp.where(lower, out_down[part], 0.0)
        vectors = [
            here[part], entered[part], above[part], below[part], behind[part],
            out_up[part][:sources], out_up[part][sources:], down[:sources], down[sources:],
        ]
        for i, vector in enumerate(vectors):
            vector_ref[part, i] = vector
        for b in range(sources):
            row = lambda i: vector_ref[part, i, b : b + 1]
            done = []
            for side, ref in ((0, low_ref), (1, high_ref)):
                x = 0 if side == 0 else rows - 1
                enter = enter_ref[part, b, x : x + 1] + below_last[x] * row(1)
                leave = leave_ref[part, b, x : x + 1] + above_first[x] * row(5) + own_last[x] * row(6)
                tile = ref[part, b] + ends[side] * row(0)
                tile = tile + jnp.where(depth == 0, enter, 0.0) + jnp.where(depth == planes - 1, leave, 0.0)
                done.append(tile)
            near_ref[part, b] = jnp.where(even_core, done[1], done[0]).astype(BF)
            far_ref[part, b] = jnp.where(even_core, done[0], done[1]).astype(BF)


def final_kernel(
    place_ref, own_w_ref, a_w_ref, b_w_ref, leaf_ref, source_ref, wave_ref, vector_ref, enter_ref, leave_ref,
    near_ref, far_ref, zlow_ref, zhigh_ref, field_ref, residual_ref,
):
    count, planes, rows, width = leaf_ref.shape[1:]
    lane = lax.broadcasted_iota(jnp.int32, (rows, width), 1)
    row = lax.broadcasted_iota(jnp.int32, (rows, width), 0)
    even_core = place_ref[0] == 1
    low_there = place_ref[2] > 0
    high_there = place_ref[2] < FRONTS - 1
    below_last, above_first = (
        column(table, width) for table in neighbour_tables(place_ref, a_w_ref, b_w_ref, planes - 1)
    )
    prolong = [column(entries(own_w_ref, 1, z), width) for z in range(planes)]
    own_last, own_first = prolong[planes - 1], prolong[0]
    start = pl.program_id(0) * count
    for b in range(count):
        field, ends = [], []
        for part in range(2):
            vec = [vector_ref[part, i, pl.ds(start + b, 1)] for i in range(9)]
            tiles = []
            for z in range(planes):
                tile = leaf_ref[part, b, z] + prolong[z] * vec[0]
                if z == 0:
                    tile = tile + enter_ref[part, b] + below_last * vec[1]
                if z == planes - 1:
                    tile = tile + leave_ref[part, b] + above_first * vec[5] + own_last * vec[6]
                field_ref[part, b, z] = tile
                tiles.append(tile)
            field.append(tiles)
            below = zlow_ref[part, b] + below_last * (vec[3] + vec[8]) + own_first * vec[7]
            above = zhigh_ref[part, b] + above_first * vec[2] + own_last * vec[4]
            ends.append((below, above))
        for part in range(2):
            tiles = field[part]
            near_rows = near_ref[part, b].astype(F32)
            far_rows = far_ref[part, b].astype(F32)
            low_rows = jnp.where(even_core, jnp.where(low_there, far_rows, 0.0), near_rows)
            high_rows = jnp.where(even_core, near_rows, jnp.where(high_there, far_rows, 0.0))
            for z in range(planes):
                diag_real = 6.0 - wave_ref[z]
                diag_imag = -DAMPING * wave_ref[z]
                here = tiles[z]
                below = tiles[z - 1] if z else ends[part][0]
                above = tiles[z + 1] if z < planes - 1 else ends[part][1]
                near = below + above
                low = jnp.where(row == 0, low_rows[z : z + 1], pltpu.roll(here, 1, 0))
                high = jnp.where(row == rows - 1, high_rows[z : z + 1], pltpu.roll(here, rows - 1, 0))
                near = near + low + high
                left = jnp.where(lane == 0, 0.0, pltpu.roll(here, 1, 1))
                right = jnp.where(lane == width - 1, 0.0, pltpu.roll(here, width - 1, 1))
                near = near + left + right
                cross = diag_imag * field[1 - part][z]
                applied = diag_real * here - near
                applied = applied - cross if part == 0 else applied + cross
                residual_ref[part, b, z] = source_ref[part, b, z] - applied


def finish(scalars, leaf, source, wave_term, vectors, *planes_in):
    two, sources, planes, rows, width = source.shape
    step = 2
    whole = pl.BlockSpec((two, step, planes, rows, width), lambda i: (0, i, 0, 0, 0))
    plane = pl.BlockSpec((two, step, rows, width), lambda i: (0, i, 0, 0))
    return pl.pallas_call(
        final_kernel,
        grid=(sources // step,),
        in_specs=[pl.BlockSpec(memory_space=pltpu.SMEM)] * 4
        + [
            whole, whole,
            pl.BlockSpec((planes, rows, width), lambda i: (0, 0, 0)),
            pl.BlockSpec(vectors.shape, lambda i: (0, 0, 0, 0)),
            plane, plane, plane, plane, plane, plane,
        ],
        out_specs=[whole, whole],
        out_shape=[jax.ShapeDtypeStruct(source.shape, F32)] * 2,
        compiler_params=pltpu.CompilerParams(vmem_limit_bytes=58 * 2**20),
        cost_estimate=pl.CostEstimate(flops=60000000, bytes_accessed=26000000, transcendentals=0),
        name="finish",
    )(*scalars, leaf, source, wave_term, vectors, *planes_in)


def after(value, *others):
    return lax.optimization_barrier((value, *others))[0]


def local(source, wave_term, leaf_inverse, separator_inverse, restrict_weight, prolong_weight):
    two, sources, planes, rows, width = source.shape
    panel = lax.axis_index("panel")
    front = lax.axis_index("front")
    even_core = front % 2 == 0
    even_panel = panel % 2 == 0
    leaf_matrix = leaf_inverse[:, 0, 0]
    separators = separator_inverse[:, 0, 0]
    root_matrix = separators[:, 3]
    place = jnp.stack([even_core.astype(jnp.int32), panel, front])
    vector = (two, sources, width)
    shape = jax.ShapeDtypeStruct

    weights = jnp.stack([restrict_weight, prolong_weight])
    traded_leaf = {which: swapped(leaf_matrix, which) for which in "AB"}
    traded_weights = {which: swapped(weights, which) for which in "AB"}
    leaf, base_terms, first_plane, last_plane, low_rows, high_rows = leaf_solve(weights, source, leaf_matrix)

    def halves(block):
        return jnp.where(even_core, block[0], block[1])

    def inside(sent, panels, near, far, cross):
        side = moved(sent, within(panels, near, cross))
        opposite = moved(halves(sent), within(panels, far, far))
        back = other_core(jnp.concatenate([side, opposite[None]]))
        return side, opposite, back

    def pair_sum(terms):
        return terms.astype(F32) + other_core(terms).astype(F32)

    every = tuple(range(PANELS))
    pair = pair_sum(base_terms.astype(BF))
    side, opposite, back = inside(pair.astype(BF), every, 2, 4, 6)
    near_term = jnp.where(even_core, side, back[:2]).astype(F32)
    far_term = jnp.where(even_core, jnp.stack([opposite, back[2]]), jnp.stack([back[2], opposite])).astype(F32)
    quad = pair + near_term
    slab = pair + side.astype(F32) + back[:2].astype(F32) + far_term
    slab = after(slab, traded_leaf["A"], traded_leaf["B"])
    base_sums = (pair, quad, slab)
    nothing = jnp.zeros(vector, F32)

    sums = whole_call(
        sums_kernel, [shape((5,) + vector, F32)], 10000000, "edge_sums", 3,
        weights, traded_weights["A"], traded_weights["B"], first_plane, last_plane,
    )[0]

    def gather(level_sums, panels, before):
        own, quad, slab = level_sums
        near = near_part(own, quad, slab, separators)
        return (near, slab, *inside(slab.astype(BF), panels, 8, 16, 24), before, root_matrix)

    def forward_close(level_sums, panels, target, which, before, parcel):
        got = gather(level_sums, panels, before)
        return whole_call(
            functools.partial(forward_kernel, target, which),
            [shape(vector, F32), shape(vector, BF), shape((2,) + vector, BF)], 200000000, "forward", 3,
            place, weights, traded_weights[which], *got, traded_leaf[which], sums, parcel,
        )

    def backward_close(level_sums, panels, target, keep, which, before, brought):
        got = gather(level_sums, panels, before)
        return whole_call(
            functools.partial(backward_kernel, target, keep, which),
            [shape(vector, F32), shape(vector, BF)], 200000000, "backward", 3,
            place, weights, traded_weights[which], *got, traded_leaf[which], sums, brought["A"], brought["B"],
        )

    def cross(terms, from_panel, to_panel):
        sent = pair_sum(terms).astype(BF)
        ends = ((from_panel, to_panel),)
        one = moved(sent, across(ends, 0, 2))
        two_ = moved(sent, across(ends, 4, 6))
        back = other_core(jnp.stack([one, two_])).astype(F32)
        one = one.astype(F32)
        own = jnp.where(even_core, one, back[0])
        quad = one + back[0]
        return own, quad, quad + two_.astype(F32) + back[1]

    state, terms, parcel = forward_close(base_sums, every, 0, "A", nothing, jnp.zeros((2,) + vector, BF))
    brought = {}
    for turn, which in enumerate("ABA"):
        target = turn + 1
        sums_now = cross(terms, turn, target)
        if turn > 0:
            brought[which] = swapped(parcel, which)
        total = tuple(a + b for a, b in zip(sums_now, base_sums))
        if turn < 2:
            state, terms, parcel = forward_close(total, (target,), target, "BA"[turn], state, parcel)
        else:
            state, terms = backward_close(total, (target,), target, False, "A", state, brought)
    for turn in range(PANELS - 1):
        from_panel = PANELS - 1 - turn
        target = from_panel - 1
        sums_now = cross(terms, from_panel, target)
        if turn < PANELS - 2:
            state, terms = backward_close(sums_now, (target,), target, True, "BA"[turn], state, brought)
        else:
            got = gather(sums_now, (target,), state)
            state = whole_call(
                functools.partial(last_kernel, target), [shape(vector, F32)], 100000000, "last", 1, place, *got
            )[0]
        if turn == 1:
            traded_b = swapped(state.astype(BF), "B")
    traded_a = swapped(state.astype(BF), "A")

    def by_parity(even_value, odd_value):
        return jnp.where(even_panel, even_value, odd_value)

    by_a = swapped(by_parity(last_plane, first_plane), "A")
    by_b = swapped(by_parity(first_plane, last_plane), "B")
    plane = shape(first_plane.shape, F32)
    enter, leave, zlow, zhigh = whole_call(
        planes_kernel, [plane] * 4, 400000000, "planes", 1,
        place, by_a, by_b, first_plane, last_plane, leaf_matrix, traded_leaf["A"], traded_leaf["B"],
    )
    scalars = (place, weights, traded_weights["A"], traded_weights["B"])
    edge = shape(low_rows.shape, BF)
    vectors, near_rows, far_rows = whole_call(
        closing_kernel, [shape((two, 9, sources, width), F32), edge, edge], 300000000, "closing", 4,
        *scalars, state, traded_a, traded_b, brought["A"], brought["B"], parcel,
        leaf_matrix, traded_leaf["A"], traded_leaf["B"], low_rows, high_rows, enter, leave,
    )
    near_front = other_core(near_rows)
    chain = [(p * FRONTS + f, p * FRONTS + (f + 1) % FRONTS) for p in range(PANELS) for f in range(1, FRONTS, 2)]
    far_front = moved(far_rows, pairing(chain))
    return tuple(
        finish(scalars, leaf, source, wave_term, vectors, enter, leave, near_front, far_front, zlow, zhigh)
    )


def solution(mesh):
    placed = (
        P(None, None, "panel", "front", None),
        P("panel", "front", None),
        P(None, "panel", "front", None, None),
        P(None, "panel", "front", None, None, None),
        P("panel", "front"),
        P("panel", "front"),
    )
    return jax.shard_map(
        local,
        mesh=mesh,
        in_specs=placed,
        out_specs=(P(None, None, "panel", "front", None), P(None, None, "panel", "front", None)),
        check_vma=False,
    )
```

time: 228 us -> 206 us (0.904)
  local copies, waits for them, and re-layouts: 32.9 us -> 14.3 us
  Pallas kernels: 33.6 us -> 46 us
  waiting for transfers between devices: 58.3 us -> 50.3 us
  other arithmetic: 14.9 us -> 9.17 us
  matrix products: 5.55 us -> 0 us
  starting transfers between devices: 80.2 us -> 83.6 us
    another operation x11 -> x0, local copies, waits for them, and re-layouts: 10.4 us -> none  [the longest x9 10.3 us: local(): vectors = jnp.stack([block.astype(F32) for block in vectors], axis=2)]
    pallas_call x2, Pallas kernels: 15.7 us -> 25.7 us  [the longest x1 16.3 us: finish(): pl.pallas_call(final_kernel, grid=(sources // step,), in_specs=[pl.BlockS...]
    ppermute x63 -> x61, waiting for transfers between devices: 58.3 us -> 50.3 us  [moved(): return lax.ppermute(block, AXES, route)]
    dot_general x12 -> x0, matrix products: 5.55 us -> none  [the longest x6 2.78 us: product(): by_imag = jnp.dot(block, matrix_imag, preferred_element_type=F32)]
    another operation x17 -> x1, other arithmetic: 4.82 us -> 0.08 us  [local(): place = jnp.stack([even_core.astype(jnp.int32), panel, front])]
    unnamed x45 -> x81, local copies, waits for them, and re-layouts: 17.9 us -> 14.2 us
    ppermute x63 -> x61, starting transfers between devices: 80.2 us -> 83.6 us  [moved(): return lax.ppermute(block, AXES, route)]
    slice x8 -> x0, local copies, waits for them, and re-layouts: 3.18 us -> none  [the longest x1 2.26 us: local(): leaf_a.append(swapped(after(leaf_matrix[:, half:], leaf_a[0]), 'A'))]
  transfers between devices with their start and end apart: 63 -> 61, of which waited for: 37 -> 39; matrix products, arithmetic and copies ran while one was open for 12% -> 5% of each run, Pallas kernels for 7% -> 9%
where the time goes in v1:
time: 206 us; the launch traced here: 205 us
  starting transfers between devices  83.6 us (41%)
  waiting for transfers between devices  50.3 us (24%)
  Pallas kernels  46 us (22%)
  local copies, waits for them, and re-layouts  14.3 us (7%)
  other arithmetic  9.17 us (4%)
    ppermute x61, starting transfers between devices, moved(): return lax.ppermute(block, AXES, route)  83.6 us
    ppermute x61, waiting for transfers between devices, moved(): return lax.ppermute(block, AXES, route)  50.3 us
    pallas_call x17, Pallas kernels, whole_call(): pl.pallas_call(kernel, in_specs=[pl.BlockSpec(memory_space=space) for spa...  20.2 us
    pallas_call x1, Pallas kernels, finish(): pl.pallas_call(final_kernel, grid=(sources // step,), in_specs=[pl.BlockS...  16.3 us
    unnamed x81, local copies, waits for them, and re-layouts  14.2 us
    pallas_call x1, Pallas kernels, leaf_solve(): pl.pallas_call(leaf_kernel, grid=(sources // step,), in_specs=[pl.BlockSp...  9.48 us
  transfers between devices with their start and end apart: 61, of which 39 were waited for; matrix products, arithmetic and copies ran while one was open for 5% of the time, Pallas kernels for 9%

profile of v1, /device:TPU:0, one launch (start us, length us, event | category | flops | bytes accessed | tf_op | source)
XLA Modules:
  0.0 205.0 jit_solution(15419281280599045989)
XLA Ops:
  0.6 4.2 %collective-permute-start.7 = (bf16[2,512,512]{2,1,0:T(8,128)(2,1)}, bf16[2,512,512]{2,1,0:T(8,128)(2,1)S(1)}, u32[]{:S(2)}, u32[]{:S(2)}) collective-permute-start(bf16[2,512,512]{2,1,0:T(8,128)(2,1)} %bitcast.147), channel_id=1, source_target_pairs={{0,96},{1,97},{2,98},{3,99},{4,100},{5,101},{6,102},{7,103},{8,104... | collective-permute-start | bytes 3145736 | tf_op jit(solution)/shard_map/ppermute | solution.py:48
  4.8 1.3 pad_maximum_fusion.14.weight_ref.own_ref.own_w_ref
  6.1 9.5 %leaf_solve.1 = (f32[2,24,8,8,512]{4,3,2,1,0:T(8,128)}, f32[6,2,4,512]{3,2,1,0:T(4,128)}, bf16[2,24,8,512]{3,2,1,0:T(8,128)(2,1)}, bf16[2,24,8,512]{3,2,1,0:T(8,...) custom-call(f32[2,8,8]{2,1,0:T(8,128)} %pad_maximum_fusion.14.weight_ref.own_ref.own_w_ref, ...), custom_call_target="tpu_custom_call" | custom-call | flops 65000000 | bytes 1600000 | tf_op jit(solution)/shard_map/leaf_solve/pallas_call | solution.py:113
  15.6 0.9 convert_bitcast_fusion
  16.7 1.2 collective-permute-done.2
  17.9 1.7 collective-permute-start.3
  19.6 2.9 %collective-permute-start.4 = (bf16[24,512]{1,0:T(8,128)(2,1)S(1)}, bf16[24,512]{1,0:T(8,128)(2,1)S(1)}, u32[]{:S(2)}, u32[]{:S(2)}) collective-permute-start(bf16[24,512]{1,0:T(8,128)(2,1)S(1)} %fusion.22), channel_id=1, source_target_pairs={{0,4},{1,5},{2,6},{3,7},{4,0},{5,1},{6,2},{7,3},{8,12},{9,13},{10,... | collective-permute-start | bytes 73736 | tf_op jit(solution)/shard_map/ppermute | solution.py:48
  22.5 2.4 %collective-permute-done.4 = bf16[24,512]{1,0:T(8,128)(2,1)S(1)} collective-permute-done((bf16[24,512]{1,0:T(8,128)(2,1)S(1)}, bf16[24,512]{1,0:T(8,128)(2,1)S(1)}, u32[]{:S(2)}, u32[]{:S(2)}) %collective-permute-start.4) | collective-permute-done | bytes 24608 | tf_op jit(solution)/shard_map/ppermute | solution.py:48
  25.7 1.5 collective-permute-start
  27.2 2.6 %copy.19 = bf16[2,1,1,4,512,512]{5,4,0,3,2,1:T(8,128)(2,1)S(1)} copy(bf16[2,1,1,4,512,512]{5,4,3,2,1,0:T(8,128)(2,1)} %param.9) | data formatting | bytes 8388608 | tf_op args[3]
  30.6 1.4 fusion.21
  32.0 1.5 collective-permute-start.8
  33.5 2.7 %collective-permute-start.9 = (bf16[24,512]{1,0:T(8,128)(2,1)}, bf16[24,512]{1,0:T(8,128)(2,1)S(1)}, u32[]{:S(2)}, u32[]{:S(2)}) collective-permute-start(bf16[24,512]{1,0:T(8,128)(2,1)} %fusion.21), channel_id=1, source_target_pairs={{0,16},{1,17},{2,18},{3,19},{4,20},{5,21},{6,22},{7,23},{8,24},{9,... | collective-permute-start | bytes 73736 | tf_op jit(solution)/shard_map/ppermute | solution.py:48
  36.3 2.9 %collective-permute-done.9.opposite_ref = bf16[24,512]{1,0:T(8,128)(2,1)S(1)} collective-permute-done((bf16[24,512]{1,0:T(8,128)(2,1)}, bf16[24,512]{1,0:T(8,128)(2,1)S(1)}, u32[]{:S(2)}, u32[]{:S(2)}) %collective-permute-start.9) | collective-permute-done | bytes 24608 | tf_op jit(solution)/shard_map/ppermute | solution.py:48
  39.5 1.0 copy-done.4
  40.5 1.0 copy-done.6
  41.5 2.1 %edge_sums.1.sums_ref = f32[5,2,24,512]{3,2,1,0:T(8,128)S(1)} custom-call(f32[2,8,8]{2,1,0:T(8,128)S(1)} %copy-done.14, f32[2,8,8]{2,1,0:T(8,128)S(1)} %collective-permute-done.by_a_ref.traded_ref.a_w_ref, f32[2,8,8]{2,1,0:T(8,128)S(1)} %collective-permute-done.1.by_b_ref.traded_ref.b_w_ref, bf16[2,24,8,512]{3,2,1,0:T(8,128)(2,1)S(1)} %copy-done.4, ...), custom_call_target="tpu_custom_call" | custom-call | flops 10000000 | bytes 50000 | tf_op jit(solution)/shard_map/edge_sums/pallas_call | solution.py:139
  43.6 2.2 %copy-done = bf16[2,1,1,4,512,512]{5,4,3,2,1,0:T(8,128)(2,1)S(1)} copy-done((bf16[2,1,1,4,512,512]{5,4,3,2,1,0:T(8,128)(2,1)S(1)}, bf16[2,1,1,4,512,512]{5,4,3,2,1,0:T(8,128)(2,1)}, u32[]{:S(2)}) %copy-start) | copy-done | bytes 4194328
  46.5 1.1 copy-done.27
  48.4 1.4 forward.3
  50.3 0.9 collective-permute-done.11
  51.2 2.8 %collective-permute-start.13 = (bf16[2,24,512]{2,1,0:T(8,128)(2,1)S(1)}, bf16[2,24,512]{2,1,0:T(8,128)(2,1)S(1)}, u32[]{:S(2)}, u32[]{:S(2)}) collective-permute-start(bf16[2,24,512]{2,1,0:T(8,128)(2,1)S(1)} %add_convert_fusion.5), channel_id=1, source_target_pairs={{0,36},{1,39},{2,38},{3,37},{4,32},{5,35},{6,34},{7,33},{8,44},{9,... | collective-permute-start | bytes 147464 | tf_op jit(solution)/shard_map/ppermute | solution.py:48
  54.0 1.7 collective-permute-start.12
  55.7 2.5 %collective-permute-done.13 = bf16[2,24,512]{2,1,0:T(8,128)(2,1)S(1)} collective-permute-done((bf16[2,24,512]{2,1,0:T(8,128)(2,1)S(1)}, bf16[2,24,512]{2,1,0:T(8,128)(2,1)S(1)}, u32[]{:S(2)}, u32[]{:S(2)}) %collective-permute-start.13) | collective-permute-done | bytes 49184 | tf_op jit(solution)/shard_map/ppermute | solution.py:48
  58.9 1.3 collective-permute-done.14
  60.9 0.8 collective-permute-done.16.opposite_ref
  63.1 1.4 forward.4
  64.9 0.9 collective-permute-done.18
  67.7 1.1 collective-permute-done.21
  69.5 0.9 collective-permute-done.23.opposite_ref
  71.9 1.4 forward.5
  73.8 0.9 collective-permute-done.25
  76.6 1.1 collective-permute-done.28
  78.4 24.6 %collective-permute-start.33 = (bf16[2,2,24,512]{3,2,1,0:T(8,128)(2,1)S(1)}, bf16[2,2,24,512]{3,2,1,0:T(8,128)(2,1)S(1)}, u32[]{:S(2)}, u32[]{:S(2)}) collective-permute-start(bf16[2,2,24,512]{3,2,1,0:T(8,128)(2,1)S(1)} %get-tuple-element.41.parcel_ref), channel_id=1, source_target_pairs={{0,96},{1,97},{2,98},{3,99},{4,100},{5,101},{6,102},{7,103},{8,104... | collective-permute-start | bytes 294920 | tf_op jit(solution)/shard_map/ppermute | solution.py:48
  103.8 1.8 collective-permute-done.33.by_b_ref.parcel_b_ref
  105.6 2.0 collective-permute-done.32.by_a_ref.parcel_a_ref
  107.6 1.4 backward.3
  109.1 1.2 collective-permute-done.34
  112.2 1.0 collective-permute-done.37
  113.8 1.0 collective-permute-done.39.opposite_ref
  116.2 1.4 backward.4
  117.9 1.1 collective-permute-done.41
  120.9 1.0 collective-permute-done.44
  122.5 1.0 collective-permute-done.46.opposite_ref
  124.9 1.4 backward.5
  127.0 1.1 collective-permute-done.48
  128.7 21.2 %collective-permute-start.50 = (bf16[2,24,512]{2,1,0:T(8,128)(2,1)}, bf16[2,24,512]{2,1,0:T(8,128)(2,1)}, u32[]{:S(2)}, u32[]{:S(2)}) collective-permute-start(bf16[2,24,512]{2,1,0:T(8,128)(2,1)} %add_convert_fusion), channel_id=1, source_target_pairs={{0,36},{1,39},{2,38},{3,37},{4,32},{5,35},{6,34},{7,33},{8,44},{9,... | collective-permute-start | bytes 147464 | tf_op jit(solution)/shard_map/ppermute | solution.py:48
  150.0 2.4 %collective-permute-done.50 = bf16[2,24,512]{2,1,0:T(8,128)(2,1)} collective-permute-done((bf16[2,24,512]{2,1,0:T(8,128)(2,1)}, bf16[2,24,512]{2,1,0:T(8,128)(2,1)}, u32[]{:S(2)}, u32[]{:S(2)}) %collective-permute-start.50) | collective-permute-done | bytes 49184 | tf_op jit(solution)/shard_map/ppermute | solution.py:48
  152.4 2.4 %collective-permute-done.49 = bf16[2,24,512]{2,1,0:T(8,128)(2,1)} collective-permute-done((bf16[2,24,512]{2,1,0:T(8,128)(2,1)}, bf16[2,24,512]{2,1,0:T(8,128)(2,1)}, u32[]{:S(2)}, u32[]{:S(2)}) %collective-permute-start.49) | collective-permute-done | bytes 49184 | tf_op jit(solution)/shard_map/ppermute | solution.py:48
  155.7 1.1 broadcast_select_fusion
  156.9 1.3 collective-permute-start.57
  158.2 0.9 fusion.24
  159.8 2.3 %collective-permute-start.53 = (bf16[24,512]{1,0:T(8,128)(2,1)S(1)}, bf16[24,512]{1,0:T(8,128)(2,1)S(1)}, u32[]{:S(2)}, u32[]{:S(2)}) collective-permute-start(bf16[24,512]{1,0:T(8,128)(2,1)S(1)} %fusion.15), channel_id=1, source_target_pairs={{0,16},{1,17},{2,18},{3,19},{4,20},{5,21},{6,22},{7,23},{8,24},{9,... | collective-permute-start | bytes 73736 | tf_op jit(solution)/shard_map/ppermute | solution.py:48
  162.1 3.1 %collective-permute-done.53.opposite_ref = bf16[24,512]{1,0:T(8,128)(2,1)S(1)} collective-permute-done((bf16[24,512]{1,0:T(8,128)(2,1)S(1)}, bf16[24,512]{1,0:T(8,128)(2,1)S(1)}, u32[]{:S(2)}, u32[]{:S(2)}) %collective-permute-start.53) | collective-permute-done | bytes 24608 | tf_op jit(solution)/shard_map/ppermute | solution.py:48
  165.3 0.9 convert_element_type.220
  166.3 2.2 %copy-done.2 = bf16[2,1,1,4,512,512]{5,4,3,2,1,0:T(8,128)(2,1)S(1)} copy-done((bf16[2,1,1,4,512,512]{5,4,3,2,1,0:T(8,128)(2,1)S(1)}, bf16[2,1,1,4,512,512]{5,4,3,2,1,0:T(8,128)(2,1)}, u32[]{:S(2)}) %copy-start.2) | copy-done | bytes 4194328
  169.2 0.8 last.1.state_ref
  170.2 2.5 %planes.1 = (f32[2,24,8,512]{3,2,1,0:T(8,128)S(1)}, f32[2,24,8,512]{3,2,1,0:T(8,128)S(1)}, f32[2,24,8,512]{3,2,1,0:T(8,128)S(1)}, f32[2,24,8,512]{3,2,1,0:T(8,128)S(1)}) custom-call(s32[3]{0:T(128)S(1)} %copy-done.33, bf16[2,24,8,512]{3,2,1,0:T(8,128)(2,1)S(1)} %collective-permute-done.57.by_a_ref, ...), custom_call_target="tpu_custom_call" | custom-call | flops 400000000 | bytes 2000000 | tf_op jit(solution)/shard_map/planes/pallas_call | solution.py:139
  172.7 0.9 copy-done.16
  174.3 2.0 closing.1
  176.3 1.0 copy-done.15
  177.3 2.7 %collective-permute-start.60 = (bf16[2,24,8,512]{3,2,1,0:T(8,128)(2,1)S(1)}, bf16[2,24,8,512]{3,2,1,0:T(8,128)(2,1)S(1)}, u32[]{:S(2)}, u32[]{:S(2)}) collective-permute-start(bf16[2,24,8,512]{3,2,1,0:T(8,128)(2,1)S(1)} %get-tuple-element.57), channel_id=1, source_target_pairs={{0,31},{1,2},{2,1},{3,4},{4,3},{5,6},{6,5},{7,8},{8,7},{9,10},{10,... | collective-permute-start | bytes 1179656 | tf_op jit(solution)/shard_map/ppermute | solution.py:48
  180.0 7.8 %collective-permute-done.60.far_ref = bf16[2,24,8,512]{3,2,1,0:T(8,128)(2,1)S(1)} collective-permute-done((bf16[2,24,8,512]{3,2,1,0:T(8,128)(2,1)S(1)}, bf16[2,24,8,512]{3,2,1,0:T(8,128)(2,1)S(1)}, u32[]{:S(2)}, u32[]{:S(2)}) %collective-permute-start.60) | collective-permute-done | bytes 393248 | tf_op jit(solution)/shard_map/ppermute | solution.py:48
  188.6 16.3 %finish.1 = (f32[2,24,8,8,512]{4,3,2,1,0:T(8,128)}, f32[2,24,8,8,512]{4,3,2,1,0:T(8,128)}) custom-call(s32[3]{0:T(128)} %copy-done.32, f32[2,8,8]{2,1,0:T(8,128)} %pad_maximum_fusion.14.weight_ref.own_ref.own_w_ref, f32[2,8,8]{2,1,0:T(8,128)} %copy-done.20, f32[2,8,8]{2,1,0:T(8,128)} %copy-done.23, f32[2,24,8,8,512]{4,3,2,1,0:T(8,128)} %get-tuple-element.31.leaf_ref, ...), custom_call_target="tpu_custom_call" | custom-call | flops 60000000 | bytes 26000000 | tf_op jit(solution)/shard_map/finish/pallas_call | solution.py:418
  (213 shorter events, 28.5 us)
Async XLA Ops:
  0.6 29.3 %collective-permute-start.7 = (bf16[2,512,512]{2,1,0:T(8,128)(2,1)}, bf16[2,512,512]{2,1,0:T(8,128)(2,1)S(1)}, u32[]{:S(2)}, u32[]{:S(2)}) collective-permute-start(bf16[2,512,512]{2,1,0:T(8,128)(2,1)} %bitcast.147), channel_id=1, source_target_pairs={{0,96},{1,97},{2,98},{3,99},{4,100},{5,101},{6,102},{7,103},{8,104... | collective-permute-start | bytes 3145736 | tf_op jit(solution)/shard_map/ppermute | solution.py:48
  4.8 25.1 %collective-permute-start.6 = (bf16[2,512,512]{2,1,0:T(8,128)(2,1)}, bf16[2,512,512]{2,1,0:T(8,128)(2,1)S(1)}, u32[]{:S(2)}, u32[]{:S(2)}) collective-permute-start(bf16[2,512,512]{2,1,0:T(8,128)(2,1)} %bitcast.148), channel_id=1, source_target_pairs={{0,32},{1,33},{2,34},{3,35},{4,36},{5,37},{6,38},{7,39},{8,40},{9,... | collective-permute-start | bytes 3145736 | tf_op jit(solution)/shard_map/ppermute | solution.py:48
  16.6 1.3 collective-permute-start.2
  17.9 7.0 %collective-permute-start.3 = (bf16[2,24,512]{2,1,0:T(8,128)(2,1)S(1)}, bf16[2,24,512]{2,1,0:T(8,128)(2,1)S(1)}, u32[]{:S(2)}, u32[]{:S(2)}) collective-permute-start(bf16[2,24,512]{2,1,0:T(8,128)(2,1)S(1)} %fusion.23), channel_id=1, source_target_pairs={{0,2},{1,7},{2,0},{3,5},{4,6},{5,3},{6,4},{7,1},{8,10},{9,15},{10,... | collective-permute-start | bytes 147464 | tf_op jit(solution)/shard_map/ppermute | solution.py:48
  19.6 5.3 %collective-permute-start.4 = (bf16[24,512]{1,0:T(8,128)(2,1)S(1)}, bf16[24,512]{1,0:T(8,128)(2,1)S(1)}, u32[]{:S(2)}, u32[]{:S(2)}) collective-permute-start(bf16[24,512]{1,0:T(8,128)(2,1)S(1)} %fusion.22), channel_id=1, source_target_pairs={{0,4},{1,5},{2,6},{3,7},{4,0},{5,1},{6,2},{7,3},{8,12},{9,13},{10,... | collective-permute-start | bytes 73736 | tf_op jit(solution)/shard_map/ppermute | solution.py:48
  24.9 5.0 %collective-permute-start.5 = (bf16[3,24,512]{2,1,0:T(8,128)(2,1)S(1)}, bf16[3,24,512]{2,1,0:T(8,128)(2,1)S(1)}, u32[]{:S(2)}, u32[]{:S(2)}) collective-permute-start(bf16[3,24,512]{2,1,0:T(8,128)(2,1)S(1)} %pad_maximum_fusion.6), channel_id=1, source_target_pairs={{0,1},{1,0},{2,3},{3,2},{4,5},{5,4},{6,7},{7,6},{8,9},{9,8},{10,11... | collective-permute-start | bytes 221192 | tf_op jit(solution)/shard_map/ppermute | solution.py:48
  25.2 14.3 %collective-permute-start.1 = (f32[2,8,8]{2,1,0:T(8,128)S(1)}, f32[2,8,8]{2,1,0:T(8,128)S(1)}, u32[]{:S(2)}, u32[]{:S(2)}) collective-permute-start(f32[2,8,8]{2,1,0:T(8,128)S(1)} %copy-done.14), channel_id=1, source_target_pairs={{0,96},{1,97},{2,98},{3,99},{4,100},{5,101},{6,102},{7,103},{8,104... | collective-permute-start | bytes 1544 | tf_op jit(solution)/shard_map/ppermute | solution.py:48
  25.7 13.8 %collective-permute-start = (f32[2,8,8]{2,1,0:T(8,128)S(1)}, f32[2,8,8]{2,1,0:T(8,128)S(1)}, u32[]{:S(2)}, u32[]{:S(2)}) collective-permute-start(f32[2,8,8]{2,1,0:T(8,128)S(1)} %copy-done.14), channel_id=1, source_target_pairs={{0,32},{1,33},{2,34},{3,35},{4,36},{5,37},{6,38},{7,39},{8,40},{9,... | collective-permute-start | bytes 1544 | tf_op jit(solution)/shard_map/ppermute | solution.py:48
  32.0 7.2 %collective-permute-start.8 = (bf16[2,24,512]{2,1,0:T(8,128)(2,1)}, bf16[2,24,512]{2,1,0:T(8,128)(2,1)S(1)}, u32[]{:S(2)}, u32[]{:S(2)}) collective-permute-start(bf16[2,24,512]{2,1,0:T(8,128)(2,1)} %convert_element_type.176), channel_id=1, source_target_pairs={{0,8},{1,25},{2,10},{3,27},{4,12},{5,29},{6,14},{7,31},{8,0},{9,17... | collective-permute-start | bytes 147464 | tf_op jit(solution)/shard_map/ppermute | solution.py:48
  33.5 5.7 %collective-permute-start.9 = (bf16[24,512]{1,0:T(8,128)(2,1)}, bf16[24,512]{1,0:T(8,128)(2,1)S(1)}, u32[]{:S(2)}, u32[]{:S(2)}) collective-permute-start(bf16[24,512]{1,0:T(8,128)(2,1)} %fusion.21), channel_id=1, source_target_pairs={{0,16},{1,17},{2,18},{3,19},{4,20},{5,21},{6,22},{7,23},{8,24},{9,... | collective-permute-start | bytes 73736 | tf_op jit(solution)/shard_map/ppermute | solution.py:48
  39.2 7.3 %collective-permute-start.10 = (bf16[3,24,512]{2,1,0:T(8,128)(2,1)S(1)}, bf16[3,24,512]{2,1,0:T(8,128)(2,1)S(1)}, u32[]{:S(2)}, u32[]{:S(2)}) collective-permute-start(bf16[3,24,512]{2,1,0:T(8,128)(2,1)S(1)} %pad_maximum_fusion.7), channel_id=1, source_target_pairs={{0,1},{1,0},{2,3},{3,2},{4,5},{5,4},{6,7},{7,6},{8,9},{9,8},{10,11... | collective-permute-start | bytes 221192 | tf_op jit(solution)/shard_map/ppermute | solution.py:48
  39.5 85.4 %copy-start.32 = (s32[3]{0:T(128)}, s32[3]{0:T(128)S(1)}, u32[]{:S(2)}) copy-start(s32[3]{0:T(128)S(1)} %pad_add_fusion.place_ref) | copy-start | bytes 40
  39.5 134.7 %copy-start.20 = (f32[2,8,8]{2,1,0:T(8,128)}, f32[2,8,8]{2,1,0:T(8,128)S(1)}, u32[]{:S(2)}) copy-start(f32[2,8,8]{2,1,0:T(8,128)S(1)} %collective-permute-done.by_a_ref.traded_ref.a_w_ref) | copy-start | bytes 1540
  49.8 1.4 collective-permute-start.11
  51.2 7.1 %collective-permute-start.13 = (bf16[2,24,512]{2,1,0:T(8,128)(2,1)S(1)}, bf16[2,24,512]{2,1,0:T(8,128)(2,1)S(1)}, u32[]{:S(2)}, u32[]{:S(2)}) collective-permute-start(bf16[2,24,512]{2,1,0:T(8,128)(2,1)S(1)} %add_convert_fusion.5), channel_id=1, source_target_pairs={{0,36},{1,39},{2,38},{3,37},{4,32},{5,35},{6,34},{7,33},{8,44},{9,... | collective-permute-start | bytes 147464 | tf_op jit(solution)/shard_map/ppermute | solution.py:48
  54.0 4.8 %collective-permute-start.12 = (bf16[2,24,512]{2,1,0:T(8,128)(2,1)S(1)}, bf16[2,24,512]{2,1,0:T(8,128)(2,1)S(1)}, u32[]{:S(2)}, u32[]{:S(2)}) collective-permute-start(bf16[2,24,512]{2,1,0:T(8,128)(2,1)S(1)} %add_convert_fusion.5), channel_id=1, source_target_pairs={{0,32},{1,35},{2,34},{3,33},{4,36},{5,39},{6,38},{7,37},{8,40},{9,... | collective-permute-start | bytes 147464 | tf_op jit(solution)/shard_map/ppermute | solution.py:48
  58.8 1.4 collective-permute-start.14
  60.3 1.5 collective-permute-start.15
  60.5 1.2 collective-permute-start.16
  61.7 1.3 collective-permute-start.17
  64.5 1.3 collective-permute-start.18
  65.8 1.3 collective-permute-start.20
  66.2 1.2 collective-permute-start.19
  67.5 1.4 collective-permute-start.21
  68.9 1.5 collective-permute-start.22
  69.2 1.2 collective-permute-start.23
  70.4 1.5 collective-permute-start.24
  73.3 42.5 %copy-start.30 = (bf16[2,2,24,512]{3,2,1,0:T(8,128)(2,1)}, bf16[2,2,24,512]{3,2,1,0:T(8,128)(2,1)S(1)}, u32[]{:S(2)}) copy-start(bf16[2,2,24,512]{3,2,1,0:T(8,128)(2,1)S(1)} %get-tuple-element.44.parcel_ref) | copy-start | bytes 294916
  73.3 1.3 collective-permute-start.25
  74.7 1.3 collective-permute-start.27
  75.1 1.2 collective-permute-start.26
  76.3 1.4 collective-permute-start.28
  77.8 25.2 %collective-permute-start.29 = (bf16[2,24,512]{2,1,0:T(8,128)(2,1)S(1)}, bf16[2,24,512]{2,1,0:T(8,128)(2,1)S(1)}, u32[]{:S(2)}, u32[]{:S(2)}) collective-permute-start(bf16[2,24,512]{2,1,0:T(8,128)(2,1)S(1)} %get-tuple-element.69), channel_id=1, source_target_pairs={{0,1},{1,0},{2,3},{3,2},{4,5},{5,4},{6,7},{7,6},{8,9},{9,8},{10,11... | collective-permute-start | bytes 147464 | tf_op jit(solution)/shard_map/ppermute | solution.py:48
  78.1 25.0 %collective-permute-start.30 = (bf16[24,512]{1,0:T(8,128)(2,1)S(1)}, bf16[24,512]{1,0:T(8,128)(2,1)S(1)}, u32[]{:S(2)}, u32[]{:S(2)}) collective-permute-start(bf16[24,512]{1,0:T(8,128)(2,1)S(1)} %fusion.18), channel_id=1, source_target_pairs={{0,1},{1,0},{2,3},{3,2},{4,5},{5,4},{6,7},{7,6},{8,9},{9,8},{10,11... | collective-permute-start | bytes 73736 | tf_op jit(solution)/shard_map/ppermute | solution.py:48
  78.4 27.2 %collective-permute-start.33 = (bf16[2,2,24,512]{3,2,1,0:T(8,128)(2,1)S(1)}, bf16[2,2,24,512]{3,2,1,0:T(8,128)(2,1)S(1)}, u32[]{:S(2)}, u32[]{:S(2)}) collective-permute-start(bf16[2,2,24,512]{3,2,1,0:T(8,128)(2,1)S(1)} %get-tuple-element.41.parcel_ref), channel_id=1, source_target_pairs={{0,96},{1,97},{2,98},{3,99},{4,100},{5,101},{6,102},{7,103},{8,104... | collective-permute-start | bytes 294920 | tf_op jit(solution)/shard_map/ppermute | solution.py:48
  103.0 4.6 %collective-permute-start.32 = (bf16[2,2,24,512]{3,2,1,0:T(8,128)(2,1)S(1)}, bf16[2,2,24,512]{3,2,1,0:T(8,128)(2,1)S(1)}, u32[]{:S(2)}, u32[]{:S(2)}) collective-permute-start(bf16[2,2,24,512]{3,2,1,0:T(8,128)(2,1)S(1)} %get-tuple-element.44.parcel_ref), channel_id=1, source_target_pairs={{0,32},{1,33},{2,34},{3,35},{4,36},{5,37},{6,38},{7,39},{8,40},{9,... | collective-permute-start | bytes 294920 | tf_op jit(solution)/shard_map/ppermute | solution.py:48
  103.0 4.6 %collective-permute-start.31 = (bf16[3,24,512]{2,1,0:T(8,128)(2,1)S(1)}, bf16[3,24,512]{2,1,0:T(8,128)(2,1)S(1)}, u32[]{:S(2)}, u32[]{:S(2)}) collective-permute-start(bf16[3,24,512]{2,1,0:T(8,128)(2,1)S(1)} %pad_maximum_fusion.10), channel_id=1, source_target_pairs={{0,1},{1,0},{2,3},{3,2},{4,5},{5,4},{6,7},{7,6},{8,9},{9,8},{10,11... | collective-permute-start | bytes 221192 | tf_op jit(solution)/shard_map/ppermute | solution.py:48
  109.0 1.3 collective-permute-start.34
  110.3 1.3 collective-permute-start.36
  110.6 1.2 collective-permute-start.35
  111.8 1.4 collective-permute-start.37
  113.2 1.6 collective-permute-start.38
  113.7 1.2 collective-permute-start.39
  114.9 1.3 collective-permute-start.40
  117.6 1.3 collective-permute-start.41
  118.9 1.3 collective-permute-start.43
  119.2 1.2 collective-permute-start.42
  120.4 1.4 collective-permute-start.44
  121.9 1.6 collective-permute-start.45
  122.3 1.2 collective-permute-start.46
  123.5 1.3 collective-permute-start.47
  126.9 1.2 collective-permute-start.48
  128.7 23.6 %collective-permute-start.50 = (bf16[2,24,512]{2,1,0:T(8,128)(2,1)}, bf16[2,24,512]{2,1,0:T(8,128)(2,1)}, u32[]{:S(2)}, u32[]{:S(2)}) collective-permute-start(bf16[2,24,512]{2,1,0:T(8,128)(2,1)} %add_convert_fusion), channel_id=1, source_target_pairs={{0,36},{1,39},{2,38},{3,37},{4,32},{5,35},{6,34},{7,33},{8,44},{9,... | collective-permute-start | bytes 147464 | tf_op jit(solution)/shard_map/ppermute | solution.py:48
  150.0 4.8 %collective-permute-start.49 = (bf16[2,24,512]{2,1,0:T(8,128)(2,1)}, bf16[2,24,512]{2,1,0:T(8,128)(2,1)}, u32[]{:S(2)}, u32[]{:S(2)}) collective-permute-start(bf16[2,24,512]{2,1,0:T(8,128)(2,1)} %add_convert_fusion), channel_id=1, source_target_pairs={{0,32},{1,35},{2,34},{3,33},{4,36},{5,39},{6,38},{7,37},{8,40},{9,... | collective-permute-start | bytes 147464 | tf_op jit(solution)/shard_map/ppermute | solution.py:48
  155.6 2.6 %collective-permute-start.51 = (bf16[2,2,24,512]{3,2,1,0:T(8,128)(2,1)S(1)}, bf16[2,2,24,512]{3,2,1,0:T(8,128)(2,1)S(1)}, u32[]{:S(2)}, u32[]{:S(2)}) collective-permute-start(bf16[2,2,24,512]{3,2,1,0:T(8,128)(2,1)S(1)} %pad_maximum_fusion.5), channel_id=1, source_target_pairs={{0,1},{1,0},{2,3},{3,2},{4,5},{5,4},{6,7},{7,6},{8,9},{9,8},{10,11... | collective-permute-start | bytes 294920 | tf_op jit(solution)/shard_map/ppermute | solution.py:48
  156.8 13.4 %collective-permute-start.58 = (bf16[2,24,8,512]{3,2,1,0:T(8,128)(2,1)S(1)}, bf16[2,24,8,512]{3,2,1,0:T(8,128)(2,1)S(1)}, u32[]{:S(2)}, u32[]{:S(2)}) collective-permute-start(bf16[2,24,8,512]{3,2,1,0:T(8,128)(2,1)S(1)} %get-tuple-element.75), channel_id=1, source_target_pairs={{0,96},{1,97},{2,98},{3,99},{4,100},{5,101},{6,102},{7,103},{8,104... | collective-permute-start | bytes 1179656 | tf_op jit(solution)/shard_map/ppermute | solution.py:48
  156.9 13.3 %collective-permute-start.57 = (bf16[2,24,8,512]{3,2,1,0:T(8,128)(2,1)S(1)}, bf16[2,24,8,512]{3,2,1,0:T(8,128)(2,1)S(1)}, u32[]{:S(2)}, u32[]{:S(2)}) collective-permute-start(bf16[2,24,8,512]{3,2,1,0:T(8,128)(2,1)S(1)} %get-tuple-element.76), channel_id=1, source_target_pairs={{0,32},{1,33},{2,34},{3,35},{4,36},{5,37},{6,38},{7,39},{8,40},{9,... | collective-permute-start | bytes 1179656 | tf_op jit(solution)/shard_map/ppermute | solution.py:48
  159.1 6.1 %collective-permute-start.52 = (bf16[2,24,512]{2,1,0:T(8,128)(2,1)S(1)}, bf16[2,24,512]{2,1,0:T(8,128)(2,1)S(1)}, u32[]{:S(2)}, u32[]{:S(2)}) collective-permute-start(bf16[2,24,512]{2,1,0:T(8,128)(2,1)S(1)} %get-tuple-element.60), channel_id=1, source_target_pairs={{0,8},{1,25},{2,10},{3,27},{4,12},{5,29},{6,14},{7,31},{8,0},{9,17... | collective-permute-start | bytes 147464 | tf_op jit(solution)/shard_map/ppermute | solution.py:48
  159.8 5.4 %collective-permute-start.53 = (bf16[24,512]{1,0:T(8,128)(2,1)S(1)}, bf16[24,512]{1,0:T(8,128)(2,1)S(1)}, u32[]{:S(2)}, u32[]{:S(2)}) collective-permute-start(bf16[24,512]{1,0:T(8,128)(2,1)S(1)} %fusion.15), channel_id=1, source_target_pairs={{0,16},{1,17},{2,18},{3,19},{4,20},{5,21},{6,22},{7,23},{8,24},{9,... | collective-permute-start | bytes 73736 | tf_op jit(solution)/shard_map/ppermute | solution.py:48
  165.2 3.9 %collective-permute-start.54 = (bf16[3,24,512]{2,1,0:T(8,128)(2,1)S(1)}, bf16[3,24,512]{2,1,0:T(8,128)(2,1)S(1)}, u32[]{:S(2)}, u32[]{:S(2)}) collective-permute-start(bf16[3,24,512]{2,1,0:T(8,128)(2,1)S(1)} %pad_maximum_fusion.13), channel_id=1, source_target_pairs={{0,1},{1,0},{2,3},{3,2},{4,5},{5,4},{6,7},{7,6},{8,9},{9,8},{10,11... | collective-permute-start | bytes 221192 | tf_op jit(solution)/shard_map/ppermute | solution.py:48
  166.2 7.4 %collective-permute-start.56 = (bf16[2,24,512]{2,1,0:T(8,128)(2,1)S(1)}, bf16[2,24,512]{2,1,0:T(8,128)(2,1)S(1)}, u32[]{:S(2)}, u32[]{:S(2)}) collective-permute-start(bf16[2,24,512]{2,1,0:T(8,128)(2,1)S(1)} %convert_element_type.220), channel_id=1, source_target_pairs={{0,96},{1,97},{2,98},{3,99},{4,100},{5,101},{6,102},{7,103},{8,104... | collective-permute-start | bytes 147464 | tf_op jit(solution)/shard_map/ppermute | solution.py:48
  170.0 4.2 %collective-permute-start.55 = (bf16[2,24,512]{2,1,0:T(8,128)(2,1)S(1)}, bf16[2,24,512]{2,1,0:T(8,128)(2,1)S(1)}, u32[]{:S(2)}, u32[]{:S(2)}) collective-permute-start(bf16[2,24,512]{2,1,0:T(8,128)(2,1)S(1)} %convert_element_type.219), channel_id=1, source_target_pairs={{0,32},{1,33},{2,34},{3,35},{4,36},{5,37},{6,38},{7,39},{8,40},{9,... | collective-permute-start | bytes 147464 | tf_op jit(solution)/shard_map/ppermute | solution.py:48
  177.3 2.7 %collective-permute-start.59 = (bf16[2,24,8,512]{3,2,1,0:T(8,128)(2,1)S(1)}, bf16[2,24,8,512]{3,2,1,0:T(8,128)(2,1)S(1)}, u32[]{:S(2)}, u32[]{:S(2)}) collective-permute-start(bf16[2,24,8,512]{3,2,1,0:T(8,128)(2,1)S(1)} %get-tuple-element.56), channel_id=1, source_target_pairs={{0,1},{1,0},{2,3},{3,2},{4,5},{5,4},{6,7},{7,6},{8,9},{9,8},{10,11... | collective-permute-start | bytes 1179656 | tf_op jit(solution)/shard_map/ppermute | solution.py:48
  177.3 10.5 %collective-permute-start.60 = (bf16[2,24,8,512]{3,2,1,0:T(8,128)(2,1)S(1)}, bf16[2,24,8,512]{3,2,1,0:T(8,128)(2,1)S(1)}, u32[]{:S(2)}, u32[]{:S(2)}) collective-permute-start(bf16[2,24,8,512]{3,2,1,0:T(8,128)(2,1)S(1)} %get-tuple-element.57), channel_id=1, source_target_pairs={{0,31},{1,2},{2,1},{3,4},{4,3},{5,6},{6,5},{7,8},{8,7},{9,10},{10,... | collective-permute-start | bytes 1179656 | tf_op jit(solution)/shard_map/ppermute | solution.py:48
  (37 other events, 456.1 us)

commit v2 on v1

--- a/solution.py
+++ b/solution.py
@@ -107,7 +107,7 @@
 
 def leaf_solve(weights, source, matrix):
     two, sources, planes, rows, width = source.shape
-    step = 4
+    step = 6
     whole = pl.BlockSpec((two, step, planes, rows, width), lambda i: (0, i, 0, 0, 0))
     plane = pl.BlockSpec((two, step, rows, width), lambda i: (0, i, 0, 0))
     leaf, total, first, last, low, high = pl.pallas_call(
@@ -120,28 +120,28 @@
         ],
         out_specs=[whole, pl.BlockSpec((1, two, step, width), lambda i: (i, 0, 0, 0)), plane, plane, plane, plane],
         out_shape=[
-            jax.ShapeDtypeStruct(source.shape, F32),
+            pltpu.HBM(source.shape, F32),
             jax.ShapeDtypeStruct((sources // step, two, step, width), F32),
             jax.ShapeDtypeStruct((two, sources, rows, width), BF),
             jax.ShapeDtypeStruct((two, sources, rows, width), BF),
             jax.ShapeDtypeStruct((two, sources, planes, width), F32),
             jax.ShapeDtypeStruct((two, sources, planes, width), F32),
         ],
-        compiler_params=pltpu.CompilerParams(vmem_limit_bytes=58 * 2**20),
+        compiler_params=pltpu.CompilerParams(vmem_limit_bytes=32 * 2**20),
         cost_estimate=pl.CostEstimate(flops=65000000, bytes_accessed=1600000, transcendentals=0),
         name="leaf_solve",
     )(weights, source, matrix)
     return leaf, total.transpose(1, 0, 2, 3).reshape(two, sources, width), first, last, low, high
 
 
-def whole_call(kernel, shapes, cost, name, smem, *args):
+def whole_call(kernel, shapes, cost, name, smem, *args, limit=14):
     spaces = [pltpu.SMEM] * smem + [pltpu.VMEM] * (len(args) - smem)
     return pl.pallas_call(
         kernel,
         in_specs=[pl.BlockSpec(memory_space=space) for space in spaces],
         out_specs=[pl.BlockSpec(memory_space=pltpu.VMEM)] * len(shapes),
         out_shape=shapes,
-        compiler_params=pltpu.CompilerParams(vmem_limit_bytes=28 * 2**20),
+        compiler_params=pltpu.CompilerParams(vmem_limit_bytes=limit * 2**20),
         cost_estimate=pl.CostEstimate(flops=cost, bytes_accessed=cost // 200, transcendentals=0),
         name=name,
     )(*args)
@@ -175,7 +175,7 @@
         far = jnp.where(even, mine, other) if part == 0 else jnp.where(even, other, mine)
         root.append(slab_ref[part] + side_ref[part].astype(F32) + back_ref[part].astype(F32) + far)
     block = jnp.concatenate(root, axis=0).astype(BF)
-    got = product(block, root_ref[0], root_ref[1], sources)
+    got = product(block, root_ref[0, 3], root_ref[1, 3], sources)
     state = []
     for part in range(2):
         old = before_ref[part]
@@ -230,14 +230,6 @@
     got = product(block, leaf_ref[0], leaf_ref[1], sources)
     for part in range(2):
         terms_ref[part] = got[part].astype(BF)
-
-
-def last_kernel(
-    target, place_ref, near_ref, slab_ref, side_ref, opposite_ref, back_ref, before_ref, root_ref, state_ref
-):
-    advanced(
-        target, True, place_ref, near_ref, slab_ref, side_ref, opposite_ref, back_ref, before_ref, root_ref, state_ref
-    )
 
 
 def sums_kernel(own_ref, by_a_ref, by_b_ref, first_ref, last_ref, out_ref):
@@ -304,9 +296,13 @@
 
 
 def closing_kernel(
-    place_ref, own_w_ref, a_w_ref, b_w_ref, state_ref, got_a_ref, got_b_ref, parcel_a_ref, parcel_b_ref, parcel_ref,
-    own_ref, leaf_a_ref, leaf_b_ref, low_ref, high_ref, enter_ref, leave_ref, vector_ref, near_ref, far_ref,
+    target, place_ref, own_w_ref, a_w_ref, b_w_ref, near_ref, slab_ref, side_ref, opposite_ref, back_ref, before_ref,
+    root_ref, got_a_ref, got_b_ref, parcel_a_ref, parcel_b_ref, parcel_ref, own_ref, leaf_a_ref, leaf_b_ref,
+    low_ref, high_ref, enter_ref, leave_ref, state_ref, vector_ref, near_rows_ref, far_rows_ref,
 ):
+    here, _ = advanced(
+        target, True, place_ref, near_ref, slab_ref, side_ref, opposite_ref, back_ref, before_ref, root_ref, state_ref
+    )
     sources, planes, width = low_ref.shape[1:]
     rows = enter_ref.shape[2]
     panel = place_ref[1]
@@ -318,9 +314,8 @@
     own_last = entries(own_w_ref, 1, planes - 1)
     own_leaf = [own_ref[0], own_ref[1]]
     lower_leaf = [jnp.where(even, leaf_b_ref[part], leaf_a_ref[part]) for part in range(2)]
-    here, entered, above, below, behind = [], [], [], [], []
-    for part in range(2):
-        here.append(state_ref[part])
+    entered, above, below, behind = [], [], [], []
+    for part in range(2):
         entered.append(jnp.where(lower, jnp.where(even, parcel_b_ref[0, part], parcel_a_ref[0, part]).astype(F32), 0.0))
         above.append(jnp.where(even, got_a_ref[part], got_b_ref[part]).astype(F32))
         below.append(jnp.where(even, got_b_ref[part], got_a_ref[part]).astype(F32))
@@ -348,12 +343,12 @@
                 tile = ref[part, b] + ends[side] * row(0)
                 tile = tile + jnp.where(depth == 0, enter, 0.0) + jnp.where(depth == planes - 1, leave, 0.0)
                 done.append(tile)
-            near_ref[part, b] = jnp.where(even_core, done[1], done[0]).astype(BF)
-            far_ref[part, b] = jnp.where(even_core, done[0], done[1]).astype(BF)
+            near_rows_ref[part, b] = jnp.where(even_core, done[1], done[0]).astype(BF)
+            far_rows_ref[part, b] = jnp.where(even_core, done[0], done[1]).astype(BF)
 
 
 def final_kernel(
-    place_ref, own_w_ref, a_w_ref, b_w_ref, leaf_ref, source_ref, wave_ref, vector_ref, enter_ref, leave_ref,
+    place_ref, own_w_ref, a_w_ref, b_w_ref, leaf_ref, source_ref, wave_ref, vector_ref, late_ref, enter_ref, leave_ref,
     near_ref, far_ref, zlow_ref, zhigh_ref, field_ref, residual_ref,
 ):
     count, planes, rows, width = leaf_ref.shape[1:]
@@ -367,28 +362,31 @@
     )
     prolong = [column(entries(own_w_ref, 1, z), width) for z in range(planes)]
     own_last, own_first = prolong[planes - 1], prolong[0]
+    even = lax.rem(place_ref[1], 2) == 0
     start = pl.program_id(0) * count
     for b in range(count):
+        at = start + b
         field, ends = [], []
         for part in range(2):
-            vec = [vector_ref[part, i, pl.ds(start + b, 1)] for i in range(9)]
+            vec = [vector_ref[part, i, pl.ds(at, 1)] for i in range(9)]
+            lower = jnp.where(even, vec[3], late_ref[part, pl.ds(at, 1)])
             tiles = []
             for z in range(planes):
                 tile = leaf_ref[part, b, z] + prolong[z] * vec[0]
                 if z == 0:
-                    tile = tile + enter_ref[part, b] + below_last * vec[1]
+                    tile = tile + enter_ref[part, at] + below_last * vec[1]
                 if z == planes - 1:
-                    tile = tile + leave_ref[part, b] + above_first * vec[5] + own_last * vec[6]
+                    tile = tile + leave_ref[part, at] + above_first * vec[5] + own_last * vec[6]
                 field_ref[part, b, z] = tile
                 tiles.append(tile)
             field.append(tiles)
-            below = zlow_ref[part, b] + below_last * (vec[3] + vec[8]) + own_first * vec[7]
-            above = zhigh_ref[part, b] + above_first * vec[2] + own_last * vec[4]
+            below = zlow_ref[part, at] + below_last * (lower + vec[8]) + own_first * vec[7]
+            above = zhigh_ref[part, at] + above_first * vec[2] + own_last * vec[4]
             ends.append((below, above))
         for part in range(2):
             tiles = field[part]
-            near_rows = near_ref[part, b].astype(F32)
-            far_rows = far_ref[part, b].astype(F32)
+            near_rows = near_ref[part, at].astype(F32)
+            far_rows = far_ref[part, at].astype(F32)
             low_rows = jnp.where(even_core, jnp.where(low_there, far_rows, 0.0), near_rows)
             high_rows = jnp.where(even_core, near_rows, jnp.where(high_there, far_rows, 0.0))
             for z in range(planes):
@@ -410,27 +408,22 @@
                 residual_ref[part, b, z] = source_ref[part, b, z] - applied
 
 
-def finish(scalars, leaf, source, wave_term, vectors, *planes_in):
+def finish(scalars, leaf, source, *others):
     two, sources, planes, rows, width = source.shape
-    step = 2
+    step = 4
     whole = pl.BlockSpec((two, step, planes, rows, width), lambda i: (0, i, 0, 0, 0))
-    plane = pl.BlockSpec((two, step, rows, width), lambda i: (0, i, 0, 0))
     return pl.pallas_call(
         final_kernel,
         grid=(sources // step,),
-        in_specs=[pl.BlockSpec(memory_space=pltpu.SMEM)] * 4
-        + [
-            whole, whole,
-            pl.BlockSpec((planes, rows, width), lambda i: (0, 0, 0)),
-            pl.BlockSpec(vectors.shape, lambda i: (0, 0, 0, 0)),
-            plane, plane, plane, plane, plane, plane,
-        ],
+        in_specs=[pl.BlockSpec(memory_space=pltpu.SMEM)] * len(scalars)
+        + [whole, whole]
+        + [pl.BlockSpec(memory_space=pltpu.VMEM)] * len(others),
         out_specs=[whole, whole],
         out_shape=[jax.ShapeDtypeStruct(source.shape, F32)] * 2,
-        compiler_params=pltpu.CompilerParams(vmem_limit_bytes=58 * 2**20),
+        compiler_params=pltpu.CompilerParams(vmem_limit_bytes=40 * 2**20),
         cost_estimate=pl.CostEstimate(flops=60000000, bytes_accessed=26000000, transcendentals=0),
         name="finish",
-    )(*scalars, leaf, source, wave_term, vectors, *planes_in)
+    )(*scalars, leaf, source, *others)
 
 
 def after(value, *others):
@@ -445,7 +438,6 @@
     even_panel = panel % 2 == 0
     leaf_matrix = leaf_inverse[:, 0, 0]
     separators = separator_inverse[:, 0, 0]
-    root_matrix = separators[:, 3]
     place = jnp.stack([even_core.astype(jnp.int32), panel, front])
     vector = (two, sources, width)
     shape = jax.ShapeDtypeStruct
@@ -454,6 +446,18 @@
     traded_leaf = {which: swapped(leaf_matrix, which) for which in "AB"}
     traded_weights = {which: swapped(weights, which) for which in "AB"}
     leaf, base_terms, first_plane, last_plane, low_rows, high_rows = leaf_solve(weights, source, leaf_matrix)
+    base_terms = after(base_terms, traded_weights["A"], traded_weights["B"])
+
+    def by_parity(even_value, odd_value):
+        return jnp.where(even_panel, even_value, odd_value)
+
+    by_a = swapped(by_parity(last_plane, first_plane), "A")
+    by_b = swapped(by_parity(first_plane, last_plane), "B")
+    plane = shape(first_plane.shape, F32)
+    planes_got = whole_call(
+        planes_kernel, [plane] * 4, 400000000, "planes", 1,
+        place, by_a, by_b, first_plane, last_plane, leaf_matrix, traded_leaf["A"], traded_leaf["B"], limit=32,
+    )
 
     def halves(block):
         return jnp.where(even_core, block[0], block[1])
@@ -486,7 +490,7 @@
     def gather(level_sums, panels, before):
         own, quad, slab = level_sums
         near = near_part(own, quad, slab, separators)
-        return (near, slab, *inside(slab.astype(BF), panels, 8, 16, 24), before, root_matrix)
+        return (near, slab, *inside(slab.astype(BF), panels, 8, 16, 24), before, separators)
 
     def forward_close(level_sums, panels, target, which, before, parcel):
         got = gather(level_sums, panels, before)
@@ -527,6 +531,11 @@
             state, terms, parcel = forward_close(total, (target,), target, "BA"[turn], state, parcel)
         else:
             state, terms = backward_close(total, (target,), target, False, "A", state, brought)
+        if turn == 0:
+            terms = after(terms, *planes_got)
+    scalars = (place, weights, traded_weights["A"], traded_weights["B"])
+    enter, leave, zlow, zhigh = planes_got
+    edge = shape(low_rows.shape, BF)
     for turn in range(PANELS - 1):
         from_panel = PANELS - 1 - turn
         target = from_panel - 1
@@ -534,36 +543,22 @@
         if turn < PANELS - 2:
             state, terms = backward_close(sums_now, (target,), target, True, "BA"[turn], state, brought)
         else:
+            got_a, got_b = (swapped(state.astype(BF), which) for which in "AB")
             got = gather(sums_now, (target,), state)
-            state = whole_call(
-                functools.partial(last_kernel, target), [shape(vector, F32)], 100000000, "last", 1, place, *got
-            )[0]
-        if turn == 1:
-            traded_b = swapped(state.astype(BF), "B")
-    traded_a = swapped(state.astype(BF), "A")
-
-    def by_parity(even_value, odd_value):
-        return jnp.where(even_panel, even_value, odd_value)
-
-    by_a = swapped(by_parity(last_plane, first_plane), "A")
-    by_b = swapped(by_parity(first_plane, last_plane), "B")
-    plane = shape(first_plane.shape, F32)
-    enter, leave, zlow, zhigh = whole_call(
-        planes_kernel, [plane] * 4, 400000000, "planes", 1,
-        place, by_a, by_b, first_plane, last_plane, leaf_matrix, traded_leaf["A"], traded_leaf["B"],
-    )
-    scalars = (place, weights, traded_weights["A"], traded_weights["B"])
-    edge = shape(low_rows.shape, BF)
-    vectors, near_rows, far_rows = whole_call(
-        closing_kernel, [shape((two, 9, sources, width), F32), edge, edge], 300000000, "closing", 4,
-        *scalars, state, traded_a, traded_b, brought["A"], brought["B"], parcel,
-        leaf_matrix, traded_leaf["A"], traded_leaf["B"], low_rows, high_rows, enter, leave,
-    )
+            state, vectors, near_rows, far_rows = whole_call(
+                functools.partial(closing_kernel, target),
+                [shape(vector, F32), shape((two, 9, sources, width), F32), edge, edge], 300000000, "closing", 4,
+                *scalars, *got, got_a, got_b, brought["A"], brought["B"], parcel,
+                leaf_matrix, traded_leaf["A"], traded_leaf["B"], low_rows, high_rows, enter, leave, limit=32,
+            )
+    late = swapped(state, "A")
     near_front = other_core(near_rows)
     chain = [(p * FRONTS + f, p * FRONTS + (f + 1) % FRONTS) for p in range(PANELS) for f in range(1, FRONTS, 2)]
     far_front = moved(far_rows, pairing(chain))
     return tuple(
-        finish(scalars, leaf, source, wave_term, vectors, enter, leave, near_front, far_front, zlow, zhigh)
+        finish(
+            scalars, leaf, source, wave_term, vectors, late, enter, leave, near_front, far_front, zlow, zhigh
+        )
     )
 
 

time: 206 us -> 210 us (1.019)
  waiting for transfers between devices: 50.3 us -> 72.4 us
  Pallas kernels: 46 us -> 37 us
  starting transfers between devices: 83.6 us -> 79 us
  other arithmetic: 9.17 us -> 4.59 us
    ppermute x61 -> x62, waiting for transfers between devices: 50.3 us -> 72.4 us  [moved(): return lax.ppermute(block, AXES, route)]
    pallas_call x1, Pallas kernels: 16.3 us -> 10.7 us  [finish(): pl.pallas_call(final_kernel, grid=(sources // step,), in_specs=[pl.BlockS...]
    ppermute x61 -> x62, starting transfers between devices: 83.6 us -> 79 us  [moved(): return lax.ppermute(block, AXES, route)]
    pallas_call x1, Pallas kernels: 9.48 us -> 6.64 us  [leaf_solve(): pl.pallas_call(leaf_kernel, grid=(sources // step,), in_specs=[pl.BlockSp...]
    unnamed x81 -> x56, local copies, waits for them, and re-layouts: 14.2 us -> 14.8 us
    pallas_call x17 -> x16, Pallas kernels: 20.2 us -> 19.7 us  [whole_call(): pl.pallas_call(kernel, in_specs=[pl.BlockSpec(memory_space=space) for spa...]
  transfers between devices with their start and end apart: 61 -> 62, of which waited for: 39 -> 43; matrix products, arithmetic and copies ran while one was open for 5% -> 1% of each run, Pallas kernels for 9% -> 8%
where the time goes in v2:
time: 210 us; the launch traced here: 209 us
  starting transfers between devices  79 us (38%)
  waiting for transfers between devices  72.4 us (34%)
  Pallas kernels  37 us (18%)
  local copies, waits for them, and re-layouts  14.9 us (7%)
  other arithmetic  4.59 us (2%)
    ppermute x62, starting transfers between devices, moved(): return lax.ppermute(block, AXES, route)  79 us
    ppermute x62, waiting for transfers between devices, moved(): return lax.ppermute(block, AXES, route)  72.4 us
    pallas_call x16, Pallas kernels, whole_call(): pl.pallas_call(kernel, in_specs=[pl.BlockSpec(memory_space=space) for spa...  19.7 us
    unnamed x56, local copies, waits for them, and re-layouts  14.8 us
    pallas_call x1, Pallas kernels, finish(): pl.pallas_call(final_kernel, grid=(sources // step,), in_specs=[pl.BlockS...  10.7 us
    pallas_call x1, Pallas kernels, leaf_solve(): pl.pallas_call(leaf_kernel, grid=(sources // step,), in_specs=[pl.BlockSp...  6.64 us
  transfers between devices with their start and end apart: 62, of which 43 were waited for; matrix products, arithmetic and copies ran while one was open for 1% of the time, Pallas kernels for 8%

profile of v2, /device:TPU:0, one launch (start us, length us, event | category | flops | bytes accessed | tf_op | source)
XLA Modules:
  0.0 209.2 jit_solution(165989339213674885)
XLA Ops:
  0.6 4.2 %collective-permute-start.7 = (bf16[2,512,512]{2,1,0:T(8,128)(2,1)}, bf16[2,512,512]{2,1,0:T(8,128)(2,1)S(1)}, u32[]{:S(2)}, u32[]{:S(2)}) collective-permute-start(bf16[2,512,512]{2,1,0:T(8,128)(2,1)} %bitcast.149), channel_id=1, source_target_pairs={{0,96},{1,97},{2,98},{3,99},{4,100},{5,101},{6,102},{7,103},{8,104... | collective-permute-start | bytes 3145736 | tf_op jit(solution)/shard_map/ppermute | solution.py:48
  6.0 1.5 collective-permute-start
  7.6 2.8 %copy-done.3 = f32[2,24,8,8,512]{4,3,2,1,0:T(8,128)S(1)} copy-done((f32[2,24,8,8,512]{4,3,2,1,0:T(8,128)S(1)}, f32[2,24,8,8,512]{4,3,2,1,0:T(8,128)}, u32[]{:S(2)}) %copy-start.3) | copy-done | bytes 6291480
  10.4 1.2 copy-done.4
  11.6 6.6 %leaf_solve.1 = (f32[2,24,8,8,512]{4,3,2,1,0:T(8,128)}, f32[4,2,6,512]{3,2,1,0:T(8,128)S(1)}, bf16[2,24,8,512]{3,2,1,0:T(8,128)(2,1)S(1)}, bf16[2,24,8,512]{3,2,...) custom-call(f32[2,8,8]{2,1,0:T(8,128)S(1)} %pad_maximum_fusion.14.weight_ref.own_ref.own_w_ref, ...), custom_call_target="tpu_custom_call" | custom-call | flops 65000000 | bytes 1600000 | tf_op jit(solution)/shard_map/leaf_solve/pallas_call | solution.py:113
  18.2 0.9 copy-done.9
  20.1 8.3 %collective-permute-done.1.by_b_ref.traded_ref.b_w_ref = f32[2,8,8]{2,1,0:T(8,128)S(1)} collective-permute-done((f32[2,8,8]{2,1,0:T(8,128)S(1)}, f32[2,8,8]{2,1,0:T(8,128)S(1)}, u32[]{:S(2)}, u32[]{:S(2)}) %collective-permute-start.1) | collective-permute-done | bytes 544 | tf_op jit(solution)/shard_map/ppermute | solution.py:48
  28.4 1.5 collective-permute-done.by_a_ref.traded_ref.a_w_ref
  30.0 1.2 collective-permute-done.2
  31.2 1.7 collective-permute-start.3
  32.8 2.9 %collective-permute-start.4 = (bf16[24,512]{1,0:T(8,128)(2,1)S(1)}, bf16[24,512]{1,0:T(8,128)(2,1)S(1)}, u32[]{:S(2)}, u32[]{:S(2)}) collective-permute-start(bf16[24,512]{1,0:T(8,128)(2,1)S(1)} %fusion.22), channel_id=1, source_target_pairs={{0,4},{1,5},{2,6},{3,7},{4,0},{5,1},{6,2},{7,3},{8,12},{9,13},{10,... | collective-permute-start | bytes 73736 | tf_op jit(solution)/shard_map/ppermute | solution.py:48
  35.7 2.4 %collective-permute-done.4 = bf16[24,512]{1,0:T(8,128)(2,1)S(1)} collective-permute-done((bf16[24,512]{1,0:T(8,128)(2,1)S(1)}, bf16[24,512]{1,0:T(8,128)(2,1)S(1)}, u32[]{:S(2)}, u32[]{:S(2)}) %collective-permute-start.4) | collective-permute-done | bytes 24608 | tf_op jit(solution)/shard_map/ppermute | solution.py:48
  38.4 1.1 collective-permute-done.5
  40.3 1.6 collective-permute-start.8
  41.9 2.8 %collective-permute-start.9 = (bf16[24,512]{1,0:T(8,128)(2,1)S(1)}, bf16[24,512]{1,0:T(8,128)(2,1)S(1)}, u32[]{:S(2)}, u32[]{:S(2)}) collective-permute-start(bf16[24,512]{1,0:T(8,128)(2,1)S(1)} %fusion.21), channel_id=1, source_target_pairs={{0,16},{1,17},{2,18},{3,19},{4,20},{5,21},{6,22},{7,23},{8,24},{9,... | collective-permute-start | bytes 73736 | tf_op jit(solution)/shard_map/ppermute | solution.py:48
  44.7 2.7 %collective-permute-done.9.opposite_ref = bf16[24,512]{1,0:T(8,128)(2,1)S(1)} collective-permute-done((bf16[24,512]{1,0:T(8,128)(2,1)S(1)}, bf16[24,512]{1,0:T(8,128)(2,1)S(1)}, u32[]{:S(2)}, u32[]{:S(2)}) %collective-permute-start.9) | collective-permute-done | bytes 24608 | tf_op jit(solution)/shard_map/ppermute | solution.py:48
  48.0 2.1 edge_sums.1.sums_ref
  50.0 2.2 %copy-done = bf16[2,1,1,4,512,512]{5,4,3,2,1,0:T(8,128)(2,1)S(1)} copy-done((bf16[2,1,1,4,512,512]{5,4,3,2,1,0:T(8,128)(2,1)S(1)}, bf16[2,1,1,4,512,512]{5,4,3,2,1,0:T(8,128)(2,1)}, u32[]{:S(2)}) %copy-start) | copy-done | bytes 4194328
  52.2 0.9 copy-done.7
  53.1 0.9 copy-done.13
  54.7 1.5 copy-done.1
  56.9 1.4 forward.3
  59.7 1.1 collective-permute-done.11
  61.5 2.7 %collective-permute-start.13 = (bf16[2,24,512]{2,1,0:T(8,128)(2,1)}, bf16[2,24,512]{2,1,0:T(8,128)(2,1)S(1)}, u32[]{:S(2)}, u32[]{:S(2)}) collective-permute-start(bf16[2,24,512]{2,1,0:T(8,128)(2,1)} %add_convert_fusion.5), channel_id=1, source_target_pairs={{0,36},{1,39},{2,38},{3,37},{4,32},{5,35},{6,34},{7,33},{8,44},{9,... | collective-permute-start | bytes 147464 | tf_op jit(solution)/shard_map/ppermute | solution.py:48
  64.1 1.7 collective-permute-start.12
  65.9 2.8 %collective-permute-done.13 = bf16[2,24,512]{2,1,0:T(8,128)(2,1)S(1)} collective-permute-done((bf16[2,24,512]{2,1,0:T(8,128)(2,1)}, bf16[2,24,512]{2,1,0:T(8,128)(2,1)S(1)}, u32[]{:S(2)}, u32[]{:S(2)}) %collective-permute-start.13) | collective-permute-done | bytes 49184 | tf_op jit(solution)/shard_map/ppermute | solution.py:48
  70.0 1.4 collective-permute-start.18
  71.4 1.0 fusion.34
  73.1 0.9 collective-permute-done.16.opposite_ref
  74.4 8.4 %collective-permute-done.19.by_b_ref = bf16[2,24,8,512]{3,2,1,0:T(8,128)(2,1)S(1)} collective-permute-done((bf16[2,24,8,512]{3,2,1,0:T(8,128)(2,1)S(1)}, bf16[2,24,8,512]{3,2,1,0:T(8,128)(2,1)S(1)}, u32[]{:S(2)}, u32[]{:S(2)}) %collective-permute-start.19) | collective-permute-done | bytes 393248 | tf_op jit(solution)/shard_map/ppermute | solution.py:48
  82.7 1.2 copy-done.5
  84.0 2.5 %planes.1 = (f32[2,24,8,512]{3,2,1,0:T(8,128)S(1)}, f32[2,24,8,512]{3,2,1,0:T(8,128)S(1)}, f32[2,24,8,512]{3,2,1,0:T(8,128)S(1)}, f32[2,24,8,512]{3,2,1,0:T(8,128)S(1)}) custom-call(s32[3]{0:T(128)S(1)} %pad_add_fusion.place_ref, bf16[2,24,8,512]{3,2,1,0:T(8,128)(2,1)S(1)} %collective-permute-done.18.by_a_ref, ...), custom_call_target="tpu_custom_call" | custom-call | flops 400000000 | bytes 2000000 | tf_op jit(solution)/shard_map/planes/pallas_call | solution.py:139
  87.2 1.4 forward.4
  88.7 1.2 collective-permute-done.20
  92.0 1.0 collective-permute-done.23
  93.7 1.0 collective-permute-done.25.opposite_ref
  96.1 1.4 forward.5
  97.7 1.1 collective-permute-done.27
  100.7 1.0 collective-permute-done.30
  102.4 19.8 %collective-permute-start.35 = (bf16[2,2,24,512]{3,2,1,0:T(8,128)(2,1)S(1)}, bf16[2,2,24,512]{3,2,1,0:T(8,128)(2,1)S(1)}, u32[]{:S(2)}, u32[]{:S(2)}) collective-permute-start(bf16[2,2,24,512]{3,2,1,0:T(8,128)(2,1)S(1)} %get-tuple-element.50.parcel_ref), channel_id=1, source_target_pairs={{0,96},{1,97},{2,98},{3,99},{4,100},{5,101},{6,102},{7,103},{8,104... | collective-permute-start | bytes 294920 | tf_op jit(solution)/shard_map/ppermute | solution.py:48
  123.0 1.8 collective-permute-done.35.by_b_ref.parcel_b_ref
  124.8 2.0 collective-permute-done.34.by_a_ref.parcel_a_ref
  126.8 1.4 backward.3
  128.3 1.2 collective-permute-done.36
  131.5 1.0 collective-permute-done.39
  133.1 1.0 collective-permute-done.41.opposite_ref
  135.5 1.4 backward.4
  137.1 1.1 collective-permute-done.43
  140.1 1.0 collective-permute-done.46
  141.7 1.0 collective-permute-done.48.opposite_ref
  144.1 1.4 backward.5
  145.7 1.1 collective-permute-done.50
  146.8 21.4 %collective-permute-start.52 = (bf16[2,24,512]{2,1,0:T(8,128)(2,1)S(1)}, bf16[2,24,512]{2,1,0:T(8,128)(2,1)S(1)}, u32[]{:S(2)}, u32[]{:S(2)}) collective-permute-start(bf16[2,24,512]{2,1,0:T(8,128)(2,1)S(1)} %add_convert_fusion), channel_id=1, source_target_pairs={{0,36},{1,39},{2,38},{3,37},{4,32},{5,35},{6,34},{7,33},{8,44},{9,... | collective-permute-start | bytes 147464 | tf_op jit(solution)/shard_map/ppermute | solution.py:48
  168.2 2.1 %collective-permute-done.52 = bf16[2,24,512]{2,1,0:T(8,128)(2,1)S(1)} collective-permute-done((bf16[2,24,512]{2,1,0:T(8,128)(2,1)S(1)}, bf16[2,24,512]{2,1,0:T(8,128)(2,1)S(1)}, u32[]{:S(2)}, u32[]{:S(2)}) %collective-permute-start.52) | collective-permute-done | bytes 49184 | tf_op jit(solution)/shard_map/ppermute | solution.py:48
  170.3 2.4 %collective-permute-done.51 = bf16[2,24,512]{2,1,0:T(8,128)(2,1)S(1)} collective-permute-done((bf16[2,24,512]{2,1,0:T(8,128)(2,1)S(1)}, bf16[2,24,512]{2,1,0:T(8,128)(2,1)S(1)}, u32[]{:S(2)}, u32[]{:S(2)}) %collective-permute-start.51) | collective-permute-done | bytes 49184 | tf_op jit(solution)/shard_map/ppermute | solution.py:48
  172.7 1.3 collective-permute-done.53
  174.7 2.3 %collective-permute-start.55 = (bf16[24,512]{1,0:T(8,128)(2,1)S(1)}, bf16[24,512]{1,0:T(8,128)(2,1)S(1)}, u32[]{:S(2)}, u32[]{:S(2)}) collective-permute-start(bf16[24,512]{1,0:T(8,128)(2,1)S(1)} %fusion.15), channel_id=1, source_target_pairs={{0,16},{1,17},{2,18},{3,19},{4,20},{5,21},{6,22},{7,23},{8,24},{9,... | collective-permute-start | bytes 73736 | tf_op jit(solution)/shard_map/ppermute | solution.py:48
  177.0 3.0 %collective-permute-done.55.opposite_ref = bf16[24,512]{1,0:T(8,128)(2,1)S(1)} collective-permute-done((bf16[24,512]{1,0:T(8,128)(2,1)S(1)}, bf16[24,512]{1,0:T(8,128)(2,1)S(1)}, u32[]{:S(2)}, u32[]{:S(2)}) %collective-permute-start.55) | collective-permute-done | bytes 24608 | tf_op jit(solution)/shard_map/ppermute | solution.py:48
  181.0 4.6 %collective-permute-done.58.got_b_ref = bf16[2,24,512]{2,1,0:T(8,128)(2,1)S(1)} collective-permute-done((bf16[2,24,512]{2,1,0:T(8,128)(2,1)S(1)}, bf16[2,24,512]{2,1,0:T(8,128)(2,1)S(1)}, u32[]{:S(2)}, u32[]{:S(2)}) %collective-permute-start.58) | collective-permute-done | bytes 49184 | tf_op jit(solution)/shard_map/ppermute | solution.py:48
  185.6 2.2 %closing.1 = (f32[2,24,512]{2,1,0:T(8,128)S(1)}, f32[2,9,24,512]{3,2,1,0:T(8,128)S(1)}, bf16[2,24,8,512]{3,2,1,0:T(8,128)(2,1)S(1)}, bf16[2,24,8,512]{3,2,1,0:T(8,128)(2,1)S(1)}) custom-call(s32[3]{0:T(128)S(1)} %pad_add_fusion.place_ref, f32[2,8,8]{2,1,0:T(8,128)S(1)} %pad_maximum_fusion.14.weight_ref.own_ref.own_w_ref, ...), custom_call_target="tpu_custom_call" | custom-call | flops 300000000 | bytes 1500000 | tf_op jit(solution)/shard_map/closing/pallas_call | solution.py:139
  187.9 3.4 %collective-permute-start.61 = (bf16[2,24,8,512]{3,2,1,0:T(8,128)(2,1)S(1)}, bf16[2,24,8,512]{3,2,1,0:T(8,128)(2,1)S(1)}, u32[]{:S(2)}, u32[]{:S(2)}) collective-permute-start(bf16[2,24,8,512]{3,2,1,0:T(8,128)(2,1)S(1)} %get-tuple-element.65), channel_id=1, source_target_pairs={{0,31},{1,2},{2,1},{3,4},{4,3},{5,6},{6,5},{7,8},{8,7},{9,10},{10,... | collective-permute-start | bytes 1179656 | tf_op jit(solution)/shard_map/ppermute | solution.py:48
  191.3 4.6 %collective-permute-done.59.late_ref = f32[2,24,512]{2,1,0:T(8,128)S(1)} collective-permute-done((f32[2,24,512]{2,1,0:T(8,128)S(1)}, f32[2,24,512]{2,1,0:T(8,128)S(1)}, u32[]{:S(2)}, u32[]{:S(2)}) %collective-permute-start.59) | collective-permute-done | bytes 98336 | tf_op jit(solution)/shard_map/ppermute | solution.py:48
  196.0 2.6 %collective-permute-done.61.far_ref = bf16[2,24,8,512]{3,2,1,0:T(8,128)(2,1)S(1)} collective-permute-done((bf16[2,24,8,512]{3,2,1,0:T(8,128)(2,1)S(1)}, bf16[2,24,8,512]{3,2,1,0:T(8,128)(2,1)S(1)}, u32[]{:S(2)}, u32[]{:S(2)}) %collective-permute-start.61) | collective-permute-done | bytes 393248 | tf_op jit(solution)/shard_map/ppermute | solution.py:48
  198.6 10.7 %finish.1 = (f32[2,24,8,8,512]{4,3,2,1,0:T(8,128)}, f32[2,24,8,8,512]{4,3,2,1,0:T(8,128)}) custom-call(s32[3]{0:T(128)S(1)} %pad_add_fusion.place_ref, f32[2,8,8]{2,1,0:T(8,128)S(1)} %pad_maximum_fusion.14.weight_ref.own_ref.own_w_ref, f32[2,8,8]{2,1,0:T(8,128)S(1)} %collective-permute-done.by_a_ref.traded_ref.a_w_ref, ...), custom_call_target="tpu_custom_call" | custom-call | flops 60000000 | bytes 26000000 | tf_op jit(solution)/shard_map/finish/pallas_call | solution.py:415
  (187 shorter events, 28.4 us)
Async XLA Ops:
  0.6 39.6 %collective-permute-start.7 = (bf16[2,512,512]{2,1,0:T(8,128)(2,1)}, bf16[2,512,512]{2,1,0:T(8,128)(2,1)S(1)}, u32[]{:S(2)}, u32[]{:S(2)}) collective-permute-start(bf16[2,512,512]{2,1,0:T(8,128)(2,1)} %bitcast.149), channel_id=1, source_target_pairs={{0,96},{1,97},{2,98},{3,99},{4,100},{5,101},{6,102},{7,103},{8,104... | collective-permute-start | bytes 3145736 | tf_op jit(solution)/shard_map/ppermute | solution.py:48
  4.8 35.4 %collective-permute-start.6 = (bf16[2,512,512]{2,1,0:T(8,128)(2,1)}, bf16[2,512,512]{2,1,0:T(8,128)(2,1)S(1)}, u32[]{:S(2)}, u32[]{:S(2)}) collective-permute-start(bf16[2,512,512]{2,1,0:T(8,128)(2,1)} %bitcast.150), channel_id=1, source_target_pairs={{0,32},{1,33},{2,34},{3,35},{4,36},{5,37},{6,38},{7,39},{8,40},{9,... | collective-permute-start | bytes 3145736 | tf_op jit(solution)/shard_map/ppermute | solution.py:48
  5.5 22.8 %collective-permute-start.1 = (f32[2,8,8]{2,1,0:T(8,128)S(1)}, f32[2,8,8]{2,1,0:T(8,128)S(1)}, u32[]{:S(2)}, u32[]{:S(2)}) collective-permute-start(f32[2,8,8]{2,1,0:T(8,128)S(1)} %pad_maximum_fusion.14.weight_ref.own_ref.own_w_ref), channel_id=1, source_target_pairs={{0,96},{1,97},{2,98},{3,99},{4,100},{5,101},{6,102},{7,103},{8,104... | collective-permute-start | bytes 1544 | tf_op jit(solution)/shard_map/ppermute | solution.py:48
  6.0 23.8 %collective-permute-start = (f32[2,8,8]{2,1,0:T(8,128)S(1)}, f32[2,8,8]{2,1,0:T(8,128)S(1)}, u32[]{:S(2)}, u32[]{:S(2)}) collective-permute-start(f32[2,8,8]{2,1,0:T(8,128)S(1)} %pad_maximum_fusion.14.weight_ref.own_ref.own_w_ref), channel_id=1, source_target_pairs={{0,32},{1,33},{2,34},{3,35},{4,36},{5,37},{6,38},{7,39},{8,40},{9,... | collective-permute-start | bytes 1544 | tf_op jit(solution)/shard_map/ppermute | solution.py:48
  29.8 1.3 collective-permute-start.2
  31.2 7.0 %collective-permute-start.3 = (bf16[2,24,512]{2,1,0:T(8,128)(2,1)S(1)}, bf16[2,24,512]{2,1,0:T(8,128)(2,1)S(1)}, u32[]{:S(2)}, u32[]{:S(2)}) collective-permute-start(bf16[2,24,512]{2,1,0:T(8,128)(2,1)S(1)} %fusion.23), channel_id=1, source_target_pairs={{0,2},{1,7},{2,0},{3,5},{4,6},{5,3},{6,4},{7,1},{8,10},{9,15},{10,... | collective-permute-start | bytes 147464 | tf_op jit(solution)/shard_map/ppermute | solution.py:48
  32.8 5.3 %collective-permute-start.4 = (bf16[24,512]{1,0:T(8,128)(2,1)S(1)}, bf16[24,512]{1,0:T(8,128)(2,1)S(1)}, u32[]{:S(2)}, u32[]{:S(2)}) collective-permute-start(bf16[24,512]{1,0:T(8,128)(2,1)S(1)} %fusion.22), channel_id=1, source_target_pairs={{0,4},{1,5},{2,6},{3,7},{4,0},{5,1},{6,2},{7,3},{8,12},{9,13},{10,... | collective-permute-start | bytes 73736 | tf_op jit(solution)/shard_map/ppermute | solution.py:48
  38.2 1.3 collective-permute-start.5
  40.3 7.1 %collective-permute-start.8 = (bf16[2,24,512]{2,1,0:T(8,128)(2,1)S(1)}, bf16[2,24,512]{2,1,0:T(8,128)(2,1)S(1)}, u32[]{:S(2)}, u32[]{:S(2)}) collective-permute-start(bf16[2,24,512]{2,1,0:T(8,128)(2,1)S(1)} %convert_element_type.166), channel_id=1, source_target_pairs={{0,8},{1,25},{2,10},{3,27},{4,12},{5,29},{6,14},{7,31},{8,0},{9,17... | collective-permute-start | bytes 147464 | tf_op jit(solution)/shard_map/ppermute | solution.py:48
  41.9 5.5 %collective-permute-start.9 = (bf16[24,512]{1,0:T(8,128)(2,1)S(1)}, bf16[24,512]{1,0:T(8,128)(2,1)S(1)}, u32[]{:S(2)}, u32[]{:S(2)}) collective-permute-start(bf16[24,512]{1,0:T(8,128)(2,1)S(1)} %fusion.21), channel_id=1, source_target_pairs={{0,16},{1,17},{2,18},{3,19},{4,20},{5,21},{6,22},{7,23},{8,24},{9,... | collective-permute-start | bytes 73736 | tf_op jit(solution)/shard_map/ppermute | solution.py:48
  47.4 7.3 %collective-permute-start.10 = (bf16[3,24,512]{2,1,0:T(8,128)(2,1)S(1)}, bf16[3,24,512]{2,1,0:T(8,128)(2,1)S(1)}, u32[]{:S(2)}, u32[]{:S(2)}) collective-permute-start(bf16[3,24,512]{2,1,0:T(8,128)(2,1)S(1)} %pad_maximum_fusion.7), channel_id=1, source_target_pairs={{0,1},{1,0},{2,3},{3,2},{4,5},{5,4},{6,7},{7,6},{8,9},{9,8},{10,11... | collective-permute-start | bytes 221192 | tf_op jit(solution)/shard_map/ppermute | solution.py:48
  59.6 1.2 collective-permute-start.11
  61.5 7.2 %collective-permute-start.13 = (bf16[2,24,512]{2,1,0:T(8,128)(2,1)}, bf16[2,24,512]{2,1,0:T(8,128)(2,1)S(1)}, u32[]{:S(2)}, u32[]{:S(2)}) collective-permute-start(bf16[2,24,512]{2,1,0:T(8,128)(2,1)} %add_convert_fusion.5), channel_id=1, source_target_pairs={{0,36},{1,39},{2,38},{3,37},{4,32},{5,35},{6,34},{7,33},{8,44},{9,... | collective-permute-start | bytes 147464 | tf_op jit(solution)/shard_map/ppermute | solution.py:48
  64.1 4.8 %collective-permute-start.12 = (bf16[2,24,512]{2,1,0:T(8,128)(2,1)}, bf16[2,24,512]{2,1,0:T(8,128)(2,1)}, u32[]{:S(2)}, u32[]{:S(2)}) collective-permute-start(bf16[2,24,512]{2,1,0:T(8,128)(2,1)} %add_convert_fusion.5), channel_id=1, source_target_pairs={{0,32},{1,35},{2,34},{3,33},{4,36},{5,39},{6,38},{7,37},{8,40},{9,... | collective-permute-start | bytes 147464 | tf_op jit(solution)/shard_map/ppermute | solution.py:48
  69.8 1.6 collective-permute-start.14
  69.9 12.8 %collective-permute-start.19 = (bf16[2,24,8,512]{3,2,1,0:T(8,128)(2,1)S(1)}, bf16[2,24,8,512]{3,2,1,0:T(8,128)(2,1)S(1)}, u32[]{:S(2)}, u32[]{:S(2)}) collective-permute-start(bf16[2,24,8,512]{3,2,1,0:T(8,128)(2,1)S(1)} %get-tuple-element.81), channel_id=1, source_target_pairs={{0,96},{1,97},{2,98},{3,99},{4,100},{5,101},{6,102},{7,103},{8,104... | collective-permute-start | bytes 1179656 | tf_op jit(solution)/shard_map/ppermute | solution.py:48
  70.0 12.7 %collective-permute-start.18 = (bf16[2,24,8,512]{3,2,1,0:T(8,128)(2,1)S(1)}, bf16[2,24,8,512]{3,2,1,0:T(8,128)(2,1)S(1)}, u32[]{:S(2)}, u32[]{:S(2)}) collective-permute-start(bf16[2,24,8,512]{3,2,1,0:T(8,128)(2,1)S(1)} %get-tuple-element.82), channel_id=1, source_target_pairs={{0,32},{1,33},{2,34},{3,35},{4,36},{5,37},{6,38},{7,39},{8,40},{9,... | collective-permute-start | bytes 1179656 | tf_op jit(solution)/shard_map/ppermute | solution.py:48
  72.5 1.5 collective-permute-start.15
  72.8 1.2 collective-permute-start.16
  74.0 13.2 %collective-permute-start.17 = (bf16[3,24,512]{2,1,0:T(8,128)(2,1)S(1)}, bf16[3,24,512]{2,1,0:T(8,128)(2,1)S(1)}, u32[]{:S(2)}, u32[]{:S(2)}) collective-permute-start(bf16[3,24,512]{2,1,0:T(8,128)(2,1)S(1)} %pad_maximum_fusion.8), channel_id=1, source_target_pairs={{0,1},{1,0},{2,3},{3,2},{4,5},{5,4},{6,7},{7,6},{8,9},{9,8},{10,11... | collective-permute-start | bytes 221192 | tf_op jit(solution)/shard_map/ppermute | solution.py:48
  88.6 1.3 collective-permute-start.20
  89.9 1.5 collective-permute-start.22
  90.4 1.2 collective-permute-start.21
  91.6 1.4 collective-permute-start.23
  93.1 1.6 collective-permute-start.24
  93.5 1.2 collective-permute-start.25
  94.7 1.3 collective-permute-start.26
  97.5 1.3 collective-permute-start.27
  98.8 1.3 collective-permute-start.29
  99.1 1.2 collective-permute-start.28
  100.3 1.4 collective-permute-start.30
  101.8 20.4 %collective-permute-start.31 = (bf16[2,24,512]{2,1,0:T(8,128)(2,1)S(1)}, bf16[2,24,512]{2,1,0:T(8,128)(2,1)S(1)}, u32[]{:S(2)}, u32[]{:S(2)}) collective-permute-start(bf16[2,24,512]{2,1,0:T(8,128)(2,1)S(1)} %get-tuple-element.75), channel_id=1, source_target_pairs={{0,1},{1,0},{2,3},{3,2},{4,5},{5,4},{6,7},{7,6},{8,9},{9,8},{10,11... | collective-permute-start | bytes 147464 | tf_op jit(solution)/shard_map/ppermute | solution.py:48
  102.2 20.0 %collective-permute-start.32 = (bf16[24,512]{1,0:T(8,128)(2,1)S(1)}, bf16[24,512]{1,0:T(8,128)(2,1)S(1)}, u32[]{:S(2)}, u32[]{:S(2)}) collective-permute-start(bf16[24,512]{1,0:T(8,128)(2,1)S(1)} %fusion.18), channel_id=1, source_target_pairs={{0,1},{1,0},{2,3},{3,2},{4,5},{5,4},{6,7},{7,6},{8,9},{9,8},{10,11... | collective-permute-start | bytes 73736 | tf_op jit(solution)/shard_map/ppermute | solution.py:48
  102.4 22.4 %collective-permute-start.35 = (bf16[2,2,24,512]{3,2,1,0:T(8,128)(2,1)S(1)}, bf16[2,2,24,512]{3,2,1,0:T(8,128)(2,1)S(1)}, u32[]{:S(2)}, u32[]{:S(2)}) collective-permute-start(bf16[2,2,24,512]{3,2,1,0:T(8,128)(2,1)S(1)} %get-tuple-element.50.parcel_ref), channel_id=1, source_target_pairs={{0,96},{1,97},{2,98},{3,99},{4,100},{5,101},{6,102},{7,103},{8,104... | collective-permute-start | bytes 294920 | tf_op jit(solution)/shard_map/ppermute | solution.py:48
  122.2 4.6 %collective-permute-start.34 = (bf16[2,2,24,512]{3,2,1,0:T(8,128)(2,1)S(1)}, bf16[2,2,24,512]{3,2,1,0:T(8,128)(2,1)S(1)}, u32[]{:S(2)}, u32[]{:S(2)}) collective-permute-start(bf16[2,2,24,512]{3,2,1,0:T(8,128)(2,1)S(1)} %get-tuple-element.53.parcel_ref), channel_id=1, source_target_pairs={{0,32},{1,33},{2,34},{3,35},{4,36},{5,37},{6,38},{7,39},{8,40},{9,... | collective-permute-start | bytes 294920 | tf_op jit(solution)/shard_map/ppermute | solution.py:48
  122.3 4.6 %collective-permute-start.33 = (bf16[3,24,512]{2,1,0:T(8,128)(2,1)S(1)}, bf16[3,24,512]{2,1,0:T(8,128)(2,1)S(1)}, u32[]{:S(2)}, u32[]{:S(2)}) collective-permute-start(bf16[3,24,512]{2,1,0:T(8,128)(2,1)S(1)} %pad_maximum_fusion.10), channel_id=1, source_target_pairs={{0,1},{1,0},{2,3},{3,2},{4,5},{5,4},{6,7},{7,6},{8,9},{9,8},{10,11... | collective-permute-start | bytes 221192 | tf_op jit(solution)/shard_map/ppermute | solution.py:48
  128.2 1.3 collective-permute-start.36
  129.5 1.3 collective-permute-start.38
  129.8 1.2 collective-permute-start.37
  131.0 1.4 collective-permute-start.39
  132.5 1.6 collective-permute-start.40
  132.9 1.2 collective-permute-start.41
  134.1 1.3 collective-permute-start.42
  136.8 1.3 collective-permute-start.43
  138.2 1.3 collective-permute-start.45
  138.4 1.2 collective-permute-start.44
  139.6 1.4 collective-permute-start.46
  141.1 1.6 collective-permute-start.47
  141.5 1.2 collective-permute-start.48
  142.7 1.3 collective-permute-start.49
  144.1 41.5 %copy-start.10 = (f32[2,24,8,512]{3,2,1,0:T(8,128)S(1)}, f32[2,24,8,512]{3,2,1,0:T(8,128)}, u32[]{:S(2)}) copy-start(f32[2,24,8,512]{3,2,1,0:T(8,128)} %copy-done.9) | copy-start | bytes 2359300
  144.1 41.5 %copy-start.12 = (f32[2,24,8,512]{3,2,1,0:T(8,128)S(1)}, f32[2,24,8,512]{3,2,1,0:T(8,128)}, u32[]{:S(2)}) copy-start(f32[2,24,8,512]{3,2,1,0:T(8,128)} %copy-done.11) | copy-start | bytes 2359300
  145.5 1.3 collective-permute-start.50
  146.8 23.5 %collective-permute-start.52 = (bf16[2,24,512]{2,1,0:T(8,128)(2,1)S(1)}, bf16[2,24,512]{2,1,0:T(8,128)(2,1)S(1)}, u32[]{:S(2)}, u32[]{:S(2)}) collective-permute-start(bf16[2,24,512]{2,1,0:T(8,128)(2,1)S(1)} %add_convert_fusion), channel_id=1, source_target_pairs={{0,36},{1,39},{2,38},{3,37},{4,32},{5,35},{6,34},{7,33},{8,44},{9,... | collective-permute-start | bytes 147464 | tf_op jit(solution)/shard_map/ppermute | solution.py:48
  168.2 4.5 %collective-permute-start.51 = (bf16[2,24,512]{2,1,0:T(8,128)(2,1)S(1)}, bf16[2,24,512]{2,1,0:T(8,128)(2,1)S(1)}, u32[]{:S(2)}, u32[]{:S(2)}) collective-permute-start(bf16[2,24,512]{2,1,0:T(8,128)(2,1)S(1)} %add_convert_fusion), channel_id=1, source_target_pairs={{0,32},{1,35},{2,34},{3,33},{4,36},{5,39},{6,38},{7,37},{8,40},{9,... | collective-permute-start | bytes 147464 | tf_op jit(solution)/shard_map/ppermute | solution.py:48
  172.6 1.4 collective-permute-start.53
  174.1 5.9 %collective-permute-start.54 = (bf16[2,24,512]{2,1,0:T(8,128)(2,1)S(1)}, bf16[2,24,512]{2,1,0:T(8,128)(2,1)S(1)}, u32[]{:S(2)}, u32[]{:S(2)}) collective-permute-start(bf16[2,24,512]{2,1,0:T(8,128)(2,1)S(1)} %get-tuple-element.66), channel_id=1, source_target_pairs={{0,8},{1,25},{2,10},{3,27},{4,12},{5,29},{6,14},{7,31},{8,0},{9,17... | collective-permute-start | bytes 147464 | tf_op jit(solution)/shard_map/ppermute | solution.py:48
  174.7 5.3 %collective-permute-start.55 = (bf16[24,512]{1,0:T(8,128)(2,1)S(1)}, bf16[24,512]{1,0:T(8,128)(2,1)S(1)}, u32[]{:S(2)}, u32[]{:S(2)}) collective-permute-start(bf16[24,512]{1,0:T(8,128)(2,1)S(1)} %fusion.15), channel_id=1, source_target_pairs={{0,16},{1,17},{2,18},{3,19},{4,20},{5,21},{6,22},{7,23},{8,24},{9,... | collective-permute-start | bytes 73736 | tf_op jit(solution)/shard_map/ppermute | solution.py:48
  180.0 5.5 %collective-permute-start.56 = (bf16[3,24,512]{2,1,0:T(8,128)(2,1)S(1)}, bf16[3,24,512]{2,1,0:T(8,128)(2,1)S(1)}, u32[]{:S(2)}, u32[]{:S(2)}) collective-permute-start(bf16[3,24,512]{2,1,0:T(8,128)(2,1)S(1)} %pad_maximum_fusion.13), channel_id=1, source_target_pairs={{0,1},{1,0},{2,3},{3,2},{4,5},{5,4},{6,7},{7,6},{8,9},{9,8},{10,11... | collective-permute-start | bytes 221192 | tf_op jit(solution)/shard_map/ppermute | solution.py:48
  180.1 5.4 %collective-permute-start.58 = (bf16[2,24,512]{2,1,0:T(8,128)(2,1)S(1)}, bf16[2,24,512]{2,1,0:T(8,128)(2,1)S(1)}, u32[]{:S(2)}, u32[]{:S(2)}) collective-permute-start(bf16[2,24,512]{2,1,0:T(8,128)(2,1)S(1)} %convert_element_type.209), channel_id=1, source_target_pairs={{0,96},{1,97},{2,98},{3,99},{4,100},{5,101},{6,102},{7,103},{8,104... | collective-permute-start | bytes 147464 | tf_op jit(solution)/shard_map/ppermute | solution.py:48
  180.2 5.3 %collective-permute-start.57 = (bf16[2,24,512]{2,1,0:T(8,128)(2,1)S(1)}, bf16[2,24,512]{2,1,0:T(8,128)(2,1)S(1)}, u32[]{:S(2)}, u32[]{:S(2)}) collective-permute-start(bf16[2,24,512]{2,1,0:T(8,128)(2,1)S(1)} %convert_element_type.209), channel_id=1, source_target_pairs={{0,32},{1,33},{2,34},{3,35},{4,36},{5,37},{6,38},{7,39},{8,40},{9,... | collective-permute-start | bytes 147464 | tf_op jit(solution)/shard_map/ppermute | solution.py:48
  187.8 8.1 %collective-permute-start.60 = (bf16[2,24,8,512]{3,2,1,0:T(8,128)(2,1)S(1)}, bf16[2,24,8,512]{3,2,1,0:T(8,128)(2,1)S(1)}, u32[]{:S(2)}, u32[]{:S(2)}) collective-permute-start(bf16[2,24,8,512]{3,2,1,0:T(8,128)(2,1)S(1)} %get-tuple-element.64), channel_id=1, source_target_pairs={{0,1},{1,0},{2,3},{3,2},{4,5},{5,4},{6,7},{7,6},{8,9},{9,8},{10,11... | collective-permute-start | bytes 1179656 | tf_op jit(solution)/shard_map/ppermute | solution.py:48
  187.9 10.6 %collective-permute-start.61 = (bf16[2,24,8,512]{3,2,1,0:T(8,128)(2,1)S(1)}, bf16[2,24,8,512]{3,2,1,0:T(8,128)(2,1)S(1)}, u32[]{:S(2)}, u32[]{:S(2)}) collective-permute-start(bf16[2,24,8,512]{3,2,1,0:T(8,128)(2,1)S(1)} %get-tuple-element.65), channel_id=1, source_target_pairs={{0,31},{1,2},{2,1},{3,4},{4,3},{5,6},{6,5},{7,8},{8,7},{9,10},{10,... | collective-permute-start | bytes 1179656 | tf_op jit(solution)/shard_map/ppermute | solution.py:48
  191.3 4.6 %collective-permute-start.59 = (f32[2,24,512]{2,1,0:T(8,128)S(1)}, f32[2,24,512]{2,1,0:T(8,128)S(1)}, u32[]{:S(2)}, u32[]{:S(2)}) collective-permute-start(f32[2,24,512]{2,1,0:T(8,128)S(1)} %get-tuple-element.63), channel_id=1, source_target_pairs={{0,32},{1,33},{2,34},{3,35},{4,36},{5,37},{6,38},{7,39},{8,40},{9,... | collective-permute-start | bytes 294920 | tf_op jit(solution)/shard_map/ppermute | solution.py:48
  (26 other events, 193.1 us)

commit v3 on v2

--- a/solution.py
+++ b/solution.py
@@ -102,12 +102,12 @@
         total = shaped[:, 0] * columns[0][None]
         for z in range(1, planes):
             total = total + shaped[:, z] * columns[z][None]
-        total_ref[0, part] = jnp.sum(total, axis=1)
+        total_ref[part] = jnp.sum(total, axis=1).astype(BF)
 
 
 def leaf_solve(weights, source, matrix):
     two, sources, planes, rows, width = source.shape
-    step = 6
+    step = 8
     whole = pl.BlockSpec((two, step, planes, rows, width), lambda i: (0, i, 0, 0, 0))
     plane = pl.BlockSpec((two, step, rows, width), lambda i: (0, i, 0, 0))
     leaf, total, first, last, low, high = pl.pallas_call(
@@ -118,20 +118,20 @@
             whole,
             pl.BlockSpec((two, width, width), lambda i: (0, 0, 0)),
         ],
-        out_specs=[whole, pl.BlockSpec((1, two, step, width), lambda i: (i, 0, 0, 0)), plane, plane, plane, plane],
+        out_specs=[whole, pl.BlockSpec((two, step, width), lambda i: (0, i, 0)), plane, plane, plane, plane],
         out_shape=[
             pltpu.HBM(source.shape, F32),
-            jax.ShapeDtypeStruct((sources // step, two, step, width), F32),
+            jax.ShapeDtypeStruct((two, sources, width), BF),
             jax.ShapeDtypeStruct((two, sources, rows, width), BF),
             jax.ShapeDtypeStruct((two, sources, rows, width), BF),
-            jax.ShapeDtypeStruct((two, sources, planes, width), F32),
-            jax.ShapeDtypeStruct((two, sources, planes, width), F32),
+            pltpu.HBM((two, sources, planes, width), F32),
+            pltpu.HBM((two, sources, planes, width), F32),
         ],
-        compiler_params=pltpu.CompilerParams(vmem_limit_bytes=32 * 2**20),
+        compiler_params=pltpu.CompilerParams(vmem_limit_bytes=46 * 2**20),
         cost_estimate=pl.CostEstimate(flops=65000000, bytes_accessed=1600000, transcendentals=0),
         name="leaf_solve",
     )(weights, source, matrix)
-    return leaf, total.transpose(1, 0, 2, 3).reshape(two, sources, width), first, last, low, high
+    return leaf, total, first, last, low, high
 
 
 def whole_call(kernel, shapes, cost, name, smem, *args, limit=14):
@@ -189,7 +189,7 @@
 
 def forward_kernel(
     target, which, place_ref, own_ref, traded_ref, near_ref, slab_ref, side_ref, opposite_ref, back_ref, before_ref,
-    root_ref, leaf_ref, sums_ref, parcel_ref, state_ref, terms_ref, out_ref,
+    root_ref, leaf_real_ref, leaf_imag_ref, sums_ref, parcel_ref, state_ref, terms_ref, out_ref,
 ):
     state, active = advanced(
         target, False, place_ref, near_ref, slab_ref, side_ref, opposite_ref, back_ref, before_ref, root_ref, state_ref
@@ -203,7 +203,7 @@
         here = state[part]
         rows += [sums_ref["AB".index(which), part] + scale * here, here, sums_ref[2, part] + own_scale * here]
     block = jnp.concatenate(rows, axis=0).astype(BF)
-    got = product(block, leaf_ref[0], leaf_ref[1], 3 * sources)
+    got = product(block, leaf_real_ref[...], leaf_imag_ref[...], 3 * sources)
     for part in range(2):
         terms_ref[part] = got[part][:sources].astype(BF)
         for i in range(2):
@@ -213,7 +213,7 @@
 
 def backward_kernel(
     target, keep, which, place_ref, own_ref, traded_ref, near_ref, slab_ref, side_ref, opposite_ref, back_ref, before_ref,
-    root_ref, leaf_ref, sums_ref, by_a_ref, by_b_ref, state_ref, terms_ref,
+    root_ref, leaf_real_ref, leaf_imag_ref, sums_ref, by_a_ref, by_b_ref, state_ref, terms_ref,
 ):
     state, _ = advanced(
         target, keep, place_ref, near_ref, slab_ref, side_ref, opposite_ref, back_ref, before_ref, root_ref, state_ref
@@ -227,7 +227,7 @@
         echo = jnp.where(even_panel, by_b_ref[1, part], by_a_ref[1, part]).astype(F32)
         rows.append(sums_ref[3 + "AB".index(which), part] + echo + scale * state[part])
     block = jnp.concatenate(rows, axis=0).astype(BF)
-    got = product(block, leaf_ref[0], leaf_ref[1], sources)
+    got = product(block, leaf_real_ref[...], leaf_imag_ref[...], sources)
     for part in range(2):
         terms_ref[part] = got[part].astype(BF)
 
@@ -248,7 +248,7 @@
 
 
 def planes_kernel(
-    place_ref, by_a_ref, by_b_ref, first_ref, last_ref, own_ref, leaf_a_ref, leaf_b_ref,
+    place_ref, by_a_ref, by_b_ref, first_ref, last_ref, own_ref, a_real_ref, a_imag_ref, b_real_ref, b_imag_ref,
     enter_ref, leave_ref, zlow_ref, zhigh_ref,
 ):
     two, sources, rows, width = first_ref.shape
@@ -267,8 +267,9 @@
     below = [jnp.where(even, by_b_ref[part], by_a_ref[part]).astype(F32) for part in range(2)]
     below = [jnp.where(lower, part, 0.0) for part in below]
     above = [jnp.where(even, by_a_ref[part], by_b_ref[part]).astype(F32) for part in range(2)]
-    upper_leaf = [jnp.where(even, leaf_a_ref[part], leaf_b_ref[part]) for part in range(2)]
-    lower_leaf = [jnp.where(even, leaf_b_ref[part], leaf_a_ref[part]) for part in range(2)]
+    leaf_a, leaf_b = (a_real_ref[...], a_imag_ref[...]), (b_real_ref[...], b_imag_ref[...])
+    upper_leaf = [jnp.where(even, leaf_a[part], leaf_b[part]) for part in range(2)]
+    lower_leaf = [jnp.where(even, leaf_b[part], leaf_a[part]) for part in range(2)]
     own_leaf = [own_ref[0], own_ref[1]]
     enter = times(below, own_leaf)
     above_enter = times([last_ref[part].astype(F32) for part in range(2)], upper_leaf)
@@ -297,7 +298,7 @@
 
 def closing_kernel(
     target, place_ref, own_w_ref, a_w_ref, b_w_ref, near_ref, slab_ref, side_ref, opposite_ref, back_ref, before_ref,
-    root_ref, got_a_ref, got_b_ref, parcel_a_ref, parcel_b_ref, parcel_ref, own_ref, leaf_a_ref, leaf_b_ref,
+    root_ref, got_a_ref, got_b_ref, parcel_a_ref, parcel_b_ref, parcel_ref, own_ref, a_real_ref, a_imag_ref, b_real_ref, b_imag_ref,
     low_ref, high_ref, enter_ref, leave_ref, state_ref, vector_ref, near_rows_ref, far_rows_ref,
 ):
     here, _ = advanced(
@@ -313,7 +314,7 @@
     below_last, above_first = neighbour_tables(place_ref, a_w_ref, b_w_ref, planes - 1)
     own_last = entries(own_w_ref, 1, planes - 1)
     own_leaf = [own_ref[0], own_ref[1]]
-    lower_leaf = [jnp.where(even, leaf_b_ref[part], leaf_a_ref[part]) for part in range(2)]
+    lower_leaf = [jnp.where(even, b, a) for a, b in ((a_real_ref[...], b_real_ref[...]), (a_imag_ref[...], b_imag_ref[...]))]
     entered, above, below, behind = [], [], [], []
     for part in range(2):
         entered.append(jnp.where(lower, jnp.where(even, parcel_b_ref[0, part], parcel_a_ref[0, part]).astype(F32), 0.0))
@@ -420,7 +421,7 @@
         + [pl.BlockSpec(memory_space=pltpu.VMEM)] * len(others),
         out_specs=[whole, whole],
         out_shape=[jax.ShapeDtypeStruct(source.shape, F32)] * 2,
-        compiler_params=pltpu.CompilerParams(vmem_limit_bytes=40 * 2**20),
+        compiler_params=pltpu.CompilerParams(vmem_limit_bytes=46 * 2**20),
         cost_estimate=pl.CostEstimate(flops=60000000, bytes_accessed=26000000, transcendentals=0),
         name="finish",
     )(*scalars, leaf, source, *others)
@@ -443,21 +444,10 @@
     shape = jax.ShapeDtypeStruct
 
     weights = jnp.stack([restrict_weight, prolong_weight])
-    traded_leaf = {which: swapped(leaf_matrix, which) for which in "AB"}
-    traded_weights = {which: swapped(weights, which) for which in "AB"}
+    traded_leaf = {which: [swapped(leaf_matrix[part], which) for part in range(2)] for which in "AB"}
+    real_parts, imag_parts = zip(*traded_leaf.values())
     leaf, base_terms, first_plane, last_plane, low_rows, high_rows = leaf_solve(weights, source, leaf_matrix)
-    base_terms = after(base_terms, traded_weights["A"], traded_weights["B"])
-
-    def by_parity(even_value, odd_value):
-        return jnp.where(even_panel, even_value, odd_value)
-
-    by_a = swapped(by_parity(last_plane, first_plane), "A")
-    by_b = swapped(by_parity(first_plane, last_plane), "B")
-    plane = shape(first_plane.shape, F32)
-    planes_got = whole_call(
-        planes_kernel, [plane] * 4, 400000000, "planes", 1,
-        place, by_a, by_b, first_plane, last_plane, leaf_matrix, traded_leaf["A"], traded_leaf["B"], limit=32,
-    )
+
 
     def halves(block):
         return jnp.where(even_core, block[0], block[1])
@@ -472,13 +462,24 @@
         return terms.astype(F32) + other_core(terms).astype(F32)
 
     every = tuple(range(PANELS))
-    pair = pair_sum(base_terms.astype(BF))
+    pair = after(pair_sum(base_terms), *real_parts)
     side, opposite, back = inside(pair.astype(BF), every, 2, 4, 6)
     near_term = jnp.where(even_core, side, back[:2]).astype(F32)
     far_term = jnp.where(even_core, jnp.stack([opposite, back[2]]), jnp.stack([back[2], opposite])).astype(F32)
     quad = pair + near_term
     slab = pair + side.astype(F32) + back[:2].astype(F32) + far_term
-    slab = after(slab, traded_leaf["A"], traded_leaf["B"])
+    slab = after(slab, *imag_parts)
+    traded_weights = {which: swapped(after(weights, slab), which) for which in "AB"}
+    def by_parity(even_value, odd_value):
+        return jnp.where(even_panel, even_value, odd_value)
+
+    by_a = swapped(after(by_parity(last_plane, first_plane), slab), "A")
+    by_b = swapped(after(by_parity(first_plane, last_plane), slab), "B")
+    plane = shape(first_plane.shape, F32)
+    planes_got = whole_call(
+        planes_kernel, [plane] * 4, 400000000, "planes", 1,
+        place, by_a, by_b, first_plane, last_plane, leaf_matrix, *traded_leaf["A"], *traded_leaf["B"], limit=26,
+    )
     base_sums = (pair, quad, slab)
     nothing = jnp.zeros(vector, F32)
 
@@ -497,7 +498,7 @@
         return whole_call(
             functools.partial(forward_kernel, target, which),
             [shape(vector, F32), shape(vector, BF), shape((2,) + vector, BF)], 200000000, "forward", 3,
-            place, weights, traded_weights[which], *got, traded_leaf[which], sums, parcel,
+            place, weights, traded_weights[which], *got, *traded_leaf[which], sums, parcel,
         )
 
     def backward_close(level_sums, panels, target, keep, which, before, brought):
@@ -505,7 +506,7 @@
         return whole_call(
             functools.partial(backward_kernel, target, keep, which),
             [shape(vector, F32), shape(vector, BF)], 200000000, "backward", 3,
-            place, weights, traded_weights[which], *got, traded_leaf[which], sums, brought["A"], brought["B"],
+            place, weights, traded_weights[which], *got, *traded_leaf[which], sums, brought["A"], brought["B"],
         )
 
     def cross(terms, from_panel, to_panel):
@@ -520,6 +521,7 @@
         return own, quad, quad + two_.astype(F32) + back[1]
 
     state, terms, parcel = forward_close(base_sums, every, 0, "A", nothing, jnp.zeros((2,) + vector, BF))
+    terms = after(terms, by_a, by_b)
     brought = {}
     for turn, which in enumerate("ABA"):
         target = turn + 1
@@ -549,7 +551,7 @@
                 functools.partial(closing_kernel, target),
                 [shape(vector, F32), shape((two, 9, sources, width), F32), edge, edge], 300000000, "closing", 4,
                 *scalars, *got, got_a, got_b, brought["A"], brought["B"], parcel,
-                leaf_matrix, traded_leaf["A"], traded_leaf["B"], low_rows, high_rows, enter, leave, limit=32,
+                leaf_matrix, *traded_leaf["A"], *traded_leaf["B"], low_rows, high_rows, enter, leave, limit=26,
             )
     late = swapped(state, "A")
     near_front = other_core(near_rows)

time: 210 us -> 203 us (0.967)
  waiting for transfers between devices: 72.4 us -> 64.4 us
  starting transfers between devices: 79 us -> 86.1 us
  local copies, waits for them, and re-layouts: 14.9 us -> 8.35 us
  Pallas kernels: 37 us -> 39.9 us
  other arithmetic: 4.59 us -> 2.46 us
    unnamed x56 -> x16, local copies, waits for them, and re-layouts: 14.8 us -> 6.22 us
    ppermute x62 -> x64, waiting for transfers between devices: 72.4 us -> 64.4 us  [moved(): return lax.ppermute(block, AXES, route)]
    ppermute x62 -> x64, starting transfers between devices: 79 us -> 86.1 us  [moved(): return lax.ppermute(block, AXES, route)]
    pallas_call x1, Pallas kernels: 10.7 us -> 12.9 us  [finish(): pl.pallas_call(final_kernel, grid=(sources // step,), in_specs=[pl.BlockS...]
    squeeze x0 -> x1, local copies, waits for them, and re-layouts: none -> 2.11 us  [local(): leaf_matrix[part]]
  transfers between devices with their start and end apart: 62 -> 64, of which waited for: 43 -> 44; matrix products, arithmetic and copies ran while one was open for 1% -> 1% of each run, Pallas kernels for 8% -> 9%
where the time goes in v3:
time: 203 us; the launch traced here: 202 us
  starting transfers between devices  86.1 us (42%)
  waiting for transfers between devices  64.4 us (32%)
  Pallas kernels  39.9 us (20%)
  local copies, waits for them, and re-layouts  8.35 us (4%)
  other arithmetic  2.46 us (1%)
    ppermute x64, starting transfers between devices, moved(): return lax.ppermute(block, AXES, route)  86.1 us
    ppermute x64, waiting for transfers between devices, moved(): return lax.ppermute(block, AXES, route)  64.4 us
    pallas_call x16, Pallas kernels, whole_call(): pl.pallas_call(kernel, in_specs=[pl.BlockSpec(memory_space=space) for spa...  20.3 us
    pallas_call x1, Pallas kernels, finish(): pl.pallas_call(final_kernel, grid=(sources // step,), in_specs=[pl.BlockS...  12.9 us
    pallas_call x1, Pallas kernels, leaf_solve(): pl.pallas_call(leaf_kernel, grid=(sources // step,), in_specs=[pl.BlockSp...  6.7 us
    unnamed x16, local copies, waits for them, and re-layouts  6.22 us
  transfers between devices with their start and end apart: 64, of which 44 were waited for; matrix products, arithmetic and copies ran while one was open for 1% of the time, Pallas kernels for 9%

profile of v3, /device:TPU:0, one launch (start us, length us, event | category | flops | bytes accessed | tf_op | source)
XLA Modules:
  0.0 202.5 jit_solution(584618565918415033)
XLA Ops:
  0.6 2.1 %slice_bitcast_fusion = (bf16[512,512]{1,0:T(8,128)(2,1)}, bf16[512,512]{1,0:T(8,128)(2,1)S(1)}) fusion(bf16[2,1,1,512,512]{4,3,2,1,0:T(8,128)(2,1)} %param.8), kind=kLoop, calls=%fused_computation | loop fusion | bytes 2097152 | tf_op jit(solution)/shard_map/squeeze | solution.py:447
  2.7 4.1 %collective-permute-start.2 = (bf16[512,512]{1,0:T(8,128)(2,1)S(1)}, bf16[512,512]{1,0:T(8,128)(2,1)S(1)}, u32[]{:S(2)}, u32[]{:S(2)}) collective-permute-start(bf16[512,512]{1,0:T(8,128)(2,1)S(1)} %get-tuple-element.90), channel_id=1, source_target_pairs={{0,96},{1,97},{2,98},{3,99},{4,100},{5,101},{6,102},{7,103},{8,104... | collective-permute-start | bytes 1572872 | tf_op jit(solution)/shard_map/ppermute | solution.py:48
  7.6 2.8 %copy-done.2 = f32[2,24,8,8,512]{4,3,2,1,0:T(8,128)S(1)} copy-done((f32[2,24,8,8,512]{4,3,2,1,0:T(8,128)S(1)}, f32[2,24,8,8,512]{4,3,2,1,0:T(8,128)}, u32[]{:S(2)}) %copy-start.2) | copy-done | bytes 6291480
  10.4 1.2 copy-done.3
  11.6 6.7 %leaf_solve.1 = (f32[2,24,8,8,512]{4,3,2,1,0:T(8,128)}, bf16[2,24,512]{2,1,0:T(8,128)(2,1)S(1)}, bf16[2,24,8,512]{3,2,1,0:T(8,128)(2,1)S(1)}, bf16[2,24,8,512]{3...) custom-call(f32[2,8,8]{2,1,0:T(8,128)S(1)} %pad_maximum_fusion.14.weight_ref.own_ref.own_w_ref, ...), custom_call_target="tpu_custom_call" | custom-call | flops 65000000 | bytes 1600000 | tf_op jit(solution)/shard_map/leaf_solve/pallas_call | solution.py:113
  18.3 1.2 collective-permute-done
  20.3 1.7 collective-permute-start.3
  21.9 2.9 %collective-permute-start.4 = (bf16[24,512]{1,0:T(8,128)(2,1)S(1)}, bf16[24,512]{1,0:T(8,128)(2,1)S(1)}, u32[]{:S(2)}, u32[]{:S(2)}) collective-permute-start(bf16[24,512]{1,0:T(8,128)(2,1)S(1)} %fusion.22), channel_id=1, source_target_pairs={{0,4},{1,5},{2,6},{3,7},{4,0},{5,1},{6,2},{7,3},{8,12},{9,13},{10,... | collective-permute-start | bytes 73736 | tf_op jit(solution)/shard_map/ppermute | solution.py:48
  24.8 1.5 collective-permute-start.7
  26.3 1.1 collective-permute-done.4
  27.5 1.0 broadcast_select_fusion
  28.8 9.3 %collective-permute-done.7.leaf_imag_ref.b_imag_ref = bf16[512,512]{1,0:T(8,128)(2,1)S(1)} collective-permute-done((bf16[512,512]{1,0:T(8,128)(2,1)}, bf16[512,512]{1,0:T(8,128)(2,1)S(1)}, u32[]{:S(2)}, u32[]{:S(2)}) %collective-permute-start.7) | collective-permute-done | bytes 524320 | tf_op jit(solution)/shard_map/ppermute | solution.py:48
  38.2 1.6 collective-permute-start.10
  39.7 0.8 collective-permute-start.13
  40.6 2.3 %collective-permute-start.14 = (bf16[2,24,8,512]{3,2,1,0:T(8,128)(2,1)}, bf16[2,24,8,512]{3,2,1,0:T(8,128)(2,1)}, u32[]{:S(2)}, u32[]{:S(2)}) collective-permute-start(bf16[2,24,8,512]{3,2,1,0:T(8,128)(2,1)} %get-tuple-element.47), channel_id=1, source_target_pairs={{0,96},{1,97},{2,98},{3,99},{4,100},{5,101},{6,102},{7,103},{8,104... | collective-permute-start | bytes 1179656 | tf_op jit(solution)/shard_map/ppermute | solution.py:48
  42.9 2.7 %collective-permute-start.11 = (bf16[24,512]{1,0:T(8,128)(2,1)S(1)}, bf16[24,512]{1,0:T(8,128)(2,1)S(1)}, u32[]{:S(2)}, u32[]{:S(2)}) collective-permute-start(bf16[24,512]{1,0:T(8,128)(2,1)S(1)} %fusion.21), channel_id=1, source_target_pairs={{0,16},{1,17},{2,18},{3,19},{4,20},{5,21},{6,22},{7,23},{8,24},{9,... | collective-permute-start | bytes 73736 | tf_op jit(solution)/shard_map/ppermute | solution.py:48
  45.6 2.6 %collective-permute-done.11.opposite_ref = bf16[24,512]{1,0:T(8,128)(2,1)S(1)} collective-permute-done((bf16[24,512]{1,0:T(8,128)(2,1)S(1)}, bf16[24,512]{1,0:T(8,128)(2,1)S(1)}, u32[]{:S(2)}, u32[]{:S(2)}) %collective-permute-start.11) | collective-permute-done | bytes 24608 | tf_op jit(solution)/shard_map/ppermute | solution.py:48
  48.4 0.9 collective-permute-start.9
  49.3 2.2 %copy-done = bf16[2,1,1,4,512,512]{5,4,3,2,1,0:T(8,128)(2,1)S(1)} copy-done((bf16[2,1,1,4,512,512]{5,4,3,2,1,0:T(8,128)(2,1)S(1)}, bf16[2,1,1,4,512,512]{5,4,3,2,1,0:T(8,128)(2,1)}, u32[]{:S(2)}) %copy-start) | copy-done | bytes 4194328
  52.2 1.1 collective-permute-done.9.by_b_ref.traded_ref.b_w_ref
  53.3 2.1 %edge_sums.1.sums_ref = f32[5,2,24,512]{3,2,1,0:T(8,128)S(1)} custom-call(f32[2,8,8]{2,1,0:T(8,128)S(1)} %pad_maximum_fusion.14.weight_ref.own_ref.own_w_ref, f32[2,8,8]{2,1,0:T(8,128)S(1)} %collective-permute-done.8.by_a_ref.traded_ref.a_w_ref, f32[2,8,8]{2,1,0:T(8,128)S(1)} %collective-permute-done.9.by_b_ref.traded_ref.b_w_ref, ...), custom_call_target="tpu_custom_call" | custom-call | flops 10000000 | bytes 50000 | tf_op jit(solution)/shard_map/edge_sums/pallas_call | solution.py:139
  55.4 1.4 forward.3
  57.0 1.2 collective-permute-done.15
  58.2 3.3 %collective-permute-start.17 = (bf16[2,24,512]{2,1,0:T(8,128)(2,1)S(1)}, bf16[2,24,512]{2,1,0:T(8,128)(2,1)S(1)}, u32[]{:S(2)}, u32[]{:S(2)}) collective-permute-start(bf16[2,24,512]{2,1,0:T(8,128)(2,1)S(1)} %add_convert_fusion.5), channel_id=1, source_target_pairs={{0,36},{1,39},{2,38},{3,37},{4,32},{5,35},{6,34},{7,33},{8,44},{9,... | collective-permute-start | bytes 147464 | tf_op jit(solution)/shard_map/ppermute | solution.py:48
  61.6 1.7 collective-permute-start.16
  63.3 1.8 collective-permute-done.17
  65.9 1.3 collective-permute-done.18
  67.9 0.8 collective-permute-done.20.opposite_ref
  69.4 3.1 %planes.1 = (f32[2,24,8,512]{3,2,1,0:T(8,128)S(1)}, f32[2,24,8,512]{3,2,1,0:T(8,128)S(1)}, f32[2,24,8,512]{3,2,1,0:T(8,128)S(1)}, f32[2,24,8,512]{3,2,1,0:T(8,128)S(1)}) custom-call(s32[3]{0:T(128)S(1)} %pad_add_fusion.place_ref, bf16[2,24,8,512]{3,2,1,0:T(8,128)(2,1)} %collective-permute-done.13.by_a_ref, ...), custom_call_target="tpu_custom_call" | custom-call | flops 400000000 | bytes 2000000 | tf_op jit(solution)/shard_map/planes/pallas_call | solution.py:139
  73.1 1.4 forward.4
  74.8 1.1 collective-permute-done.22
  76.5 0.7 collective-permute-done.24
  77.8 1.0 collective-permute-done.25
  79.4 1.0 collective-permute-done.27.opposite_ref
  81.8 1.4 forward.5
  83.5 1.1 collective-permute-done.29
  85.2 0.7 collective-permute-done.31
  86.5 1.0 collective-permute-done.32
  88.1 24.6 %collective-permute-start.37 = (bf16[2,2,24,512]{3,2,1,0:T(8,128)(2,1)S(1)}, bf16[2,2,24,512]{3,2,1,0:T(8,128)(2,1)S(1)}, u32[]{:S(2)}, u32[]{:S(2)}) collective-permute-start(bf16[2,2,24,512]{3,2,1,0:T(8,128)(2,1)S(1)} %get-tuple-element.58.parcel_ref), channel_id=1, source_target_pairs={{0,96},{1,97},{2,98},{3,99},{4,100},{5,101},{6,102},{7,103},{8,104... | collective-permute-start | bytes 294920 | tf_op jit(solution)/shard_map/ppermute | solution.py:48
  113.5 1.8 collective-permute-done.37.by_b_ref.parcel_b_ref
  115.3 2.0 collective-permute-done.36.by_a_ref.parcel_a_ref
  117.3 1.4 backward.3
  118.8 1.2 collective-permute-done.38
  121.9 1.0 collective-permute-done.41
  123.5 1.0 collective-permute-done.43.opposite_ref
  125.9 1.4 backward.4
  127.5 1.1 collective-permute-done.45
  130.5 1.0 collective-permute-done.48
  132.4 1.0 collective-permute-done.50.opposite_ref
  134.8 1.4 backward.5
  136.4 1.1 collective-permute-done.52
  137.5 21.5 %collective-permute-start.54 = (bf16[2,24,512]{2,1,0:T(8,128)(2,1)S(1)}, bf16[2,24,512]{2,1,0:T(8,128)(2,1)S(1)}, u32[]{:S(2)}, u32[]{:S(2)}) collective-permute-start(bf16[2,24,512]{2,1,0:T(8,128)(2,1)S(1)} %add_convert_fusion), channel_id=1, source_target_pairs={{0,36},{1,39},{2,38},{3,37},{4,32},{5,35},{6,34},{7,33},{8,44},{9,... | collective-permute-start | bytes 147464 | tf_op jit(solution)/shard_map/ppermute | solution.py:48
  158.9 2.1 %collective-permute-done.54 = bf16[2,24,512]{2,1,0:T(8,128)(2,1)S(1)} collective-permute-done((bf16[2,24,512]{2,1,0:T(8,128)(2,1)S(1)}, bf16[2,24,512]{2,1,0:T(8,128)(2,1)S(1)}, u32[]{:S(2)}, u32[]{:S(2)}) %collective-permute-start.54) | collective-permute-done | bytes 49184 | tf_op jit(solution)/shard_map/ppermute | solution.py:48
  161.1 2.4 %collective-permute-done.53 = bf16[2,24,512]{2,1,0:T(8,128)(2,1)S(1)} collective-permute-done((bf16[2,24,512]{2,1,0:T(8,128)(2,1)S(1)}, bf16[2,24,512]{2,1,0:T(8,128)(2,1)S(1)}, u32[]{:S(2)}, u32[]{:S(2)}) %collective-permute-start.53) | collective-permute-done | bytes 49184 | tf_op jit(solution)/shard_map/ppermute | solution.py:48
  163.5 1.3 collective-permute-done.55
  164.9 0.8 collective-permute-start.56
  165.7 2.3 %collective-permute-start.57 = (bf16[24,512]{1,0:T(8,128)(2,1)S(1)}, bf16[24,512]{1,0:T(8,128)(2,1)S(1)}, u32[]{:S(2)}, u32[]{:S(2)}) collective-permute-start(bf16[24,512]{1,0:T(8,128)(2,1)S(1)} %fusion.15), channel_id=1, source_target_pairs={{0,16},{1,17},{2,18},{3,19},{4,20},{5,21},{6,22},{7,23},{8,24},{9,... | collective-permute-start | bytes 73736 | tf_op jit(solution)/shard_map/ppermute | solution.py:48
  168.0 3.0 %collective-permute-done.57.opposite_ref = bf16[24,512]{1,0:T(8,128)(2,1)S(1)} collective-permute-done((bf16[24,512]{1,0:T(8,128)(2,1)S(1)}, bf16[24,512]{1,0:T(8,128)(2,1)S(1)}, u32[]{:S(2)}, u32[]{:S(2)}) %collective-permute-start.57) | collective-permute-done | bytes 24608 | tf_op jit(solution)/shard_map/ppermute | solution.py:48
  172.0 4.6 %collective-permute-done.60.got_b_ref = bf16[2,24,512]{2,1,0:T(8,128)(2,1)S(1)} collective-permute-done((bf16[2,24,512]{2,1,0:T(8,128)(2,1)S(1)}, bf16[2,24,512]{2,1,0:T(8,128)(2,1)S(1)}, u32[]{:S(2)}, u32[]{:S(2)}) %collective-permute-start.60) | collective-permute-done | bytes 49184 | tf_op jit(solution)/shard_map/ppermute | solution.py:48
  176.6 2.2 %closing.1 = (f32[2,24,512]{2,1,0:T(8,128)S(1)}, f32[2,9,24,512]{3,2,1,0:T(8,128)S(1)}, bf16[2,24,8,512]{3,2,1,0:T(8,128)(2,1)S(1)}, bf16[2,24,8,512]{3,2,1,0:T(8,128)(2,1)S(1)}) custom-call(s32[3]{0:T(128)S(1)} %pad_add_fusion.place_ref, f32[2,8,8]{2,1,0:T(8,128)S(1)} %pad_maximum_fusion.14.weight_ref.own_ref.own_w_ref, ...), custom_call_target="tpu_custom_call" | custom-call | flops 300000000 | bytes 1500000 | tf_op jit(solution)/shard_map/closing/pallas_call | solution.py:139
  178.9 2.8 %collective-permute-start.63 = (bf16[2,24,8,512]{3,2,1,0:T(8,128)(2,1)S(1)}, bf16[2,24,8,512]{3,2,1,0:T(8,128)(2,1)S(1)}, u32[]{:S(2)}, u32[]{:S(2)}) collective-permute-start(bf16[2,24,8,512]{3,2,1,0:T(8,128)(2,1)S(1)} %get-tuple-element.73), channel_id=1, source_target_pairs={{0,31},{1,2},{2,1},{3,4},{4,3},{5,6},{6,5},{7,8},{8,7},{9,10},{10,... | collective-permute-start | bytes 1179656 | tf_op jit(solution)/shard_map/ppermute | solution.py:48
  181.7 4.6 %collective-permute-done.61.late_ref = f32[2,24,512]{2,1,0:T(8,128)S(1)} collective-permute-done((f32[2,24,512]{2,1,0:T(8,128)S(1)}, f32[2,24,512]{2,1,0:T(8,128)S(1)}, u32[]{:S(2)}, u32[]{:S(2)}) %collective-permute-start.61) | collective-permute-done | bytes 98336 | tf_op jit(solution)/shard_map/ppermute | solution.py:48
  186.4 3.1 %collective-permute-done.63.far_ref = bf16[2,24,8,512]{3,2,1,0:T(8,128)(2,1)S(1)} collective-permute-done((bf16[2,24,8,512]{3,2,1,0:T(8,128)(2,1)S(1)}, bf16[2,24,8,512]{3,2,1,0:T(8,128)(2,1)S(1)}, u32[]{:S(2)}, u32[]{:S(2)}) %collective-permute-start.63) | collective-permute-done | bytes 393248 | tf_op jit(solution)/shard_map/ppermute | solution.py:48
  189.5 12.9 %finish.1 = (f32[2,24,8,8,512]{4,3,2,1,0:T(8,128)}, f32[2,24,8,8,512]{4,3,2,1,0:T(8,128)}) custom-call(s32[3]{0:T(128)S(1)} %pad_add_fusion.place_ref, f32[2,8,8]{2,1,0:T(8,128)S(1)} %pad_maximum_fusion.14.weight_ref.own_ref.own_w_ref, f32[2,8,8]{2,1,0:T(8,128)S(1)} %collective-permute-done.8.by_a_ref.traded_ref.a_w_ref, ...), custom_call_target="tpu_custom_call" | custom-call | flops 60000000 | bytes 26000000 | tf_op jit(solution)/shard_map/finish/pallas_call | solution.py:416
  (150 shorter events, 21.7 us)
Async XLA Ops:
  2.7 16.8 %collective-permute-start.2 = (bf16[512,512]{1,0:T(8,128)(2,1)S(1)}, bf16[512,512]{1,0:T(8,128)(2,1)S(1)}, u32[]{:S(2)}, u32[]{:S(2)}) collective-permute-start(bf16[512,512]{1,0:T(8,128)(2,1)S(1)} %get-tuple-element.90), channel_id=1, source_target_pairs={{0,96},{1,97},{2,98},{3,99},{4,100},{5,101},{6,102},{7,103},{8,104... | collective-permute-start | bytes 1572872 | tf_op jit(solution)/shard_map/ppermute | solution.py:48
  6.9 13.4 %collective-permute-start.1 = (bf16[512,512]{1,0:T(8,128)(2,1)S(1)}, bf16[512,512]{1,0:T(8,128)(2,1)S(1)}, u32[]{:S(2)}, u32[]{:S(2)}) collective-permute-start(bf16[512,512]{1,0:T(8,128)(2,1)S(1)} %get-tuple-element.90), channel_id=1, source_target_pairs={{0,32},{1,33},{2,34},{3,35},{4,36},{5,37},{6,38},{7,39},{8,40},{9,... | collective-permute-start | bytes 1572872 | tf_op jit(solution)/shard_map/ppermute | solution.py:48
  18.3 1.2 collective-permute-start
  20.3 7.2 %collective-permute-start.3 = (bf16[2,24,512]{2,1,0:T(8,128)(2,1)S(1)}, bf16[2,24,512]{2,1,0:T(8,128)(2,1)S(1)}, u32[]{:S(2)}, u32[]{:S(2)}) collective-permute-start(bf16[2,24,512]{2,1,0:T(8,128)(2,1)S(1)} %convert_element_type.157), channel_id=1, source_target_pairs={{0,2},{1,7},{2,0},{3,5},{4,6},{5,3},{6,4},{7,1},{8,10},{9,15},{10,... | collective-permute-start | bytes 147464 | tf_op jit(solution)/shard_map/ppermute | solution.py:48
  21.9 5.5 %collective-permute-start.4 = (bf16[24,512]{1,0:T(8,128)(2,1)S(1)}, bf16[24,512]{1,0:T(8,128)(2,1)S(1)}, u32[]{:S(2)}, u32[]{:S(2)}) collective-permute-start(bf16[24,512]{1,0:T(8,128)(2,1)S(1)} %fusion.22), channel_id=1, source_target_pairs={{0,4},{1,5},{2,6},{3,7},{4,0},{5,1},{6,2},{7,3},{8,12},{9,13},{10,... | collective-permute-start | bytes 73736 | tf_op jit(solution)/shard_map/ppermute | solution.py:48
  24.8 13.3 %collective-permute-start.7 = (bf16[512,512]{1,0:T(8,128)(2,1)}, bf16[512,512]{1,0:T(8,128)(2,1)S(1)}, u32[]{:S(2)}, u32[]{:S(2)}) collective-permute-start(bf16[512,512]{1,0:T(8,128)(2,1)} %get-tuple-element.89), channel_id=1, source_target_pairs={{0,96},{1,97},{2,98},{3,99},{4,100},{5,101},{6,102},{7,103},{8,104... | collective-permute-start | bytes 1572872 | tf_op jit(solution)/shard_map/ppermute | solution.py:48
  26.3 11.8 %collective-permute-start.6 = (bf16[512,512]{1,0:T(8,128)(2,1)}, bf16[512,512]{1,0:T(8,128)(2,1)S(1)}, u32[]{:S(2)}, u32[]{:S(2)}) collective-permute-start(bf16[512,512]{1,0:T(8,128)(2,1)} %get-tuple-element.89), channel_id=1, source_target_pairs={{0,32},{1,33},{2,34},{3,35},{4,36},{5,37},{6,38},{7,39},{8,40},{9,... | collective-permute-start | bytes 1572872 | tf_op jit(solution)/shard_map/ppermute | solution.py:48
  27.4 1.3 collective-permute-start.5
  38.2 10.1 %collective-permute-start.10 = (bf16[2,24,512]{2,1,0:T(8,128)(2,1)S(1)}, bf16[2,24,512]{2,1,0:T(8,128)(2,1)S(1)}, u32[]{:S(2)}, u32[]{:S(2)}) collective-permute-start(bf16[2,24,512]{2,1,0:T(8,128)(2,1)S(1)} %convert_element_type.162), channel_id=1, source_target_pairs={{0,8},{1,25},{2,10},{3,27},{4,12},{5,29},{6,14},{7,31},{8,0},{9,17... | collective-permute-start | bytes 147464 | tf_op jit(solution)/shard_map/ppermute | solution.py:48
  39.7 17.1 %collective-permute-start.13 = (bf16[2,24,8,512]{3,2,1,0:T(8,128)(2,1)}, bf16[2,24,8,512]{3,2,1,0:T(8,128)(2,1)}, u32[]{:S(2)}, u32[]{:S(2)}) collective-permute-start(bf16[2,24,8,512]{3,2,1,0:T(8,128)(2,1)} %get-tuple-element.46), channel_id=1, source_target_pairs={{0,32},{1,33},{2,34},{3,35},{4,36},{5,37},{6,38},{7,39},{8,40},{9,... | collective-permute-start | bytes 1179656 | tf_op jit(solution)/shard_map/ppermute | solution.py:48
  40.6 16.3 %collective-permute-start.14 = (bf16[2,24,8,512]{3,2,1,0:T(8,128)(2,1)}, bf16[2,24,8,512]{3,2,1,0:T(8,128)(2,1)}, u32[]{:S(2)}, u32[]{:S(2)}) collective-permute-start(bf16[2,24,8,512]{3,2,1,0:T(8,128)(2,1)} %get-tuple-element.47), channel_id=1, source_target_pairs={{0,96},{1,97},{2,98},{3,99},{4,100},{5,101},{6,102},{7,103},{8,104... | collective-permute-start | bytes 1179656 | tf_op jit(solution)/shard_map/ppermute | solution.py:48
  42.9 5.3 %collective-permute-start.11 = (bf16[24,512]{1,0:T(8,128)(2,1)S(1)}, bf16[24,512]{1,0:T(8,128)(2,1)S(1)}, u32[]{:S(2)}, u32[]{:S(2)}) collective-permute-start(bf16[24,512]{1,0:T(8,128)(2,1)S(1)} %fusion.21), channel_id=1, source_target_pairs={{0,16},{1,17},{2,18},{3,19},{4,20},{5,21},{6,22},{7,23},{8,24},{9,... | collective-permute-start | bytes 73736 | tf_op jit(solution)/shard_map/ppermute | solution.py:48
  48.3 7.1 %collective-permute-start.12 = (bf16[3,24,512]{2,1,0:T(8,128)(2,1)S(1)}, bf16[3,24,512]{2,1,0:T(8,128)(2,1)S(1)}, u32[]{:S(2)}, u32[]{:S(2)}) collective-permute-start(bf16[3,24,512]{2,1,0:T(8,128)(2,1)S(1)} %pad_maximum_fusion.7), channel_id=1, source_target_pairs={{0,1},{1,0},{2,3},{3,2},{4,5},{5,4},{6,7},{7,6},{8,9},{9,8},{10,11... | collective-permute-start | bytes 221192 | tf_op jit(solution)/shard_map/ppermute | solution.py:48
  48.4 4.9 %collective-permute-start.9 = (f32[2,8,8]{2,1,0:T(8,128)S(1)}, f32[2,8,8]{2,1,0:T(8,128)S(1)}, u32[]{:S(2)}, u32[]{:S(2)}) collective-permute-start(f32[2,8,8]{2,1,0:T(8,128)S(1)} %pad_maximum_fusion.14.weight_ref.own_ref.own_w_ref), channel_id=1, source_target_pairs={{0,96},{1,97},{2,98},{3,99},{4,100},{5,101},{6,102},{7,103},{8,104... | collective-permute-start | bytes 1544 | tf_op jit(solution)/shard_map/ppermute | solution.py:48
  49.3 4.0 %collective-permute-start.8 = (f32[2,8,8]{2,1,0:T(8,128)S(1)}, f32[2,8,8]{2,1,0:T(8,128)S(1)}, u32[]{:S(2)}, u32[]{:S(2)}) collective-permute-start(f32[2,8,8]{2,1,0:T(8,128)S(1)} %pad_maximum_fusion.14.weight_ref.own_ref.own_w_ref), channel_id=1, source_target_pairs={{0,32},{1,33},{2,34},{3,35},{4,36},{5,37},{6,38},{7,39},{8,40},{9,... | collective-permute-start | bytes 1544 | tf_op jit(solution)/shard_map/ppermute | solution.py:48
  56.9 1.3 collective-permute-start.15
  58.2 6.9 %collective-permute-start.17 = (bf16[2,24,512]{2,1,0:T(8,128)(2,1)S(1)}, bf16[2,24,512]{2,1,0:T(8,128)(2,1)S(1)}, u32[]{:S(2)}, u32[]{:S(2)}) collective-permute-start(bf16[2,24,512]{2,1,0:T(8,128)(2,1)S(1)} %add_convert_fusion.5), channel_id=1, source_target_pairs={{0,36},{1,39},{2,38},{3,37},{4,32},{5,35},{6,34},{7,33},{8,44},{9,... | collective-permute-start | bytes 147464 | tf_op jit(solution)/shard_map/ppermute | solution.py:48
  61.6 4.3 %collective-permute-start.16 = (bf16[2,24,512]{2,1,0:T(8,128)(2,1)S(1)}, bf16[2,24,512]{2,1,0:T(8,128)(2,1)S(1)}, u32[]{:S(2)}, u32[]{:S(2)}) collective-permute-start(bf16[2,24,512]{2,1,0:T(8,128)(2,1)S(1)} %add_convert_fusion.5), channel_id=1, source_target_pairs={{0,32},{1,35},{2,34},{3,33},{4,36},{5,39},{6,38},{7,37},{8,40},{9,... | collective-permute-start | bytes 147464 | tf_op jit(solution)/shard_map/ppermute | solution.py:48
  65.8 1.4 collective-permute-start.18
  67.3 1.5 collective-permute-start.19
  67.5 1.2 collective-permute-start.20
  68.8 4.4 %collective-permute-start.21 = (bf16[3,24,512]{2,1,0:T(8,128)(2,1)S(1)}, bf16[3,24,512]{2,1,0:T(8,128)(2,1)S(1)}, u32[]{:S(2)}, u32[]{:S(2)}) collective-permute-start(bf16[3,24,512]{2,1,0:T(8,128)(2,1)S(1)} %pad_maximum_fusion.8), channel_id=1, source_target_pairs={{0,1},{1,0},{2,3},{3,2},{4,5},{5,4},{6,7},{7,6},{8,9},{9,8},{10,11... | collective-permute-start | bytes 221192 | tf_op jit(solution)/shard_map/ppermute | solution.py:48
  74.6 1.3 collective-permute-start.22
  75.9 1.3 collective-permute-start.24
  76.1 1.2 collective-permute-start.23
  77.4 1.4 collective-permute-start.25
  78.8 1.6 collective-permute-start.26
  79.3 1.2 collective-permute-start.27
  80.5 1.3 collective-permute-start.28
  83.2 1.3 collective-permute-start.29
  84.6 1.3 collective-permute-start.31
  84.8 1.2 collective-permute-start.30
  86.1 1.4 collective-permute-start.32
  87.5 25.2 %collective-permute-start.33 = (bf16[2,24,512]{2,1,0:T(8,128)(2,1)S(1)}, bf16[2,24,512]{2,1,0:T(8,128)(2,1)S(1)}, u32[]{:S(2)}, u32[]{:S(2)}) collective-permute-start(bf16[2,24,512]{2,1,0:T(8,128)(2,1)S(1)} %get-tuple-element.83), channel_id=1, source_target_pairs={{0,1},{1,0},{2,3},{3,2},{4,5},{5,4},{6,7},{7,6},{8,9},{9,8},{10,11... | collective-permute-start | bytes 147464 | tf_op jit(solution)/shard_map/ppermute | solution.py:48
  88.0 24.7 %collective-permute-start.34 = (bf16[24,512]{1,0:T(8,128)(2,1)S(1)}, bf16[24,512]{1,0:T(8,128)(2,1)S(1)}, u32[]{:S(2)}, u32[]{:S(2)}) collective-permute-start(bf16[24,512]{1,0:T(8,128)(2,1)S(1)} %fusion.18), channel_id=1, source_target_pairs={{0,1},{1,0},{2,3},{3,2},{4,5},{5,4},{6,7},{7,6},{8,9},{9,8},{10,11... | collective-permute-start | bytes 73736 | tf_op jit(solution)/shard_map/ppermute | solution.py:48
  88.1 27.1 %collective-permute-start.37 = (bf16[2,2,24,512]{3,2,1,0:T(8,128)(2,1)S(1)}, bf16[2,2,24,512]{3,2,1,0:T(8,128)(2,1)S(1)}, u32[]{:S(2)}, u32[]{:S(2)}) collective-permute-start(bf16[2,2,24,512]{3,2,1,0:T(8,128)(2,1)S(1)} %get-tuple-element.58.parcel_ref), channel_id=1, source_target_pairs={{0,96},{1,97},{2,98},{3,99},{4,100},{5,101},{6,102},{7,103},{8,104... | collective-permute-start | bytes 294920 | tf_op jit(solution)/shard_map/ppermute | solution.py:48
  112.7 4.6 %collective-permute-start.36 = (bf16[2,2,24,512]{3,2,1,0:T(8,128)(2,1)S(1)}, bf16[2,2,24,512]{3,2,1,0:T(8,128)(2,1)S(1)}, u32[]{:S(2)}, u32[]{:S(2)}) collective-permute-start(bf16[2,2,24,512]{3,2,1,0:T(8,128)(2,1)S(1)} %get-tuple-element.61.parcel_ref), channel_id=1, source_target_pairs={{0,32},{1,33},{2,34},{3,35},{4,36},{5,37},{6,38},{7,39},{8,40},{9,... | collective-permute-start | bytes 294920 | tf_op jit(solution)/shard_map/ppermute | solution.py:48
  112.7 4.6 %collective-permute-start.35 = (bf16[3,24,512]{2,1,0:T(8,128)(2,1)S(1)}, bf16[3,24,512]{2,1,0:T(8,128)(2,1)S(1)}, u32[]{:S(2)}, u32[]{:S(2)}) collective-permute-start(bf16[3,24,512]{2,1,0:T(8,128)(2,1)S(1)} %pad_maximum_fusion.10), channel_id=1, source_target_pairs={{0,1},{1,0},{2,3},{3,2},{4,5},{5,4},{6,7},{7,6},{8,9},{9,8},{10,11... | collective-permute-start | bytes 221192 | tf_op jit(solution)/shard_map/ppermute | solution.py:48
  118.7 1.3 collective-permute-start.38
  120.0 1.3 collective-permute-start.40
  120.2 1.2 collective-permute-start.39
  121.5 1.4 collective-permute-start.41
  122.9 1.6 collective-permute-start.42
  123.4 1.2 collective-permute-start.43
  124.6 1.3 collective-permute-start.44
  127.3 1.3 collective-permute-start.45
  128.6 1.3 collective-permute-start.47
  128.9 1.2 collective-permute-start.46
  130.1 1.4 collective-permute-start.48
  131.5 1.9 collective-permute-start.49
  132.2 1.2 collective-permute-start.50
  133.4 1.3 collective-permute-start.51
  136.1 1.3 collective-permute-start.52
  137.5 23.6 %collective-permute-start.54 = (bf16[2,24,512]{2,1,0:T(8,128)(2,1)S(1)}, bf16[2,24,512]{2,1,0:T(8,128)(2,1)S(1)}, u32[]{:S(2)}, u32[]{:S(2)}) collective-permute-start(bf16[2,24,512]{2,1,0:T(8,128)(2,1)S(1)} %add_convert_fusion), channel_id=1, source_target_pairs={{0,36},{1,39},{2,38},{3,37},{4,32},{5,35},{6,34},{7,33},{8,44},{9,... | collective-permute-start | bytes 147464 | tf_op jit(solution)/shard_map/ppermute | solution.py:48
  158.9 4.5 %collective-permute-start.53 = (bf16[2,24,512]{2,1,0:T(8,128)(2,1)S(1)}, bf16[2,24,512]{2,1,0:T(8,128)(2,1)S(1)}, u32[]{:S(2)}, u32[]{:S(2)}) collective-permute-start(bf16[2,24,512]{2,1,0:T(8,128)(2,1)S(1)} %add_convert_fusion), channel_id=1, source_target_pairs={{0,32},{1,35},{2,34},{3,33},{4,36},{5,39},{6,38},{7,37},{8,40},{9,... | collective-permute-start | bytes 147464 | tf_op jit(solution)/shard_map/ppermute | solution.py:48
  163.4 1.4 collective-permute-start.55
  164.9 6.2 %collective-permute-start.56 = (bf16[2,24,512]{2,1,0:T(8,128)(2,1)S(1)}, bf16[2,24,512]{2,1,0:T(8,128)(2,1)S(1)}, u32[]{:S(2)}, u32[]{:S(2)}) collective-permute-start(bf16[2,24,512]{2,1,0:T(8,128)(2,1)S(1)} %get-tuple-element.74), channel_id=1, source_target_pairs={{0,8},{1,25},{2,10},{3,27},{4,12},{5,29},{6,14},{7,31},{8,0},{9,17... | collective-permute-start | bytes 147464 | tf_op jit(solution)/shard_map/ppermute | solution.py:48
  165.7 5.3 %collective-permute-start.57 = (bf16[24,512]{1,0:T(8,128)(2,1)S(1)}, bf16[24,512]{1,0:T(8,128)(2,1)S(1)}, u32[]{:S(2)}, u32[]{:S(2)}) collective-permute-start(bf16[24,512]{1,0:T(8,128)(2,1)S(1)} %fusion.15), channel_id=1, source_target_pairs={{0,16},{1,17},{2,18},{3,19},{4,20},{5,21},{6,22},{7,23},{8,24},{9,... | collective-permute-start | bytes 73736 | tf_op jit(solution)/shard_map/ppermute | solution.py:48
  171.0 5.5 %collective-permute-start.58 = (bf16[3,24,512]{2,1,0:T(8,128)(2,1)S(1)}, bf16[3,24,512]{2,1,0:T(8,128)(2,1)S(1)}, u32[]{:S(2)}, u32[]{:S(2)}) collective-permute-start(bf16[3,24,512]{2,1,0:T(8,128)(2,1)S(1)} %pad_maximum_fusion.13), channel_id=1, source_target_pairs={{0,1},{1,0},{2,3},{3,2},{4,5},{5,4},{6,7},{7,6},{8,9},{9,8},{10,11... | collective-permute-start | bytes 221192 | tf_op jit(solution)/shard_map/ppermute | solution.py:48
  171.2 5.4 %collective-permute-start.60 = (bf16[2,24,512]{2,1,0:T(8,128)(2,1)S(1)}, bf16[2,24,512]{2,1,0:T(8,128)(2,1)S(1)}, u32[]{:S(2)}, u32[]{:S(2)}) collective-permute-start(bf16[2,24,512]{2,1,0:T(8,128)(2,1)S(1)} %convert_element_type.205), channel_id=1, source_target_pairs={{0,96},{1,97},{2,98},{3,99},{4,100},{5,101},{6,102},{7,103},{8,104... | collective-permute-start | bytes 147464 | tf_op jit(solution)/shard_map/ppermute | solution.py:48
  171.2 5.3 %collective-permute-start.59 = (bf16[2,24,512]{2,1,0:T(8,128)(2,1)S(1)}, bf16[2,24,512]{2,1,0:T(8,128)(2,1)S(1)}, u32[]{:S(2)}, u32[]{:S(2)}) collective-permute-start(bf16[2,24,512]{2,1,0:T(8,128)(2,1)S(1)} %convert_element_type.205), channel_id=1, source_target_pairs={{0,32},{1,33},{2,34},{3,35},{4,36},{5,37},{6,38},{7,39},{8,40},{9,... | collective-permute-start | bytes 147464 | tf_op jit(solution)/shard_map/ppermute | solution.py:48
  178.8 7.5 %collective-permute-start.62 = (bf16[2,24,8,512]{3,2,1,0:T(8,128)(2,1)S(1)}, bf16[2,24,8,512]{3,2,1,0:T(8,128)(2,1)S(1)}, u32[]{:S(2)}, u32[]{:S(2)}) collective-permute-start(bf16[2,24,8,512]{3,2,1,0:T(8,128)(2,1)S(1)} %get-tuple-element.72), channel_id=1, source_target_pairs={{0,1},{1,0},{2,3},{3,2},{4,5},{5,4},{6,7},{7,6},{8,9},{9,8},{10,11... | collective-permute-start | bytes 1179656 | tf_op jit(solution)/shard_map/ppermute | solution.py:48
  178.9 10.6 %collective-permute-start.63 = (bf16[2,24,8,512]{3,2,1,0:T(8,128)(2,1)S(1)}, bf16[2,24,8,512]{3,2,1,0:T(8,128)(2,1)S(1)}, u32[]{:S(2)}, u32[]{:S(2)}) collective-permute-start(bf16[2,24,8,512]{3,2,1,0:T(8,128)(2,1)S(1)} %get-tuple-element.73), channel_id=1, source_target_pairs={{0,31},{1,2},{2,1},{3,4},{4,3},{5,6},{6,5},{7,8},{8,7},{9,10},{10,... | collective-permute-start | bytes 1179656 | tf_op jit(solution)/shard_map/ppermute | solution.py:48
  181.7 4.6 %collective-permute-start.61 = (f32[2,24,512]{2,1,0:T(8,128)S(1)}, f32[2,24,512]{2,1,0:T(8,128)S(1)}, u32[]{:S(2)}, u32[]{:S(2)}) collective-permute-start(f32[2,24,512]{2,1,0:T(8,128)S(1)} %get-tuple-element.71), channel_id=1, source_target_pairs={{0,32},{1,33},{2,34},{3,35},{4,36},{5,37},{6,38},{7,39},{8,40},{9,... | collective-permute-start | bytes 294920 | tf_op jit(solution)/shard_map/ppermute | solution.py:48
  (8 other events, 129.1 us)

commit v4 on v3

--- a/solution.py
+++ b/solution.py
@@ -127,7 +127,7 @@
             pltpu.HBM((two, sources, planes, width), F32),
             pltpu.HBM((two, sources, planes, width), F32),
         ],
-        compiler_params=pltpu.CompilerParams(vmem_limit_bytes=46 * 2**20),
+        compiler_params=pltpu.CompilerParams(vmem_limit_bytes=40 * 2**20),
         cost_estimate=pl.CostEstimate(flops=65000000, bytes_accessed=1600000, transcendentals=0),
         name="leaf_solve",
     )(weights, source, matrix)
@@ -421,7 +421,7 @@
         + [pl.BlockSpec(memory_space=pltpu.VMEM)] * len(others),
         out_specs=[whole, whole],
         out_shape=[jax.ShapeDtypeStruct(source.shape, F32)] * 2,
-        compiler_params=pltpu.CompilerParams(vmem_limit_bytes=46 * 2**20),
+        compiler_params=pltpu.CompilerParams(vmem_limit_bytes=40 * 2**20),
         cost_estimate=pl.CostEstimate(flops=60000000, bytes_accessed=26000000, transcendentals=0),
         name="finish",
     )(*scalars, leaf, source, *others)
@@ -444,7 +444,11 @@
     shape = jax.ShapeDtypeStruct
 
     weights = jnp.stack([restrict_weight, prolong_weight])
-    traded_leaf = {which: [swapped(leaf_matrix[part], which) for part in range(2)] for which in "AB"}
+    traded_weights = {which: swapped(weights, which) for which in "AB"}
+    tables = tuple(traded_weights.values())
+    traded_leaf = {
+        which: [swapped(after(leaf_matrix[part], *tables), which) for part in range(2)] for which in "AB"
+    }
     real_parts, imag_parts = zip(*traded_leaf.values())
     leaf, base_terms, first_plane, last_plane, low_rows, high_rows = leaf_solve(weights, source, leaf_matrix)
 
@@ -468,8 +472,6 @@
     far_term = jnp.where(even_core, jnp.stack([opposite, back[2]]), jnp.stack([back[2], opposite])).astype(F32)
     quad = pair + near_term
     slab = pair + side.astype(F32) + back[:2].astype(F32) + far_term
-    slab = after(slab, *imag_parts)
-    traded_weights = {which: swapped(after(weights, slab), which) for which in "AB"}
     def by_parity(even_value, odd_value):
         return jnp.where(even_panel, even_value, odd_value)
 
@@ -521,7 +523,7 @@
         return own, quad, quad + two_.astype(F32) + back[1]
 
     state, terms, parcel = forward_close(base_sums, every, 0, "A", nothing, jnp.zeros((2,) + vector, BF))
-    terms = after(terms, by_a, by_b)
+    terms = after(terms, imag_parts[1])
     brought = {}
     for turn, which in enumerate("ABA"):
         target = turn + 1
@@ -533,8 +535,8 @@
             state, terms, parcel = forward_close(total, (target,), target, "BA"[turn], state, parcel)
         else:
             state, terms = backward_close(total, (target,), target, False, "A", state, brought)
-        if turn == 0:
-            terms = after(terms, *planes_got)
+        if turn < 2:
+            terms = after(terms, *((by_a, by_b), planes_got)[turn])
     scalars = (place, weights, traded_weights["A"], traded_weights["B"])
     enter, leave, zlow, zhigh = planes_got
     edge = shape(low_rows.shape, BF)
@@ -546,7 +548,7 @@
             state, terms = backward_close(sums_now, (target,), target, True, "BA"[turn], state, brought)
         else:
             got_a, got_b = (swapped(state.astype(BF), which) for which in "AB")
-            got = gather(sums_now, (target,), state)
+            got = gather((*sums_now[:2], after(sums_now[2], got_a, got_b)), (target,), state)
             state, vectors, near_rows, far_rows = whole_call(
                 functools.partial(closing_kernel, target),
                 [shape(vector, F32), shape((two, 9, sources, width), F32), edge, edge], 300000000, "closing", 4,

time: 203 us -> 202 us (level)
  local copies, waits for them, and re-layouts: 8.35 us -> 17.7 us
  waiting for transfers between devices: 64.4 us -> 58 us
  starting transfers between devices: 86.1 us -> 82.6 us
  Pallas kernels: 39.9 us -> 37.1 us
  other arithmetic: 2.46 us -> 4.66 us
    unnamed x16 -> x48, local copies, waits for them, and re-layouts: 6.22 us -> 15.6 us
    ppermute x64, waiting for transfers between devices: 64.4 us -> 58 us  [moved(): return lax.ppermute(block, AXES, route)]
    ppermute x64, starting transfers between devices: 86.1 us -> 82.6 us  [moved(): return lax.ppermute(block, AXES, route)]
    pallas_call x1, Pallas kernels: 12.9 us -> 10.8 us  [finish(): pl.pallas_call(final_kernel, grid=(sources // step,), in_specs=[pl.BlockS...]
  transfers between devices with their start and end apart: 64 -> 64, of which waited for: 44 -> 42; matrix products, arithmetic and copies ran while one was open for 1% -> 2% of each run, Pallas kernels for 9% -> 9%
where the time goes in v4:
time: 202 us; the launch traced here: 201 us
  starting transfers between devices  82.6 us (41%)
  waiting for transfers between devices  58 us (29%)
  Pallas kernels  37.1 us (18%)
  local copies, waits for them, and re-layouts  17.7 us (9%)
  other arithmetic  4.66 us (2%)
    ppermute x64, starting transfers between devices, moved(): return lax.ppermute(block, AXES, route)  82.6 us
    ppermute x64, waiting for transfers between devices, moved(): return lax.ppermute(block, AXES, route)  58 us
    pallas_call x16, Pallas kernels, whole_call(): pl.pallas_call(kernel, in_specs=[pl.BlockSpec(memory_space=space) for spa...  19.6 us
    unnamed x48, local copies, waits for them, and re-layouts  15.6 us
    pallas_call x1, Pallas kernels, finish(): pl.pallas_call(final_kernel, grid=(sources // step,), in_specs=[pl.BlockS...  10.8 us
    pallas_call x1, Pallas kernels, leaf_solve(): pl.pallas_call(leaf_kernel, grid=(sources // step,), in_specs=[pl.BlockSp...  6.69 us
  transfers between devices with their start and end apart: 64, of which 42 were waited for; matrix products, arithmetic and copies ran while one was open for 2% of the time, Pallas kernels for 9%

profile of v4, /device:TPU:0, one launch (start us, length us, event | category | flops | bytes accessed | tf_op | source)
XLA Modules:
  0.0 201.2 jit_solution(12347496033369780205)
XLA Ops:
  1.3 4.1 %collective-permute-start.1 = (f32[2,8,8]{2,1,0:T(8,128)S(1)}, f32[2,8,8]{2,1,0:T(8,128)S(1)}, u32[]{:S(2)}, u32[]{:S(2)}) collective-permute-start(f32[2,8,8]{2,1,0:T(8,128)S(1)} %pad_maximum_fusion.14.weight_ref.own_ref.own_w_ref), channel_id=1, source_target_pairs={{0,96},{1,97},{2,98},{3,99},{4,100},{5,101},{6,102},{7,103},{8,104... | collective-permute-start | bytes 1544 | tf_op jit(solution)/shard_map/ppermute | solution.py:48
  5.5 2.1 %slice_bitcast_fusion = (bf16[512,512]{1,0:T(8,128)(2,1)}, bf16[512,512]{1,0:T(8,128)(2,1)S(1)}) fusion(bf16[2,1,1,512,512]{4,3,2,1,0:T(8,128)(2,1)} %param.8), kind=kLoop, calls=%fused_computation | loop fusion | bytes 2097152 | tf_op jit(solution)/shard_map/squeeze | solution.py:450
  7.5 1.6 collective-permute-done.by_a_ref.traded_ref.a_w_ref
  9.1 1.2 collective-permute-start.4
  10.3 2.8 %copy-done.4 = f32[2,24,8,8,512]{4,3,2,1,0:T(8,128)S(1)} copy-done((f32[2,24,8,8,512]{4,3,2,1,0:T(8,128)S(1)}, f32[2,24,8,8,512]{4,3,2,1,0:T(8,128)}, u32[]{:S(2)}) %copy-start.4) | copy-done | bytes 6291480
  13.1 1.2 copy-done.5
  14.3 6.7 %leaf_solve.1 = (f32[2,24,8,8,512]{4,3,2,1,0:T(8,128)}, bf16[2,24,512]{2,1,0:T(8,128)(2,1)S(1)}, bf16[2,24,8,512]{3,2,1,0:T(8,128)(2,1)S(1)}, bf16[2,24,8,512]{3...) custom-call(f32[2,8,8]{2,1,0:T(8,128)S(1)} %pad_maximum_fusion.14.weight_ref.own_ref.own_w_ref, ...), custom_call_target="tpu_custom_call" | custom-call | flops 65000000 | bytes 1600000 | tf_op jit(solution)/shard_map/leaf_solve/pallas_call | solution.py:113
  21.0 1.2 collective-permute-done.2
  22.6 1.7 collective-permute-start.5
  24.2 2.9 %collective-permute-start.6 = (bf16[24,512]{1,0:T(8,128)(2,1)S(1)}, bf16[24,512]{1,0:T(8,128)(2,1)S(1)}, u32[]{:S(2)}, u32[]{:S(2)}) collective-permute-start(bf16[24,512]{1,0:T(8,128)(2,1)S(1)} %fusion.22), channel_id=1, source_target_pairs={{0,4},{1,5},{2,6},{3,7},{4,0},{5,1},{6,2},{7,3},{8,12},{9,13},{10,... | collective-permute-start | bytes 73736 | tf_op jit(solution)/shard_map/ppermute | solution.py:48
  27.1 2.6 %collective-permute-done.6 = bf16[24,512]{1,0:T(8,128)(2,1)S(1)} collective-permute-done((bf16[24,512]{1,0:T(8,128)(2,1)S(1)}, bf16[24,512]{1,0:T(8,128)(2,1)S(1)}, u32[]{:S(2)}, u32[]{:S(2)}) %collective-permute-start.6) | collective-permute-done | bytes 24608 | tf_op jit(solution)/shard_map/ppermute | solution.py:48
  29.9 1.7 collective-permute-start.12
  31.6 1.4 collective-permute-start.11
  33.8 1.5 collective-permute-start.8
  35.3 2.7 %collective-permute-start.9 = (bf16[24,512]{1,0:T(8,128)(2,1)S(1)}, bf16[24,512]{1,0:T(8,128)(2,1)S(1)}, u32[]{:S(2)}, u32[]{:S(2)}) collective-permute-start(bf16[24,512]{1,0:T(8,128)(2,1)S(1)} %fusion.21), channel_id=1, source_target_pairs={{0,16},{1,17},{2,18},{3,19},{4,20},{5,21},{6,22},{7,23},{8,24},{9,... | collective-permute-start | bytes 73736 | tf_op jit(solution)/shard_map/ppermute | solution.py:48
  38.0 2.7 %collective-permute-done.9.opposite_ref = bf16[24,512]{1,0:T(8,128)(2,1)S(1)} collective-permute-done((bf16[24,512]{1,0:T(8,128)(2,1)S(1)}, bf16[24,512]{1,0:T(8,128)(2,1)S(1)}, u32[]{:S(2)}, u32[]{:S(2)}) %collective-permute-start.9) | collective-permute-done | bytes 24608 | tf_op jit(solution)/shard_map/ppermute | solution.py:48
  41.2 2.1 %edge_sums.1.sums_ref = f32[5,2,24,512]{3,2,1,0:T(8,128)S(1)} custom-call(f32[2,8,8]{2,1,0:T(8,128)S(1)} %pad_maximum_fusion.14.weight_ref.own_ref.own_w_ref, f32[2,8,8]{2,1,0:T(8,128)S(1)} %collective-permute-done.by_a_ref.traded_ref.a_w_ref, f32[2,8,8]{2,1,0:T(8,128)S(1)} %collective-permute-done.1.by_b_ref.traded_ref.b_w_ref, ...), custom_call_target="tpu_custom_call" | custom-call | flops 10000000 | bytes 50000 | tf_op jit(solution)/shard_map/edge_sums/pallas_call | solution.py:139
  43.3 2.2 %copy-done = bf16[2,1,1,4,512,512]{5,4,3,2,1,0:T(8,128)(2,1)S(1)} copy-done((bf16[2,1,1,4,512,512]{5,4,3,2,1,0:T(8,128)(2,1)S(1)}, bf16[2,1,1,4,512,512]{5,4,3,2,1,0:T(8,128)(2,1)}, u32[]{:S(2)}) %copy-start) | copy-done | bytes 4194328
  45.5 0.9 copy-done.7
  46.4 0.9 copy-done.10
  48.0 1.5 copy-done.1
  50.2 1.4 forward.3
  53.0 1.1 collective-permute-done.13
  54.8 3.0 %collective-permute-start.15 = (bf16[2,24,512]{2,1,0:T(8,128)(2,1)}, bf16[2,24,512]{2,1,0:T(8,128)(2,1)S(1)}, u32[]{:S(2)}, u32[]{:S(2)}) collective-permute-start(bf16[2,24,512]{2,1,0:T(8,128)(2,1)} %add_convert_fusion.5), channel_id=1, source_target_pairs={{0,36},{1,39},{2,38},{3,37},{4,32},{5,35},{6,34},{7,33},{8,44},{9,... | collective-permute-start | bytes 147464 | tf_op jit(solution)/shard_map/ppermute | solution.py:48
  57.7 1.4 collective-permute-start.14
  59.1 2.7 %collective-permute-done.15 = bf16[2,24,512]{2,1,0:T(8,128)(2,1)S(1)} collective-permute-done((bf16[2,24,512]{2,1,0:T(8,128)(2,1)}, bf16[2,24,512]{2,1,0:T(8,128)(2,1)S(1)}, u32[]{:S(2)}, u32[]{:S(2)}) %collective-permute-start.15) | collective-permute-done | bytes 49184 | tf_op jit(solution)/shard_map/ppermute | solution.py:48
  63.4 1.2 collective-permute-start.20
  64.7 1.1 fusion.31
  67.7 2.2 %copy-done.2 = bf16[2,1,1,4,512,512]{5,4,3,2,1,0:T(8,128)(2,1)S(1)} copy-done((bf16[2,1,1,4,512,512]{5,4,3,2,1,0:T(8,128)(2,1)S(1)}, bf16[2,1,1,4,512,512]{5,4,3,2,1,0:T(8,128)(2,1)}, u32[]{:S(2)}) %copy-start.2) | copy-done | bytes 4194328
  70.5 1.5 copy-done.3
  72.0 1.4 forward.4
  73.4 1.6 collective-permute-done.20.by_a_ref
  75.0 2.0 %collective-permute-done.21.by_b_ref = bf16[2,24,8,512]{3,2,1,0:T(8,128)(2,1)S(1)} collective-permute-done((bf16[2,24,8,512]{3,2,1,0:T(8,128)(2,1)S(1)}, bf16[2,24,8,512]{3,2,1,0:T(8,128)(2,1)S(1)}, u32[]{:S(2)}, u32[]{:S(2)}) %collective-permute-start.21) | collective-permute-done | bytes 393248 | tf_op jit(solution)/shard_map/ppermute | solution.py:48
  77.0 1.2 collective-permute-done.22
  80.4 1.0 collective-permute-done.25
  82.0 1.0 collective-permute-done.27.opposite_ref
  83.3 2.5 %planes.1 = (f32[2,24,8,512]{3,2,1,0:T(8,128)S(1)}, f32[2,24,8,512]{3,2,1,0:T(8,128)S(1)}, f32[2,24,8,512]{3,2,1,0:T(8,128)S(1)}, f32[2,24,8,512]{3,2,1,0:T(8,128)S(1)}) custom-call(s32[3]{0:T(128)S(1)} %pad_add_fusion.place_ref, bf16[2,24,8,512]{3,2,1,0:T(8,128)(2,1)S(1)} %collective-permute-done.20.by_a_ref, ...), custom_call_target="tpu_custom_call" | custom-call | flops 400000000 | bytes 2000000 | tf_op jit(solution)/shard_map/planes/pallas_call | solution.py:139
  86.5 1.4 forward.5
  91.2 1.1 collective-permute-done.32
  93.0 20.9 %collective-permute-start.37 = (bf16[2,2,24,512]{3,2,1,0:T(8,128)(2,1)S(1)}, bf16[2,2,24,512]{3,2,1,0:T(8,128)(2,1)S(1)}, u32[]{:S(2)}, u32[]{:S(2)}) collective-permute-start(bf16[2,2,24,512]{3,2,1,0:T(8,128)(2,1)S(1)} %get-tuple-element.56.parcel_ref), channel_id=1, source_target_pairs={{0,96},{1,97},{2,98},{3,99},{4,100},{5,101},{6,102},{7,103},{8,104... | collective-permute-start | bytes 294920 | tf_op jit(solution)/shard_map/ppermute | solution.py:48
  114.6 1.8 collective-permute-done.37.by_b_ref.parcel_b_ref
  116.4 2.0 %collective-permute-done.36.by_a_ref.parcel_a_ref = bf16[2,2,24,512]{3,2,1,0:T(8,128)(2,1)S(1)} collective-permute-done((bf16[2,2,24,512]{3,2,1,0:T(8,128)(2,1)S(1)}, bf16[2,2,24,512]{3,2,1,0:T(8,128)(2,1)S(1)}, u32[]{:S(2)}, u32[]{:S(2)}) %collective-permute-start.36) | collective-permute-done | bytes 98336 | tf_op jit(solution)/shard_map/ppermute | solution.py:48
  118.5 1.4 backward.3
  119.9 1.2 collective-permute-done.38
  123.1 1.0 collective-permute-done.41
  124.7 1.0 collective-permute-done.43.opposite_ref
  127.1 1.4 backward.4
  128.7 1.1 collective-permute-done.45
  131.7 1.0 collective-permute-done.48
  133.3 1.0 collective-permute-done.50.opposite_ref
  135.7 1.4 backward.5
  137.3 1.1 collective-permute-done.52
  138.4 21.5 %collective-permute-start.54 = (bf16[2,24,512]{2,1,0:T(8,128)(2,1)S(1)}, bf16[2,24,512]{2,1,0:T(8,128)(2,1)S(1)}, u32[]{:S(2)}, u32[]{:S(2)}) collective-permute-start(bf16[2,24,512]{2,1,0:T(8,128)(2,1)S(1)} %add_convert_fusion), channel_id=1, source_target_pairs={{0,36},{1,39},{2,38},{3,37},{4,32},{5,35},{6,34},{7,33},{8,44},{9,... | collective-permute-start | bytes 147464 | tf_op jit(solution)/shard_map/ppermute | solution.py:48
  160.0 2.1 %collective-permute-done.54 = bf16[2,24,512]{2,1,0:T(8,128)(2,1)S(1)} collective-permute-done((bf16[2,24,512]{2,1,0:T(8,128)(2,1)S(1)}, bf16[2,24,512]{2,1,0:T(8,128)(2,1)S(1)}, u32[]{:S(2)}, u32[]{:S(2)}) %collective-permute-start.54) | collective-permute-done | bytes 49184 | tf_op jit(solution)/shard_map/ppermute | solution.py:48
  162.1 2.4 %collective-permute-done.53 = bf16[2,24,512]{2,1,0:T(8,128)(2,1)S(1)} collective-permute-done((bf16[2,24,512]{2,1,0:T(8,128)(2,1)S(1)}, bf16[2,24,512]{2,1,0:T(8,128)(2,1)S(1)}, u32[]{:S(2)}, u32[]{:S(2)}) %collective-permute-start.53) | collective-permute-done | bytes 49184 | tf_op jit(solution)/shard_map/ppermute | solution.py:48
  164.6 1.3 collective-permute-start.56
  166.0 4.0 %collective-permute-done.57.got_b_ref = bf16[2,24,512]{2,1,0:T(8,128)(2,1)S(1)} collective-permute-done((bf16[2,24,512]{2,1,0:T(8,128)(2,1)S(1)}, bf16[2,24,512]{2,1,0:T(8,128)(2,1)S(1)}, u32[]{:S(2)}, u32[]{:S(2)}) %collective-permute-start.57) | collective-permute-done | bytes 49184 | tf_op jit(solution)/shard_map/ppermute | solution.py:48
  170.8 2.3 %collective-permute-start.59 = (bf16[24,512]{1,0:T(8,128)(2,1)S(1)}, bf16[24,512]{1,0:T(8,128)(2,1)S(1)}, u32[]{:S(2)}, u32[]{:S(2)}) collective-permute-start(bf16[24,512]{1,0:T(8,128)(2,1)S(1)} %fusion.15), channel_id=1, source_target_pairs={{0,16},{1,17},{2,18},{3,19},{4,20},{5,21},{6,22},{7,23},{8,24},{9,... | collective-permute-start | bytes 73736 | tf_op jit(solution)/shard_map/ppermute | solution.py:48
  173.1 3.0 %collective-permute-done.59.opposite_ref = bf16[24,512]{1,0:T(8,128)(2,1)S(1)} collective-permute-done((bf16[24,512]{1,0:T(8,128)(2,1)S(1)}, bf16[24,512]{1,0:T(8,128)(2,1)S(1)}, u32[]{:S(2)}, u32[]{:S(2)}) %collective-permute-start.59) | collective-permute-done | bytes 24608 | tf_op jit(solution)/shard_map/ppermute | solution.py:48
  177.5 2.2 %closing.1 = (f32[2,24,512]{2,1,0:T(8,128)S(1)}, f32[2,9,24,512]{3,2,1,0:T(8,128)S(1)}, bf16[2,24,8,512]{3,2,1,0:T(8,128)(2,1)S(1)}, bf16[2,24,8,512]{3,2,1,0:T(8,128)(2,1)S(1)}) custom-call(s32[3]{0:T(128)S(1)} %pad_add_fusion.place_ref, f32[2,8,8]{2,1,0:T(8,128)S(1)} %pad_maximum_fusion.14.weight_ref.own_ref.own_w_ref, ...), custom_call_target="tpu_custom_call" | custom-call | flops 300000000 | bytes 1500000 | tf_op jit(solution)/shard_map/closing/pallas_call | solution.py:139
  179.9 2.9 %collective-permute-start.63 = (bf16[2,24,8,512]{3,2,1,0:T(8,128)(2,1)S(1)}, bf16[2,24,8,512]{3,2,1,0:T(8,128)(2,1)S(1)}, u32[]{:S(2)}, u32[]{:S(2)}) collective-permute-start(bf16[2,24,8,512]{3,2,1,0:T(8,128)(2,1)S(1)} %get-tuple-element.77), channel_id=1, source_target_pairs={{0,31},{1,2},{2,1},{3,4},{4,3},{5,6},{6,5},{7,8},{8,7},{9,10},{10,... | collective-permute-start | bytes 1179656 | tf_op jit(solution)/shard_map/ppermute | solution.py:48
  182.8 4.6 %collective-permute-done.61.late_ref = f32[2,24,512]{2,1,0:T(8,128)S(1)} collective-permute-done((f32[2,24,512]{2,1,0:T(8,128)S(1)}, f32[2,24,512]{2,1,0:T(8,128)S(1)}, u32[]{:S(2)}, u32[]{:S(2)}) %collective-permute-start.61) | collective-permute-done | bytes 98336 | tf_op jit(solution)/shard_map/ppermute | solution.py:48
  187.4 3.0 %collective-permute-done.63.far_ref = bf16[2,24,8,512]{3,2,1,0:T(8,128)(2,1)S(1)} collective-permute-done((bf16[2,24,8,512]{3,2,1,0:T(8,128)(2,1)S(1)}, bf16[2,24,8,512]{3,2,1,0:T(8,128)(2,1)S(1)}, u32[]{:S(2)}, u32[]{:S(2)}) %collective-permute-start.63) | collective-permute-done | bytes 393248 | tf_op jit(solution)/shard_map/ppermute | solution.py:48
  190.5 10.8 %finish.1 = (f32[2,24,8,8,512]{4,3,2,1,0:T(8,128)}, f32[2,24,8,8,512]{4,3,2,1,0:T(8,128)}) custom-call(s32[3]{0:T(128)S(1)} %pad_add_fusion.place_ref, f32[2,8,8]{2,1,0:T(8,128)S(1)} %pad_maximum_fusion.14.weight_ref.own_ref.own_w_ref, f32[2,8,8]{2,1,0:T(8,128)S(1)} %collective-permute-done.by_a_ref.traded_ref.a_w_ref, ...), custom_call_target="tpu_custom_call" | custom-call | flops 60000000 | bytes 26000000 | tf_op jit(solution)/shard_map/finish/pallas_call | solution.py:416
  (183 shorter events, 29.5 us)
Async XLA Ops:
  1.3 6.2 %collective-permute-start.1 = (f32[2,8,8]{2,1,0:T(8,128)S(1)}, f32[2,8,8]{2,1,0:T(8,128)S(1)}, u32[]{:S(2)}, u32[]{:S(2)}) collective-permute-start(f32[2,8,8]{2,1,0:T(8,128)S(1)} %pad_maximum_fusion.14.weight_ref.own_ref.own_w_ref), channel_id=1, source_target_pairs={{0,96},{1,97},{2,98},{3,99},{4,100},{5,101},{6,102},{7,103},{8,104... | collective-permute-start | bytes 1544 | tf_op jit(solution)/shard_map/ppermute | solution.py:48
  5.5 3.7 %collective-permute-start = (f32[2,8,8]{2,1,0:T(8,128)S(1)}, f32[2,8,8]{2,1,0:T(8,128)S(1)}, u32[]{:S(2)}, u32[]{:S(2)}) collective-permute-start(f32[2,8,8]{2,1,0:T(8,128)S(1)} %pad_maximum_fusion.14.weight_ref.own_ref.own_w_ref), channel_id=1, source_target_pairs={{0,32},{1,33},{2,34},{3,35},{4,36},{5,37},{6,38},{7,39},{8,40},{9,... | collective-permute-start | bytes 1544 | tf_op jit(solution)/shard_map/ppermute | solution.py:48
  9.1 13.4 %collective-permute-start.4 = (bf16[512,512]{1,0:T(8,128)(2,1)S(1)}, bf16[512,512]{1,0:T(8,128)(2,1)S(1)}, u32[]{:S(2)}, u32[]{:S(2)}) collective-permute-start(bf16[512,512]{1,0:T(8,128)(2,1)S(1)} %get-tuple-element.42), channel_id=1, source_target_pairs={{0,96},{1,97},{2,98},{3,99},{4,100},{5,101},{6,102},{7,103},{8,104... | collective-permute-start | bytes 1572872 | tf_op jit(solution)/shard_map/ppermute | solution.py:48
  10.3 12.2 %collective-permute-start.3 = (bf16[512,512]{1,0:T(8,128)(2,1)S(1)}, bf16[512,512]{1,0:T(8,128)(2,1)S(1)}, u32[]{:S(2)}, u32[]{:S(2)}) collective-permute-start(bf16[512,512]{1,0:T(8,128)(2,1)S(1)} %get-tuple-element.42), channel_id=1, source_target_pairs={{0,32},{1,33},{2,34},{3,35},{4,36},{5,37},{6,38},{7,39},{8,40},{9,... | collective-permute-start | bytes 1572872 | tf_op jit(solution)/shard_map/ppermute | solution.py:48
  21.0 1.2 collective-permute-start.2
  22.6 7.2 %collective-permute-start.5 = (bf16[2,24,512]{2,1,0:T(8,128)(2,1)S(1)}, bf16[2,24,512]{2,1,0:T(8,128)(2,1)S(1)}, u32[]{:S(2)}, u32[]{:S(2)}) collective-permute-start(bf16[2,24,512]{2,1,0:T(8,128)(2,1)S(1)} %convert_element_type.157), channel_id=1, source_target_pairs={{0,2},{1,7},{2,0},{3,5},{4,6},{5,3},{6,4},{7,1},{8,10},{9,15},{10,... | collective-permute-start | bytes 147464 | tf_op jit(solution)/shard_map/ppermute | solution.py:48
  24.2 5.5 %collective-permute-start.6 = (bf16[24,512]{1,0:T(8,128)(2,1)S(1)}, bf16[24,512]{1,0:T(8,128)(2,1)S(1)}, u32[]{:S(2)}, u32[]{:S(2)}) collective-permute-start(bf16[24,512]{1,0:T(8,128)(2,1)S(1)} %fusion.22), channel_id=1, source_target_pairs={{0,4},{1,5},{2,6},{3,7},{4,0},{5,1},{6,2},{7,3},{8,12},{9,13},{10,... | collective-permute-start | bytes 73736 | tf_op jit(solution)/shard_map/ppermute | solution.py:48
  29.7 3.3 %collective-permute-start.7 = (bf16[3,24,512]{2,1,0:T(8,128)(2,1)S(1)}, bf16[3,24,512]{2,1,0:T(8,128)(2,1)S(1)}, u32[]{:S(2)}, u32[]{:S(2)}) collective-permute-start(bf16[3,24,512]{2,1,0:T(8,128)(2,1)S(1)} %pad_maximum_fusion.6), channel_id=1, source_target_pairs={{0,1},{1,0},{2,3},{3,2},{4,5},{5,4},{6,7},{7,6},{8,9},{9,8},{10,11... | collective-permute-start | bytes 221192 | tf_op jit(solution)/shard_map/ppermute | solution.py:48
  29.9 22.9 %collective-permute-start.12 = (bf16[512,512]{1,0:T(8,128)(2,1)}, bf16[512,512]{1,0:T(8,128)(2,1)S(1)}, u32[]{:S(2)}, u32[]{:S(2)}) collective-permute-start(bf16[512,512]{1,0:T(8,128)(2,1)} %get-tuple-element.44), channel_id=1, source_target_pairs={{0,96},{1,97},{2,98},{3,99},{4,100},{5,101},{6,102},{7,103},{8,104... | collective-permute-start | bytes 1572872 | tf_op jit(solution)/shard_map/ppermute | solution.py:48
  31.6 16.4 %collective-permute-start.11 = (bf16[512,512]{1,0:T(8,128)(2,1)}, bf16[512,512]{1,0:T(8,128)(2,1)S(1)}, u32[]{:S(2)}, u32[]{:S(2)}) collective-permute-start(bf16[512,512]{1,0:T(8,128)(2,1)} %get-tuple-element.44), channel_id=1, source_target_pairs={{0,32},{1,33},{2,34},{3,35},{4,36},{5,37},{6,38},{7,39},{8,40},{9,... | collective-permute-start | bytes 1572872 | tf_op jit(solution)/shard_map/ppermute | solution.py:48
  33.8 6.9 %collective-permute-start.8 = (bf16[2,24,512]{2,1,0:T(8,128)(2,1)S(1)}, bf16[2,24,512]{2,1,0:T(8,128)(2,1)S(1)}, u32[]{:S(2)}, u32[]{:S(2)}) collective-permute-start(bf16[2,24,512]{2,1,0:T(8,128)(2,1)S(1)} %get-tuple-element.92), channel_id=1, source_target_pairs={{0,8},{1,25},{2,10},{3,27},{4,12},{5,29},{6,14},{7,31},{8,0},{9,17... | collective-permute-start | bytes 147464 | tf_op jit(solution)/shard_map/ppermute | solution.py:48
  35.3 5.4 %collective-permute-start.9 = (bf16[24,512]{1,0:T(8,128)(2,1)S(1)}, bf16[24,512]{1,0:T(8,128)(2,1)S(1)}, u32[]{:S(2)}, u32[]{:S(2)}) collective-permute-start(bf16[24,512]{1,0:T(8,128)(2,1)S(1)} %fusion.21), channel_id=1, source_target_pairs={{0,16},{1,17},{2,18},{3,19},{4,20},{5,21},{6,22},{7,23},{8,24},{9,... | collective-permute-start | bytes 73736 | tf_op jit(solution)/shard_map/ppermute | solution.py:48
  40.7 7.3 %collective-permute-start.10 = (bf16[3,24,512]{2,1,0:T(8,128)(2,1)S(1)}, bf16[3,24,512]{2,1,0:T(8,128)(2,1)S(1)}, u32[]{:S(2)}, u32[]{:S(2)}) collective-permute-start(bf16[3,24,512]{2,1,0:T(8,128)(2,1)S(1)} %pad_maximum_fusion.7), channel_id=1, source_target_pairs={{0,1},{1,0},{2,3},{3,2},{4,5},{5,4},{6,7},{7,6},{8,9},{9,8},{10,11... | collective-permute-start | bytes 221192 | tf_op jit(solution)/shard_map/ppermute | solution.py:48
  52.9 1.2 collective-permute-start.13
  54.8 7.1 %collective-permute-start.15 = (bf16[2,24,512]{2,1,0:T(8,128)(2,1)}, bf16[2,24,512]{2,1,0:T(8,128)(2,1)S(1)}, u32[]{:S(2)}, u32[]{:S(2)}) collective-permute-start(bf16[2,24,512]{2,1,0:T(8,128)(2,1)} %add_convert_fusion.5), channel_id=1, source_target_pairs={{0,36},{1,39},{2,38},{3,37},{4,32},{5,35},{6,34},{7,33},{8,44},{9,... | collective-permute-start | bytes 147464 | tf_op jit(solution)/shard_map/ppermute | solution.py:48
  57.7 4.7 %collective-permute-start.14 = (bf16[2,24,512]{2,1,0:T(8,128)(2,1)}, bf16[2,24,512]{2,1,0:T(8,128)(2,1)}, u32[]{:S(2)}, u32[]{:S(2)}) collective-permute-start(bf16[2,24,512]{2,1,0:T(8,128)(2,1)} %add_convert_fusion.5), channel_id=1, source_target_pairs={{0,32},{1,35},{2,34},{3,33},{4,36},{5,39},{6,38},{7,37},{8,40},{9,... | collective-permute-start | bytes 147464 | tf_op jit(solution)/shard_map/ppermute | solution.py:48
  63.3 1.4 collective-permute-start.16
  63.4 11.6 %collective-permute-start.20 = (bf16[2,24,8,512]{3,2,1,0:T(8,128)(2,1)S(1)}, bf16[2,24,8,512]{3,2,1,0:T(8,128)(2,1)S(1)}, u32[]{:S(2)}, u32[]{:S(2)}) collective-permute-start(bf16[2,24,8,512]{3,2,1,0:T(8,128)(2,1)S(1)} %get-tuple-element.52), channel_id=1, source_target_pairs={{0,32},{1,33},{2,34},{3,35},{4,36},{5,37},{6,38},{7,39},{8,40},{9,... | collective-permute-start | bytes 1179656 | tf_op jit(solution)/shard_map/ppermute | solution.py:48
  64.6 12.4 %collective-permute-start.21 = (bf16[2,24,8,512]{3,2,1,0:T(8,128)(2,1)S(1)}, bf16[2,24,8,512]{3,2,1,0:T(8,128)(2,1)S(1)}, u32[]{:S(2)}, u32[]{:S(2)}) collective-permute-start(bf16[2,24,8,512]{3,2,1,0:T(8,128)(2,1)S(1)} %get-tuple-element.53), channel_id=1, source_target_pairs={{0,96},{1,97},{2,98},{3,99},{4,100},{5,101},{6,102},{7,103},{8,104... | collective-permute-start | bytes 1179656 | tf_op jit(solution)/shard_map/ppermute | solution.py:48
  65.8 1.5 collective-permute-start.17
  66.0 1.2 collective-permute-start.18
  67.2 3.3 %collective-permute-start.19 = (bf16[3,24,512]{2,1,0:T(8,128)(2,1)S(1)}, bf16[3,24,512]{2,1,0:T(8,128)(2,1)S(1)}, u32[]{:S(2)}, u32[]{:S(2)}) collective-permute-start(bf16[3,24,512]{2,1,0:T(8,128)(2,1)S(1)} %pad_maximum_fusion.8), channel_id=1, source_target_pairs={{0,1},{1,0},{2,3},{3,2},{4,5},{5,4},{6,7},{7,6},{8,9},{9,8},{10,11... | collective-permute-start | bytes 221192 | tf_op jit(solution)/shard_map/ppermute | solution.py:48
  77.0 1.2 collective-permute-start.22
  78.3 1.3 collective-permute-start.24
  78.5 1.2 collective-permute-start.23
  79.8 1.6 collective-permute-start.25
  81.4 1.6 collective-permute-start.26
  81.9 1.2 collective-permute-start.27
  83.1 3.4 %collective-permute-start.28 = (bf16[3,24,512]{2,1,0:T(8,128)(2,1)S(1)}, bf16[3,24,512]{2,1,0:T(8,128)(2,1)S(1)}, u32[]{:S(2)}, u32[]{:S(2)}) collective-permute-start(bf16[3,24,512]{2,1,0:T(8,128)(2,1)S(1)} %pad_maximum_fusion.9), channel_id=1, source_target_pairs={{0,1},{1,0},{2,3},{3,2},{4,5},{5,4},{6,7},{7,6},{8,9},{9,8},{10,11... | collective-permute-start | bytes 221192 | tf_op jit(solution)/shard_map/ppermute | solution.py:48
  87.9 1.3 collective-permute-start.29
  89.2 1.3 collective-permute-start.31
  89.7 1.2 collective-permute-start.30
  90.9 1.4 collective-permute-start.32
  92.4 21.5 %collective-permute-start.33 = (bf16[2,24,512]{2,1,0:T(8,128)(2,1)S(1)}, bf16[2,24,512]{2,1,0:T(8,128)(2,1)S(1)}, u32[]{:S(2)}, u32[]{:S(2)}) collective-permute-start(bf16[2,24,512]{2,1,0:T(8,128)(2,1)S(1)} %get-tuple-element.86), channel_id=1, source_target_pairs={{0,1},{1,0},{2,3},{3,2},{4,5},{5,4},{6,7},{7,6},{8,9},{9,8},{10,11... | collective-permute-start | bytes 147464 | tf_op jit(solution)/shard_map/ppermute | solution.py:48
  92.6 21.2 %collective-permute-start.34 = (bf16[24,512]{1,0:T(8,128)(2,1)S(1)}, bf16[24,512]{1,0:T(8,128)(2,1)S(1)}, u32[]{:S(2)}, u32[]{:S(2)}) collective-permute-start(bf16[24,512]{1,0:T(8,128)(2,1)S(1)} %fusion.18), channel_id=1, source_target_pairs={{0,1},{1,0},{2,3},{3,2},{4,5},{5,4},{6,7},{7,6},{8,9},{9,8},{10,11... | collective-permute-start | bytes 73736 | tf_op jit(solution)/shard_map/ppermute | solution.py:48
  93.0 23.5 %collective-permute-start.37 = (bf16[2,2,24,512]{3,2,1,0:T(8,128)(2,1)S(1)}, bf16[2,2,24,512]{3,2,1,0:T(8,128)(2,1)S(1)}, u32[]{:S(2)}, u32[]{:S(2)}) collective-permute-start(bf16[2,2,24,512]{3,2,1,0:T(8,128)(2,1)S(1)} %get-tuple-element.56.parcel_ref), channel_id=1, source_target_pairs={{0,96},{1,97},{2,98},{3,99},{4,100},{5,101},{6,102},{7,103},{8,104... | collective-permute-start | bytes 294920 | tf_op jit(solution)/shard_map/ppermute | solution.py:48
  113.8 4.6 %collective-permute-start.36 = (bf16[2,2,24,512]{3,2,1,0:T(8,128)(2,1)S(1)}, bf16[2,2,24,512]{3,2,1,0:T(8,128)(2,1)S(1)}, u32[]{:S(2)}, u32[]{:S(2)}) collective-permute-start(bf16[2,2,24,512]{3,2,1,0:T(8,128)(2,1)S(1)} %get-tuple-element.64.parcel_ref), channel_id=1, source_target_pairs={{0,32},{1,33},{2,34},{3,35},{4,36},{5,37},{6,38},{7,39},{8,40},{9,... | collective-permute-start | bytes 294920 | tf_op jit(solution)/shard_map/ppermute | solution.py:48
  113.9 4.6 %collective-permute-start.35 = (bf16[3,24,512]{2,1,0:T(8,128)(2,1)S(1)}, bf16[3,24,512]{2,1,0:T(8,128)(2,1)S(1)}, u32[]{:S(2)}, u32[]{:S(2)}) collective-permute-start(bf16[3,24,512]{2,1,0:T(8,128)(2,1)S(1)} %pad_maximum_fusion.10), channel_id=1, source_target_pairs={{0,1},{1,0},{2,3},{3,2},{4,5},{5,4},{6,7},{7,6},{8,9},{9,8},{10,11... | collective-permute-start | bytes 221192 | tf_op jit(solution)/shard_map/ppermute | solution.py:48
  119.8 1.3 collective-permute-start.38
  121.2 1.3 collective-permute-start.40
  121.4 1.2 collective-permute-start.39
  122.7 1.4 collective-permute-start.41
  124.1 1.6 collective-permute-start.42
  124.5 1.2 collective-permute-start.43
  125.7 1.3 collective-permute-start.44
  128.5 1.3 collective-permute-start.45
  129.8 1.3 collective-permute-start.47
  130.0 1.2 collective-permute-start.46
  131.3 1.4 collective-permute-start.48
  132.7 1.6 collective-permute-start.49
  133.1 1.2 collective-permute-start.50
  134.4 1.3 collective-permute-start.51
  137.1 1.3 collective-permute-start.52
  138.4 23.7 %collective-permute-start.54 = (bf16[2,24,512]{2,1,0:T(8,128)(2,1)S(1)}, bf16[2,24,512]{2,1,0:T(8,128)(2,1)S(1)}, u32[]{:S(2)}, u32[]{:S(2)}) collective-permute-start(bf16[2,24,512]{2,1,0:T(8,128)(2,1)S(1)} %add_convert_fusion), channel_id=1, source_target_pairs={{0,36},{1,39},{2,38},{3,37},{4,32},{5,35},{6,34},{7,33},{8,44},{9,... | collective-permute-start | bytes 147464 | tf_op jit(solution)/shard_map/ppermute | solution.py:48
  160.0 4.5 %collective-permute-start.53 = (bf16[2,24,512]{2,1,0:T(8,128)(2,1)S(1)}, bf16[2,24,512]{2,1,0:T(8,128)(2,1)S(1)}, u32[]{:S(2)}, u32[]{:S(2)}) collective-permute-start(bf16[2,24,512]{2,1,0:T(8,128)(2,1)S(1)} %add_convert_fusion), channel_id=1, source_target_pairs={{0,32},{1,35},{2,34},{3,33},{4,36},{5,39},{6,38},{7,37},{8,40},{9,... | collective-permute-start | bytes 147464 | tf_op jit(solution)/shard_map/ppermute | solution.py:48
  164.4 1.5 collective-permute-start.55
  164.6 5.4 %collective-permute-start.57 = (bf16[2,24,512]{2,1,0:T(8,128)(2,1)S(1)}, bf16[2,24,512]{2,1,0:T(8,128)(2,1)S(1)}, u32[]{:S(2)}, u32[]{:S(2)}) collective-permute-start(bf16[2,24,512]{2,1,0:T(8,128)(2,1)S(1)} %convert_element_type.204), channel_id=1, source_target_pairs={{0,96},{1,97},{2,98},{3,99},{4,100},{5,101},{6,102},{7,103},{8,104... | collective-permute-start | bytes 147464 | tf_op jit(solution)/shard_map/ppermute | solution.py:48
  164.6 5.3 %collective-permute-start.56 = (bf16[2,24,512]{2,1,0:T(8,128)(2,1)S(1)}, bf16[2,24,512]{2,1,0:T(8,128)(2,1)S(1)}, u32[]{:S(2)}, u32[]{:S(2)}) collective-permute-start(bf16[2,24,512]{2,1,0:T(8,128)(2,1)S(1)} %convert_element_type.204), channel_id=1, source_target_pairs={{0,32},{1,33},{2,34},{3,35},{4,36},{5,37},{6,38},{7,39},{8,40},{9,... | collective-permute-start | bytes 147464 | tf_op jit(solution)/shard_map/ppermute | solution.py:48
  170.0 6.1 %collective-permute-start.58 = (bf16[2,24,512]{2,1,0:T(8,128)(2,1)S(1)}, bf16[2,24,512]{2,1,0:T(8,128)(2,1)S(1)}, u32[]{:S(2)}, u32[]{:S(2)}) collective-permute-start(bf16[2,24,512]{2,1,0:T(8,128)(2,1)S(1)} %convert_element_type.205), channel_id=1, source_target_pairs={{0,8},{1,25},{2,10},{3,27},{4,12},{5,29},{6,14},{7,31},{8,0},{9,17... | collective-permute-start | bytes 147464 | tf_op jit(solution)/shard_map/ppermute | solution.py:48
  170.8 5.3 %collective-permute-start.59 = (bf16[24,512]{1,0:T(8,128)(2,1)S(1)}, bf16[24,512]{1,0:T(8,128)(2,1)S(1)}, u32[]{:S(2)}, u32[]{:S(2)}) collective-permute-start(bf16[24,512]{1,0:T(8,128)(2,1)S(1)} %fusion.15), channel_id=1, source_target_pairs={{0,16},{1,17},{2,18},{3,19},{4,20},{5,21},{6,22},{7,23},{8,24},{9,... | collective-permute-start | bytes 73736 | tf_op jit(solution)/shard_map/ppermute | solution.py:48
  176.1 1.3 collective-permute-start.60
  179.7 7.7 %collective-permute-start.62 = (bf16[2,24,8,512]{3,2,1,0:T(8,128)(2,1)S(1)}, bf16[2,24,8,512]{3,2,1,0:T(8,128)(2,1)S(1)}, u32[]{:S(2)}, u32[]{:S(2)}) collective-permute-start(bf16[2,24,8,512]{3,2,1,0:T(8,128)(2,1)S(1)} %get-tuple-element.76), channel_id=1, source_target_pairs={{0,1},{1,0},{2,3},{3,2},{4,5},{5,4},{6,7},{7,6},{8,9},{9,8},{10,11... | collective-permute-start | bytes 1179656 | tf_op jit(solution)/shard_map/ppermute | solution.py:48
  179.9 10.5 %collective-permute-start.63 = (bf16[2,24,8,512]{3,2,1,0:T(8,128)(2,1)S(1)}, bf16[2,24,8,512]{3,2,1,0:T(8,128)(2,1)S(1)}, u32[]{:S(2)}, u32[]{:S(2)}) collective-permute-start(bf16[2,24,8,512]{3,2,1,0:T(8,128)(2,1)S(1)} %get-tuple-element.77), channel_id=1, source_target_pairs={{0,31},{1,2},{2,1},{3,4},{4,3},{5,6},{6,5},{7,8},{8,7},{9,10},{10,... | collective-permute-start | bytes 1179656 | tf_op jit(solution)/shard_map/ppermute | solution.py:48
  182.8 4.6 %collective-permute-start.61 = (f32[2,24,512]{2,1,0:T(8,128)S(1)}, f32[2,24,512]{2,1,0:T(8,128)S(1)}, u32[]{:S(2)}, u32[]{:S(2)}) collective-permute-start(f32[2,24,512]{2,1,0:T(8,128)S(1)} %get-tuple-element.75), channel_id=1, source_target_pairs={{0,32},{1,33},{2,34},{3,35},{4,36},{5,37},{6,38},{7,39},{8,40},{9,... | collective-permute-start | bytes 294920 | tf_op jit(solution)/shard_map/ppermute | solution.py:48
  (24 other events, 223.2 us)

commit v5 on v4

--- a/solution.py
+++ b/solution.py
@@ -147,7 +147,43 @@
     )(*args)
 
 
-def near_kernel(own_ref, quad_ref, slab_ref, matrix_ref, out_ref):
+def near_kernel(own_ref, quad_ref, slab_ref, matrix_ref, out_ref, root_ref, held_ref, arrived):
+    sources, width = own_ref.shape[1:]
+    levels = (own_ref, quad_ref, slab_ref)
+    copies = [
+        pltpu.make_async_copy(matrix_ref.at[:, level], held_ref.at[level], arrived.at[level])
+        for level in range(len(levels))
+    ]
+    copies.append(pltpu.make_async_copy(matrix_ref.at[:, len(levels)], root_ref, arrived.at[len(levels)]))
+    for copy in copies:
+        copy.start()
+    total = None
+    for level, ref in enumerate(levels):
+        block = ref[...].reshape(2 * sources, width).astype(BF)
+        copies[level].wait()
+        got = product(block, held_ref[level, 0], held_ref[level, 1], sources)
+        total = got if total is None else (total[0] + got[0], total[1] + got[1])
+    out_ref[0] = total[0]
+    out_ref[1] = total[1]
+    copies[-1].wait()
+
+
+def near_part(own, quad, slab, separators):
+    matrix = (separators.shape[0],) + separators.shape[2:]
+    vmem = pl.BlockSpec(memory_space=pltpu.VMEM)
+    return pl.pallas_call(
+        near_kernel,
+        in_specs=[vmem, vmem, vmem, pl.BlockSpec(memory_space=pl.ANY)],
+        out_specs=[vmem, vmem],
+        out_shape=[jax.ShapeDtypeStruct(own.shape, F32), jax.ShapeDtypeStruct(matrix, BF)],
+        scratch_shapes=[pltpu.VMEM((3,) + matrix, BF), pltpu.SemaphoreType.DMA((4,))],
+        compiler_params=pltpu.CompilerParams(vmem_limit_bytes=14 * 2**20),
+        cost_estimate=pl.CostEstimate(flops=150000000, bytes_accessed=750000, transcendentals=0),
+        name="near_part",
+    )(own, quad, slab, separators)
+
+
+def held_kernel(own_ref, quad_ref, slab_ref, matrix_ref, out_ref):
     sources, width = own_ref.shape[1:]
     total = None
     for level, ref in enumerate((own_ref, quad_ref, slab_ref)):
@@ -158,9 +194,9 @@
     out_ref[1] = total[1]
 
 
-def near_part(own, quad, slab, separators):
+def held_part(own, quad, slab, separators):
     return whole_call(
-        near_kernel, [jax.ShapeDtypeStruct(own.shape, F32)], 150000000, "near_part", 0, own, quad, slab, separators
+        held_kernel, [jax.ShapeDtypeStruct(own.shape, F32)], 150000000, "near_part", 0, own, quad, slab, separators
     )[0]
 
 
@@ -175,7 +211,7 @@
         far = jnp.where(even, mine, other) if part == 0 else jnp.where(even, other, mine)
         root.append(slab_ref[part] + side_ref[part].astype(F32) + back_ref[part].astype(F32) + far)
     block = jnp.concatenate(root, axis=0).astype(BF)
-    got = product(block, root_ref[0, 3], root_ref[1, 3], sources)
+    got = product(block, root_ref[0], root_ref[1], sources)
     state = []
     for part in range(2):
         old = before_ref[part]
@@ -432,6 +468,7 @@
 
 
 def local(source, wave_term, leaf_inverse, separator_inverse, restrict_weight, prolong_weight):
+    source = pltpu.with_memory_space_constraint(source, pltpu.HBM)
     two, sources, planes, rows, width = source.shape
     panel = lax.axis_index("panel")
     front = lax.axis_index("front")
@@ -439,6 +476,8 @@
     even_panel = panel % 2 == 0
     leaf_matrix = leaf_inverse[:, 0, 0]
     separators = separator_inverse[:, 0, 0]
+    root_matrix = separators[:, 3]
+    fetched = pltpu.with_memory_space_constraint(separators, pltpu.HBM)
     place = jnp.stack([even_core.astype(jnp.int32), panel, front])
     vector = (two, sources, width)
     shape = jax.ShapeDtypeStruct
@@ -490,13 +529,16 @@
         weights, traded_weights["A"], traded_weights["B"], first_plane, last_plane,
     )[0]
 
-    def gather(level_sums, panels, before):
+    def gather(level_sums, panels, before, first=False):
         own, quad, slab = level_sums
-        near = near_part(own, quad, slab, separators)
-        return (near, slab, *inside(slab.astype(BF), panels, 8, 16, 24), before, separators)
+        if first:
+            near, root = near_part(own, quad, slab, fetched)
+        else:
+            near, root = held_part(own, quad, slab, separators), root_matrix
+        return (near, slab, *inside(slab.astype(BF), panels, 8, 16, 24), before, root)
 
     def forward_close(level_sums, panels, target, which, before, parcel):
-        got = gather(level_sums, panels, before)
+        got = gather(level_sums, panels, before, target < 2)
         return whole_call(
             functools.partial(forward_kernel, target, which),
             [shape(vector, F32), shape(vector, BF), shape((2,) + vector, BF)], 200000000, "forward", 3,

time: 202 us -> 198 us (0.980)
  local copies, waits for them, and re-layouts: 17.7 us -> 8.76 us
  Pallas kernels: 37.1 us -> 42.2 us
  waiting for transfers between devices: 58 us -> 61.1 us
  starting transfers between devices: 82.6 us -> 79.6 us
    unnamed x48 -> x41, local copies, waits for them, and re-layouts: 15.6 us -> 6.62 us
    pallas_call x0 -> x2, Pallas kernels: none -> 4.41 us  [near_part(): pl.pallas_call(near_kernel, in_specs=[vmem, vmem, vmem, pl.BlockSpec(memo...]
    ppermute x64, waiting for transfers between devices: 58 us -> 61.1 us  [moved(): return lax.ppermute(block, AXES, route)]
    ppermute x64, starting transfers between devices: 82.6 us -> 79.6 us  [moved(): return lax.ppermute(block, AXES, route)]
    pallas_call x16 -> x14, Pallas kernels: 19.6 us -> 18.4 us  [whole_call(): pl.pallas_call(kernel, in_specs=[pl.BlockSpec(memory_space=space) for spa...]
  transfers between devices with their start and end apart: 64 -> 64, of which waited for: 42 -> 43; matrix products, arithmetic and copies ran while one was open for 2% -> 2% of each run, Pallas kernels for 9% -> 12%
where the time goes in v5:
time: 198 us
  starting transfers between devices  79.6 us (40%)
  waiting for transfers between devices  61.1 us (31%)
  Pallas kernels  42.2 us (21%)
  local copies, waits for them, and re-layouts  8.76 us (4%)
  other arithmetic  4.64 us (2%)
    ppermute x64, starting transfers between devices, moved(): return lax.ppermute(block, AXES, route)  79.6 us
    ppermute x64, waiting for transfers between devices, moved(): return lax.ppermute(block, AXES, route)  61.1 us
    pallas_call x14, Pallas kernels, whole_call(): pl.pallas_call(kernel, in_specs=[pl.BlockSpec(memory_space=space) for spa...  18.4 us
    pallas_call x1, Pallas kernels, finish(): pl.pallas_call(final_kernel, grid=(sources // step,), in_specs=[pl.BlockS...  10.8 us
    pallas_call x1, Pallas kernels, leaf_solve(): pl.pallas_call(leaf_kernel, grid=(sources // step,), in_specs=[pl.BlockSp...  8.68 us
    unnamed x41, local copies, waits for them, and re-layouts  6.62 us
    pallas_call x2, Pallas kernels, near_part(): pl.pallas_call(near_kernel, in_specs=[vmem, vmem, vmem, pl.BlockSpec(memo...  4.41 us
  transfers between devices with their start and end apart: 64, of which 43 were waited for; matrix products, arithmetic and copies ran while one was open for 2% of the time, Pallas kernels for 12%

profile of v5, /device:TPU:0, one launch (start us, length us, event | category | flops | bytes accessed | tf_op | source)
XLA Modules:
  0.0 197.5 jit_solution(2777094014278798625)
XLA Ops:
  1.3 4.1 %collective-permute-start.1 = (f32[2,8,8]{2,1,0:T(8,128)S(1)}, f32[2,8,8]{2,1,0:T(8,128)S(1)}, u32[]{:S(2)}, u32[]{:S(2)}) collective-permute-start(f32[2,8,8]{2,1,0:T(8,128)S(1)} %pad_maximum_fusion.14.weight_ref.own_ref.own_w_ref), channel_id=1, source_target_pairs={{0,96},{1,97},{2,98},{3,99},{4,100},{5,101},{6,102},{7,103},{8,104... | collective-permute-start | bytes 1544 | tf_op jit(solution)/shard_map/ppermute | solution.py:48
  5.5 2.1 %slice_bitcast_fusion.1 = (bf16[512,512]{1,0:T(8,128)(2,1)}, bf16[512,512]{1,0:T(8,128)(2,1)S(1)}) fusion(bf16[2,1,1,512,512]{4,3,2,1,0:T(8,128)(2,1)} %param.8), kind=kLoop, calls=%fused_computation.2 | loop fusion | bytes 2097152 | tf_op jit(solution)/shard_map/squeeze | solution.py:489
  7.5 1.6 collective-permute-done.by_a_ref.traded_ref.a_w_ref
  9.1 1.2 collective-permute-start.4
  10.3 1.2 copy-done.1
  11.6 8.7 %leaf_solve.1 = (f32[2,24,8,8,512]{4,3,2,1,0:T(8,128)}, bf16[2,24,512]{2,1,0:T(8,128)(2,1)S(1)}, bf16[2,24,8,512]{3,2,1,0:T(8,128)(2,1)S(1)}, bf16[2,24,8,512]{3...) custom-call(f32[2,8,8]{2,1,0:T(8,128)S(1)} %pad_maximum_fusion.14.weight_ref.own_ref.own_w_ref, ...), custom_call_target="tpu_custom_call" | custom-call | flops 65000000 | bytes 1600000 | tf_op jit(solution)/shard_map/leaf_solve/pallas_call | solution.py:113
  20.2 1.2 collective-permute-done.2
  21.5 1.1 collective-permute-done.4.leaf_real_ref.b_real_ref
  22.6 1.7 collective-permute-start.5
  24.2 2.9 %collective-permute-start.6 = (bf16[24,512]{1,0:T(8,128)(2,1)S(1)}, bf16[24,512]{1,0:T(8,128)(2,1)S(1)}, u32[]{:S(2)}, u32[]{:S(2)}) collective-permute-start(bf16[24,512]{1,0:T(8,128)(2,1)S(1)} %fusion.22), channel_id=1, source_target_pairs={{0,4},{1,5},{2,6},{3,7},{4,0},{5,1},{6,2},{7,3},{8,12},{9,13},{10,... | collective-permute-start | bytes 73736 | tf_op jit(solution)/shard_map/ppermute | solution.py:48
  27.1 2.5 %collective-permute-done.6 = bf16[24,512]{1,0:T(8,128)(2,1)S(1)} collective-permute-done((bf16[24,512]{1,0:T(8,128)(2,1)S(1)}, bf16[24,512]{1,0:T(8,128)(2,1)S(1)}, u32[]{:S(2)}, u32[]{:S(2)}) %collective-permute-start.6) | collective-permute-done | bytes 24608 | tf_op jit(solution)/shard_map/ppermute | solution.py:48
  29.8 1.9 collective-permute-start.12
  33.0 1.5 collective-permute-start.8
  34.5 2.7 %collective-permute-start.9 = (bf16[24,512]{1,0:T(8,128)(2,1)S(1)}, bf16[24,512]{1,0:T(8,128)(2,1)S(1)}, u32[]{:S(2)}, u32[]{:S(2)}) collective-permute-start(bf16[24,512]{1,0:T(8,128)(2,1)S(1)} %fusion.21), channel_id=1, source_target_pairs={{0,16},{1,17},{2,18},{3,19},{4,20},{5,21},{6,22},{7,23},{8,24},{9,... | collective-permute-start | bytes 73736 | tf_op jit(solution)/shard_map/ppermute | solution.py:48
  37.2 2.7 %collective-permute-done.9.opposite_ref = bf16[24,512]{1,0:T(8,128)(2,1)S(1)} collective-permute-done((bf16[24,512]{1,0:T(8,128)(2,1)S(1)}, bf16[24,512]{1,0:T(8,128)(2,1)S(1)}, u32[]{:S(2)}, u32[]{:S(2)}) %collective-permute-start.9) | collective-permute-done | bytes 24608 | tf_op jit(solution)/shard_map/ppermute | solution.py:48
  40.4 2.1 %edge_sums.1.sums_ref = f32[5,2,24,512]{3,2,1,0:T(8,128)S(1)} custom-call(f32[2,8,8]{2,1,0:T(8,128)S(1)} %pad_maximum_fusion.14.weight_ref.own_ref.own_w_ref, f32[2,8,8]{2,1,0:T(8,128)S(1)} %collective-permute-done.by_a_ref.traded_ref.a_w_ref, f32[2,8,8]{2,1,0:T(8,128)S(1)} %collective-permute-done.1.by_b_ref.traded_ref.b_w_ref, ...), custom_call_target="tpu_custom_call" | custom-call | flops 10000000 | bytes 50000 | tf_op jit(solution)/shard_map/edge_sums/pallas_call | solution.py:139
  42.5 0.9 copy-done.3
  43.4 0.9 copy-done.6
  44.3 2.2 %near_part.7 = (f32[2,24,512]{2,1,0:T(8,128)S(1)}, bf16[2,512,512]{2,1,0:T(8,128)(2,1)S(1)}) custom-call(f32[2,24,512]{2,1,0:T(8,128)S(1)} %convert_add_fusion.8.own_ref, f32[2,24,512]{2,1,0:T(8,128)S(1)} %copy-done.6, f32[2,24,512]{2,1,0:T(8,128)S(1)} %copy-done.3, bf16[2,4,512,512]{3,2,1,0:T(8,128)(2,1)} %bitcast.141), custom_call_target="tpu_custom_call" | custom-call | flops 150000000 | bytes 750000 | tf_op jit(solution)/shard_map/near_part/pallas_call | solution.py:174
  46.6 0.9 copy-done.4
  48.2 1.4 forward.3
  51.0 1.1 collective-permute-done.13
  52.8 3.7 %collective-permute-start.15 = (bf16[2,24,512]{2,1,0:T(8,128)(2,1)}, bf16[2,24,512]{2,1,0:T(8,128)(2,1)S(1)}, u32[]{:S(2)}, u32[]{:S(2)}) collective-permute-start(bf16[2,24,512]{2,1,0:T(8,128)(2,1)} %add_convert_fusion.5), channel_id=1, source_target_pairs={{0,36},{1,39},{2,38},{3,37},{4,32},{5,35},{6,34},{7,33},{8,44},{9,... | collective-permute-start | bytes 147464 | tf_op jit(solution)/shard_map/ppermute | solution.py:48
  57.2 2.4 %collective-permute-done.15 = bf16[2,24,512]{2,1,0:T(8,128)(2,1)S(1)} collective-permute-done((bf16[2,24,512]{2,1,0:T(8,128)(2,1)}, bf16[2,24,512]{2,1,0:T(8,128)(2,1)S(1)}, u32[]{:S(2)}, u32[]{:S(2)}) %collective-permute-start.15) | collective-permute-done | bytes 49184 | tf_op jit(solution)/shard_map/ppermute | solution.py:48
  59.6 1.3 collective-permute-done.14
  60.9 0.8 pad_maximum_fusion
  61.9 1.1 collective-permute-start.20
  63.1 1.0 fusion.31
  64.8 0.8 collective-permute-done.18.opposite_ref
  66.0 2.2 %near_part.8 = (f32[2,24,512]{2,1,0:T(8,128)S(1)}, bf16[2,512,512]{2,1,0:T(8,128)(2,1)S(1)}) custom-call(f32[2,24,512]{2,1,0:T(8,128)S(1)} %get-tuple-element.114.own_ref, f32[2,24,512]{2,1,0:T(8,128)S(1)} %get-tuple-element.113.quad_ref, f32[2,24,512]{2,1,0:T(8,128)S(1)} %get-tuple-element.99.slab_ref, bf16[2,4,512,512]{3,2,1,0:T(8,128)(2,1)} %bitcast.142), custom_call_target="tpu_custom_call" | custom-call | flops 150000000 | bytes 750000 | tf_op jit(solution)/shard_map/near_part/pallas_call | solution.py:174
  68.3 1.4 forward.4
  69.7 3.7 %collective-permute-done.20.by_a_ref = bf16[2,24,8,512]{3,2,1,0:T(8,128)(2,1)S(1)} collective-permute-done((bf16[2,24,8,512]{3,2,1,0:T(8,128)(2,1)S(1)}, bf16[2,24,8,512]{3,2,1,0:T(8,128)(2,1)S(1)}, u32[]{:S(2)}, u32[]{:S(2)}) %collective-permute-start.20) | collective-permute-done | bytes 393248 | tf_op jit(solution)/shard_map/ppermute | solution.py:48
  73.5 2.0 collective-permute-done.21.by_b_ref
  75.4 1.2 collective-permute-done.22
  78.8 1.0 collective-permute-done.25
  81.8 2.5 %planes.1 = (f32[2,24,8,512]{3,2,1,0:T(8,128)S(1)}, f32[2,24,8,512]{3,2,1,0:T(8,128)S(1)}, f32[2,24,8,512]{3,2,1,0:T(8,128)S(1)}, f32[2,24,8,512]{3,2,1,0:T(8,128)S(1)}) custom-call(s32[3]{0:T(128)S(1)} %pad_add_fusion.place_ref, bf16[2,24,8,512]{3,2,1,0:T(8,128)(2,1)S(1)} %collective-permute-done.20.by_a_ref, ...), custom_call_target="tpu_custom_call" | custom-call | flops 400000000 | bytes 2000000 | tf_op jit(solution)/shard_map/planes/pallas_call | solution.py:139
  85.0 1.4 forward.5
  86.8 0.9 collective-permute-done.29
  89.6 1.1 collective-permute-done.32
  91.4 18.8 %collective-permute-start.37 = (bf16[2,2,24,512]{3,2,1,0:T(8,128)(2,1)S(1)}, bf16[2,2,24,512]{3,2,1,0:T(8,128)(2,1)S(1)}, u32[]{:S(2)}, u32[]{:S(2)}) collective-permute-start(bf16[2,2,24,512]{3,2,1,0:T(8,128)(2,1)S(1)} %get-tuple-element.64.parcel_ref), channel_id=1, source_target_pairs={{0,96},{1,97},{2,98},{3,99},{4,100},{5,101},{6,102},{7,103},{8,104... | collective-permute-start | bytes 294920 | tf_op jit(solution)/shard_map/ppermute | solution.py:48
  111.0 1.8 collective-permute-done.37.by_b_ref.parcel_b_ref
  112.8 2.0 %collective-permute-done.36.by_a_ref.parcel_a_ref = bf16[2,2,24,512]{3,2,1,0:T(8,128)(2,1)S(1)} collective-permute-done((bf16[2,2,24,512]{3,2,1,0:T(8,128)(2,1)S(1)}, bf16[2,2,24,512]{3,2,1,0:T(8,128)(2,1)S(1)}, u32[]{:S(2)}, u32[]{:S(2)}) %collective-permute-start.36) | collective-permute-done | bytes 98336 | tf_op jit(solution)/shard_map/ppermute | solution.py:48
  114.8 1.4 backward.3
  116.3 1.2 collective-permute-done.38
  119.5 1.0 collective-permute-done.41
  121.1 1.0 collective-permute-done.43.opposite_ref
  123.5 1.4 backward.4
  125.1 1.1 collective-permute-done.45
  128.1 1.0 collective-permute-done.48
  129.7 1.0 collective-permute-done.50.opposite_ref
  132.1 1.4 backward.5
  133.9 1.1 collective-permute-done.52
  135.0 21.4 %collective-permute-start.54 = (bf16[2,24,512]{2,1,0:T(8,128)(2,1)S(1)}, bf16[2,24,512]{2,1,0:T(8,128)(2,1)S(1)}, u32[]{:S(2)}, u32[]{:S(2)}) collective-permute-start(bf16[2,24,512]{2,1,0:T(8,128)(2,1)S(1)} %add_convert_fusion), channel_id=1, source_target_pairs={{0,36},{1,39},{2,38},{3,37},{4,32},{5,35},{6,34},{7,33},{8,44},{9,... | collective-permute-start | bytes 147464 | tf_op jit(solution)/shard_map/ppermute | solution.py:48
  156.4 2.1 %collective-permute-done.54 = bf16[2,24,512]{2,1,0:T(8,128)(2,1)S(1)} collective-permute-done((bf16[2,24,512]{2,1,0:T(8,128)(2,1)S(1)}, bf16[2,24,512]{2,1,0:T(8,128)(2,1)S(1)}, u32[]{:S(2)}, u32[]{:S(2)}) %collective-permute-start.54) | collective-permute-done | bytes 49184 | tf_op jit(solution)/shard_map/ppermute | solution.py:48
  158.5 2.4 %collective-permute-done.53 = bf16[2,24,512]{2,1,0:T(8,128)(2,1)S(1)} collective-permute-done((bf16[2,24,512]{2,1,0:T(8,128)(2,1)S(1)}, bf16[2,24,512]{2,1,0:T(8,128)(2,1)S(1)}, u32[]{:S(2)}, u32[]{:S(2)}) %collective-permute-start.53) | collective-permute-done | bytes 49184 | tf_op jit(solution)/shard_map/ppermute | solution.py:48
  161.1 1.2 collective-permute-start.56
  162.3 4.1 %collective-permute-done.57.got_b_ref = bf16[2,24,512]{2,1,0:T(8,128)(2,1)S(1)} collective-permute-done((bf16[2,24,512]{2,1,0:T(8,128)(2,1)S(1)}, bf16[2,24,512]{2,1,0:T(8,128)(2,1)S(1)}, u32[]{:S(2)}, u32[]{:S(2)}) %collective-permute-start.57) | collective-permute-done | bytes 49184 | tf_op jit(solution)/shard_map/ppermute | solution.py:48
  167.1 2.3 %collective-permute-start.59 = (bf16[24,512]{1,0:T(8,128)(2,1)S(1)}, bf16[24,512]{1,0:T(8,128)(2,1)S(1)}, u32[]{:S(2)}, u32[]{:S(2)}) collective-permute-start(bf16[24,512]{1,0:T(8,128)(2,1)S(1)} %fusion.15), channel_id=1, source_target_pairs={{0,16},{1,17},{2,18},{3,19},{4,20},{5,21},{6,22},{7,23},{8,24},{9,... | collective-permute-start | bytes 73736 | tf_op jit(solution)/shard_map/ppermute | solution.py:48
  169.4 3.0 %collective-permute-done.59.opposite_ref = bf16[24,512]{1,0:T(8,128)(2,1)S(1)} collective-permute-done((bf16[24,512]{1,0:T(8,128)(2,1)S(1)}, bf16[24,512]{1,0:T(8,128)(2,1)S(1)}, u32[]{:S(2)}, u32[]{:S(2)}) %collective-permute-start.59) | collective-permute-done | bytes 24608 | tf_op jit(solution)/shard_map/ppermute | solution.py:48
  173.8 2.2 %closing.1 = (f32[2,24,512]{2,1,0:T(8,128)S(1)}, f32[2,9,24,512]{3,2,1,0:T(8,128)S(1)}, bf16[2,24,8,512]{3,2,1,0:T(8,128)(2,1)S(1)}, bf16[2,24,8,512]{3,2,1,0:T(8,128)(2,1)S(1)}) custom-call(s32[3]{0:T(128)S(1)} %pad_add_fusion.place_ref, f32[2,8,8]{2,1,0:T(8,128)S(1)} %pad_maximum_fusion.14.weight_ref.own_ref.own_w_ref, ...), custom_call_target="tpu_custom_call" | custom-call | flops 300000000 | bytes 1500000 | tf_op jit(solution)/shard_map/closing/pallas_call | solution.py:139
  176.2 2.9 %collective-permute-start.63 = (bf16[2,24,8,512]{3,2,1,0:T(8,128)(2,1)S(1)}, bf16[2,24,8,512]{3,2,1,0:T(8,128)(2,1)S(1)}, u32[]{:S(2)}, u32[]{:S(2)}) collective-permute-start(bf16[2,24,8,512]{3,2,1,0:T(8,128)(2,1)S(1)} %get-tuple-element.85), channel_id=1, source_target_pairs={{0,31},{1,2},{2,1},{3,4},{4,3},{5,6},{6,5},{7,8},{8,7},{9,10},{10,... | collective-permute-start | bytes 1179656 | tf_op jit(solution)/shard_map/ppermute | solution.py:48
  179.2 4.6 %collective-permute-done.61.late_ref = f32[2,24,512]{2,1,0:T(8,128)S(1)} collective-permute-done((f32[2,24,512]{2,1,0:T(8,128)S(1)}, f32[2,24,512]{2,1,0:T(8,128)S(1)}, u32[]{:S(2)}, u32[]{:S(2)}) %collective-permute-start.61) | collective-permute-done | bytes 98336 | tf_op jit(solution)/shard_map/ppermute | solution.py:48
  183.8 3.0 %collective-permute-done.63.far_ref = bf16[2,24,8,512]{3,2,1,0:T(8,128)(2,1)S(1)} collective-permute-done((bf16[2,24,8,512]{3,2,1,0:T(8,128)(2,1)S(1)}, bf16[2,24,8,512]{3,2,1,0:T(8,128)(2,1)S(1)}, u32[]{:S(2)}, u32[]{:S(2)}) %collective-permute-start.63) | collective-permute-done | bytes 393248 | tf_op jit(solution)/shard_map/ppermute | solution.py:48
  186.8 10.8 %finish.1 = (f32[2,24,8,8,512]{4,3,2,1,0:T(8,128)}, f32[2,24,8,8,512]{4,3,2,1,0:T(8,128)}) custom-call(s32[3]{0:T(128)S(1)} %pad_add_fusion.place_ref, f32[2,8,8]{2,1,0:T(8,128)S(1)} %pad_maximum_fusion.14.weight_ref.own_ref.own_w_ref, f32[2,8,8]{2,1,0:T(8,128)S(1)} %collective-permute-done.by_a_ref.traded_ref.a_w_ref, ...), custom_call_target="tpu_custom_call" | custom-call | flops 60000000 | bytes 26000000 | tf_op jit(solution)/shard_map/finish/pallas_call | solution.py:452
  (177 shorter events, 27.1 us)
Async XLA Ops:
  1.3 6.2 %collective-permute-start.1 = (f32[2,8,8]{2,1,0:T(8,128)S(1)}, f32[2,8,8]{2,1,0:T(8,128)S(1)}, u32[]{:S(2)}, u32[]{:S(2)}) collective-permute-start(f32[2,8,8]{2,1,0:T(8,128)S(1)} %pad_maximum_fusion.14.weight_ref.own_ref.own_w_ref), channel_id=1, source_target_pairs={{0,96},{1,97},{2,98},{3,99},{4,100},{5,101},{6,102},{7,103},{8,104... | collective-permute-start | bytes 1544 | tf_op jit(solution)/shard_map/ppermute | solution.py:48
  5.5 3.7 %collective-permute-start = (f32[2,8,8]{2,1,0:T(8,128)S(1)}, f32[2,8,8]{2,1,0:T(8,128)S(1)}, u32[]{:S(2)}, u32[]{:S(2)}) collective-permute-start(f32[2,8,8]{2,1,0:T(8,128)S(1)} %pad_maximum_fusion.14.weight_ref.own_ref.own_w_ref), channel_id=1, source_target_pairs={{0,32},{1,33},{2,34},{3,35},{4,36},{5,37},{6,38},{7,39},{8,40},{9,... | collective-permute-start | bytes 1544 | tf_op jit(solution)/shard_map/ppermute | solution.py:48
  9.1 13.4 %collective-permute-start.4 = (bf16[512,512]{1,0:T(8,128)(2,1)S(1)}, bf16[512,512]{1,0:T(8,128)(2,1)S(1)}, u32[]{:S(2)}, u32[]{:S(2)}) collective-permute-start(bf16[512,512]{1,0:T(8,128)(2,1)S(1)} %get-tuple-element.46), channel_id=1, source_target_pairs={{0,96},{1,97},{2,98},{3,99},{4,100},{5,101},{6,102},{7,103},{8,104... | collective-permute-start | bytes 1572872 | tf_op jit(solution)/shard_map/ppermute | solution.py:48
  10.3 12.2 %collective-permute-start.3 = (bf16[512,512]{1,0:T(8,128)(2,1)S(1)}, bf16[512,512]{1,0:T(8,128)(2,1)S(1)}, u32[]{:S(2)}, u32[]{:S(2)}) collective-permute-start(bf16[512,512]{1,0:T(8,128)(2,1)S(1)} %get-tuple-element.46), channel_id=1, source_target_pairs={{0,32},{1,33},{2,34},{3,35},{4,36},{5,37},{6,38},{7,39},{8,40},{9,... | collective-permute-start | bytes 1572872 | tf_op jit(solution)/shard_map/ppermute | solution.py:48
  20.2 1.2 collective-permute-start.2
  22.6 7.1 %collective-permute-start.5 = (bf16[2,24,512]{2,1,0:T(8,128)(2,1)S(1)}, bf16[2,24,512]{2,1,0:T(8,128)(2,1)S(1)}, u32[]{:S(2)}, u32[]{:S(2)}) collective-permute-start(bf16[2,24,512]{2,1,0:T(8,128)(2,1)S(1)} %convert_element_type.157), channel_id=1, source_target_pairs={{0,2},{1,7},{2,0},{3,5},{4,6},{5,3},{6,4},{7,1},{8,10},{9,15},{10,... | collective-permute-start | bytes 147464 | tf_op jit(solution)/shard_map/ppermute | solution.py:48
  24.2 5.4 %collective-permute-start.6 = (bf16[24,512]{1,0:T(8,128)(2,1)S(1)}, bf16[24,512]{1,0:T(8,128)(2,1)S(1)}, u32[]{:S(2)}, u32[]{:S(2)}) collective-permute-start(bf16[24,512]{1,0:T(8,128)(2,1)S(1)} %fusion.22), channel_id=1, source_target_pairs={{0,4},{1,5},{2,6},{3,7},{4,0},{5,1},{6,2},{7,3},{8,12},{9,13},{10,... | collective-permute-start | bytes 73736 | tf_op jit(solution)/shard_map/ppermute | solution.py:48
  29.7 2.6 %collective-permute-start.7 = (bf16[3,24,512]{2,1,0:T(8,128)(2,1)S(1)}, bf16[3,24,512]{2,1,0:T(8,128)(2,1)S(1)}, u32[]{:S(2)}, u32[]{:S(2)}) collective-permute-start(bf16[3,24,512]{2,1,0:T(8,128)(2,1)S(1)} %pad_maximum_fusion.6), channel_id=1, source_target_pairs={{0,1},{1,0},{2,3},{3,2},{4,5},{5,4},{6,7},{7,6},{8,9},{9,8},{10,11... | collective-permute-start | bytes 221192 | tf_op jit(solution)/shard_map/ppermute | solution.py:48
  29.8 21.1 %collective-permute-start.12 = (bf16[512,512]{1,0:T(8,128)(2,1)}, bf16[512,512]{1,0:T(8,128)(2,1)S(1)}, u32[]{:S(2)}, u32[]{:S(2)}) collective-permute-start(bf16[512,512]{1,0:T(8,128)(2,1)} %get-tuple-element.50), channel_id=1, source_target_pairs={{0,96},{1,97},{2,98},{3,99},{4,100},{5,101},{6,102},{7,103},{8,104... | collective-permute-start | bytes 1572872 | tf_op jit(solution)/shard_map/ppermute | solution.py:48
  31.7 14.9 %collective-permute-start.11 = (bf16[512,512]{1,0:T(8,128)(2,1)}, bf16[512,512]{1,0:T(8,128)(2,1)S(1)}, u32[]{:S(2)}, u32[]{:S(2)}) collective-permute-start(bf16[512,512]{1,0:T(8,128)(2,1)} %get-tuple-element.50), channel_id=1, source_target_pairs={{0,32},{1,33},{2,34},{3,35},{4,36},{5,37},{6,38},{7,39},{8,40},{9,... | collective-permute-start | bytes 1572872 | tf_op jit(solution)/shard_map/ppermute | solution.py:48
  33.0 6.9 %collective-permute-start.8 = (bf16[2,24,512]{2,1,0:T(8,128)(2,1)S(1)}, bf16[2,24,512]{2,1,0:T(8,128)(2,1)S(1)}, u32[]{:S(2)}, u32[]{:S(2)}) collective-permute-start(bf16[2,24,512]{2,1,0:T(8,128)(2,1)S(1)} %get-tuple-element.100), channel_id=1, source_target_pairs={{0,8},{1,25},{2,10},{3,27},{4,12},{5,29},{6,14},{7,31},{8,0},{9,17... | collective-permute-start | bytes 147464 | tf_op jit(solution)/shard_map/ppermute | solution.py:48
  34.5 5.4 %collective-permute-start.9 = (bf16[24,512]{1,0:T(8,128)(2,1)S(1)}, bf16[24,512]{1,0:T(8,128)(2,1)S(1)}, u32[]{:S(2)}, u32[]{:S(2)}) collective-permute-start(bf16[24,512]{1,0:T(8,128)(2,1)S(1)} %fusion.21), channel_id=1, source_target_pairs={{0,16},{1,17},{2,18},{3,19},{4,20},{5,21},{6,22},{7,23},{8,24},{9,... | collective-permute-start | bytes 73736 | tf_op jit(solution)/shard_map/ppermute | solution.py:48
  39.9 6.7 %collective-permute-start.10 = (bf16[3,24,512]{2,1,0:T(8,128)(2,1)S(1)}, bf16[3,24,512]{2,1,0:T(8,128)(2,1)S(1)}, u32[]{:S(2)}, u32[]{:S(2)}) collective-permute-start(bf16[3,24,512]{2,1,0:T(8,128)(2,1)S(1)} %pad_maximum_fusion.7), channel_id=1, source_target_pairs={{0,1},{1,0},{2,3},{3,2},{4,5},{5,4},{6,7},{7,6},{8,9},{9,8},{10,11... | collective-permute-start | bytes 221192 | tf_op jit(solution)/shard_map/ppermute | solution.py:48
  50.9 1.2 collective-permute-start.13
  52.8 6.8 %collective-permute-start.15 = (bf16[2,24,512]{2,1,0:T(8,128)(2,1)}, bf16[2,24,512]{2,1,0:T(8,128)(2,1)S(1)}, u32[]{:S(2)}, u32[]{:S(2)}) collective-permute-start(bf16[2,24,512]{2,1,0:T(8,128)(2,1)} %add_convert_fusion.5), channel_id=1, source_target_pairs={{0,36},{1,39},{2,38},{3,37},{4,32},{5,35},{6,34},{7,33},{8,44},{9,... | collective-permute-start | bytes 147464 | tf_op jit(solution)/shard_map/ppermute | solution.py:48
  56.5 4.4 %collective-permute-start.14 = (bf16[2,24,512]{2,1,0:T(8,128)(2,1)}, bf16[2,24,512]{2,1,0:T(8,128)(2,1)}, u32[]{:S(2)}, u32[]{:S(2)}) collective-permute-start(bf16[2,24,512]{2,1,0:T(8,128)(2,1)} %add_convert_fusion.5), channel_id=1, source_target_pairs={{0,32},{1,35},{2,34},{3,33},{4,36},{5,39},{6,38},{7,37},{8,40},{9,... | collective-permute-start | bytes 147464 | tf_op jit(solution)/shard_map/ppermute | solution.py:48
  61.7 1.4 collective-permute-start.16
  61.9 11.6 %collective-permute-start.20 = (bf16[2,24,8,512]{3,2,1,0:T(8,128)(2,1)S(1)}, bf16[2,24,8,512]{3,2,1,0:T(8,128)(2,1)S(1)}, u32[]{:S(2)}, u32[]{:S(2)}) collective-permute-start(bf16[2,24,8,512]{3,2,1,0:T(8,128)(2,1)S(1)} %get-tuple-element.60), channel_id=1, source_target_pairs={{0,32},{1,33},{2,34},{3,35},{4,36},{5,37},{6,38},{7,39},{8,40},{9,... | collective-permute-start | bytes 1179656 | tf_op jit(solution)/shard_map/ppermute | solution.py:48
  63.0 12.4 %collective-permute-start.21 = (bf16[2,24,8,512]{3,2,1,0:T(8,128)(2,1)S(1)}, bf16[2,24,8,512]{3,2,1,0:T(8,128)(2,1)S(1)}, u32[]{:S(2)}, u32[]{:S(2)}) collective-permute-start(bf16[2,24,8,512]{3,2,1,0:T(8,128)(2,1)S(1)} %get-tuple-element.61), channel_id=1, source_target_pairs={{0,96},{1,97},{2,98},{3,99},{4,100},{5,101},{6,102},{7,103},{8,104... | collective-permute-start | bytes 1179656 | tf_op jit(solution)/shard_map/ppermute | solution.py:48
  64.2 1.5 collective-permute-start.17
  64.4 1.2 collective-permute-start.18
  65.6 2.6 %collective-permute-start.19 = (bf16[3,24,512]{2,1,0:T(8,128)(2,1)S(1)}, bf16[3,24,512]{2,1,0:T(8,128)(2,1)S(1)}, u32[]{:S(2)}, u32[]{:S(2)}) collective-permute-start(bf16[3,24,512]{2,1,0:T(8,128)(2,1)S(1)} %pad_maximum_fusion.8), channel_id=1, source_target_pairs={{0,1},{1,0},{2,3},{3,2},{4,5},{5,4},{6,7},{7,6},{8,9},{9,8},{10,11... | collective-permute-start | bytes 221192 | tf_op jit(solution)/shard_map/ppermute | solution.py:48
  75.4 1.2 collective-permute-start.22
  76.7 1.3 collective-permute-start.24
  76.9 1.2 collective-permute-start.23
  78.2 1.6 collective-permute-start.25
  79.8 1.6 collective-permute-start.26
  80.3 1.2 collective-permute-start.27
  81.5 3.5 %collective-permute-start.28 = (bf16[3,24,512]{2,1,0:T(8,128)(2,1)S(1)}, bf16[3,24,512]{2,1,0:T(8,128)(2,1)S(1)}, u32[]{:S(2)}, u32[]{:S(2)}) collective-permute-start(bf16[3,24,512]{2,1,0:T(8,128)(2,1)S(1)} %pad_maximum_fusion.9), channel_id=1, source_target_pairs={{0,1},{1,0},{2,3},{3,2},{4,5},{5,4},{6,7},{7,6},{8,9},{9,8},{10,11... | collective-permute-start | bytes 221192 | tf_op jit(solution)/shard_map/ppermute | solution.py:48
  86.4 1.3 collective-permute-start.29
  87.7 1.3 collective-permute-start.31
  88.1 1.2 collective-permute-start.30
  89.4 1.4 collective-permute-start.32
  90.8 19.4 %collective-permute-start.33 = (bf16[2,24,512]{2,1,0:T(8,128)(2,1)S(1)}, bf16[2,24,512]{2,1,0:T(8,128)(2,1)S(1)}, u32[]{:S(2)}, u32[]{:S(2)}) collective-permute-start(bf16[2,24,512]{2,1,0:T(8,128)(2,1)S(1)} %get-tuple-element.94), channel_id=1, source_target_pairs={{0,1},{1,0},{2,3},{3,2},{4,5},{5,4},{6,7},{7,6},{8,9},{9,8},{10,11... | collective-permute-start | bytes 147464 | tf_op jit(solution)/shard_map/ppermute | solution.py:48
  91.1 19.1 %collective-permute-start.34 = (bf16[24,512]{1,0:T(8,128)(2,1)S(1)}, bf16[24,512]{1,0:T(8,128)(2,1)S(1)}, u32[]{:S(2)}, u32[]{:S(2)}) collective-permute-start(bf16[24,512]{1,0:T(8,128)(2,1)S(1)} %fusion.18), channel_id=1, source_target_pairs={{0,1},{1,0},{2,3},{3,2},{4,5},{5,4},{6,7},{7,6},{8,9},{9,8},{10,11... | collective-permute-start | bytes 73736 | tf_op jit(solution)/shard_map/ppermute | solution.py:48
  91.4 21.4 %collective-permute-start.37 = (bf16[2,2,24,512]{3,2,1,0:T(8,128)(2,1)S(1)}, bf16[2,2,24,512]{3,2,1,0:T(8,128)(2,1)S(1)}, u32[]{:S(2)}, u32[]{:S(2)}) collective-permute-start(bf16[2,2,24,512]{3,2,1,0:T(8,128)(2,1)S(1)} %get-tuple-element.64.parcel_ref), channel_id=1, source_target_pairs={{0,96},{1,97},{2,98},{3,99},{4,100},{5,101},{6,102},{7,103},{8,104... | collective-permute-start | bytes 294920 | tf_op jit(solution)/shard_map/ppermute | solution.py:48
  110.2 4.6 %collective-permute-start.36 = (bf16[2,2,24,512]{3,2,1,0:T(8,128)(2,1)S(1)}, bf16[2,2,24,512]{3,2,1,0:T(8,128)(2,1)S(1)}, u32[]{:S(2)}, u32[]{:S(2)}) collective-permute-start(bf16[2,2,24,512]{3,2,1,0:T(8,128)(2,1)S(1)} %get-tuple-element.72.parcel_ref), channel_id=1, source_target_pairs={{0,32},{1,33},{2,34},{3,35},{4,36},{5,37},{6,38},{7,39},{8,40},{9,... | collective-permute-start | bytes 294920 | tf_op jit(solution)/shard_map/ppermute | solution.py:48
  110.2 4.6 %collective-permute-start.35 = (bf16[3,24,512]{2,1,0:T(8,128)(2,1)S(1)}, bf16[3,24,512]{2,1,0:T(8,128)(2,1)S(1)}, u32[]{:S(2)}, u32[]{:S(2)}) collective-permute-start(bf16[3,24,512]{2,1,0:T(8,128)(2,1)S(1)} %pad_maximum_fusion.10), channel_id=1, source_target_pairs={{0,1},{1,0},{2,3},{3,2},{4,5},{5,4},{6,7},{7,6},{8,9},{9,8},{10,11... | collective-permute-start | bytes 221192 | tf_op jit(solution)/shard_map/ppermute | solution.py:48
  116.2 1.3 collective-permute-start.38
  117.5 1.3 collective-permute-start.40
  117.8 1.2 collective-permute-start.39
  119.0 1.4 collective-permute-start.41
  120.5 1.6 collective-permute-start.42
  120.9 1.2 collective-permute-start.43
  122.1 1.3 collective-permute-start.44
  124.8 1.3 collective-permute-start.45
  126.2 1.3 collective-permute-start.47
  126.4 1.2 collective-permute-start.46
  127.6 1.4 collective-permute-start.48
  129.1 1.6 collective-permute-start.49
  129.5 1.2 collective-permute-start.50
  130.7 1.3 collective-permute-start.51
  133.4 1.5 collective-permute-start.52
  135.0 23.5 %collective-permute-start.54 = (bf16[2,24,512]{2,1,0:T(8,128)(2,1)S(1)}, bf16[2,24,512]{2,1,0:T(8,128)(2,1)S(1)}, u32[]{:S(2)}, u32[]{:S(2)}) collective-permute-start(bf16[2,24,512]{2,1,0:T(8,128)(2,1)S(1)} %add_convert_fusion), channel_id=1, source_target_pairs={{0,36},{1,39},{2,38},{3,37},{4,32},{5,35},{6,34},{7,33},{8,44},{9,... | collective-permute-start | bytes 147464 | tf_op jit(solution)/shard_map/ppermute | solution.py:48
  156.4 4.5 %collective-permute-start.53 = (bf16[2,24,512]{2,1,0:T(8,128)(2,1)S(1)}, bf16[2,24,512]{2,1,0:T(8,128)(2,1)S(1)}, u32[]{:S(2)}, u32[]{:S(2)}) collective-permute-start(bf16[2,24,512]{2,1,0:T(8,128)(2,1)S(1)} %add_convert_fusion), channel_id=1, source_target_pairs={{0,32},{1,35},{2,34},{3,33},{4,36},{5,39},{6,38},{7,37},{8,40},{9,... | collective-permute-start | bytes 147464 | tf_op jit(solution)/shard_map/ppermute | solution.py:48
  160.9 1.4 collective-permute-start.55
  161.0 5.4 %collective-permute-start.57 = (bf16[2,24,512]{2,1,0:T(8,128)(2,1)S(1)}, bf16[2,24,512]{2,1,0:T(8,128)(2,1)S(1)}, u32[]{:S(2)}, u32[]{:S(2)}) collective-permute-start(bf16[2,24,512]{2,1,0:T(8,128)(2,1)S(1)} %convert_element_type.204), channel_id=1, source_target_pairs={{0,96},{1,97},{2,98},{3,99},{4,100},{5,101},{6,102},{7,103},{8,104... | collective-permute-start | bytes 147464 | tf_op jit(solution)/shard_map/ppermute | solution.py:48
  161.1 5.3 %collective-permute-start.56 = (bf16[2,24,512]{2,1,0:T(8,128)(2,1)S(1)}, bf16[2,24,512]{2,1,0:T(8,128)(2,1)S(1)}, u32[]{:S(2)}, u32[]{:S(2)}) collective-permute-start(bf16[2,24,512]{2,1,0:T(8,128)(2,1)S(1)} %convert_element_type.204), channel_id=1, source_target_pairs={{0,32},{1,33},{2,34},{3,35},{4,36},{5,37},{6,38},{7,39},{8,40},{9,... | collective-permute-start | bytes 147464 | tf_op jit(solution)/shard_map/ppermute | solution.py:48
  166.5 6.0 %collective-permute-start.58 = (bf16[2,24,512]{2,1,0:T(8,128)(2,1)S(1)}, bf16[2,24,512]{2,1,0:T(8,128)(2,1)S(1)}, u32[]{:S(2)}, u32[]{:S(2)}) collective-permute-start(bf16[2,24,512]{2,1,0:T(8,128)(2,1)S(1)} %convert_element_type.205), channel_id=1, source_target_pairs={{0,8},{1,25},{2,10},{3,27},{4,12},{5,29},{6,14},{7,31},{8,0},{9,17... | collective-permute-start | bytes 147464 | tf_op jit(solution)/shard_map/ppermute | solution.py:48
  167.1 5.3 %collective-permute-start.59 = (bf16[24,512]{1,0:T(8,128)(2,1)S(1)}, bf16[24,512]{1,0:T(8,128)(2,1)S(1)}, u32[]{:S(2)}, u32[]{:S(2)}) collective-permute-start(bf16[24,512]{1,0:T(8,128)(2,1)S(1)} %fusion.15), channel_id=1, source_target_pairs={{0,16},{1,17},{2,18},{3,19},{4,20},{5,21},{6,22},{7,23},{8,24},{9,... | collective-permute-start | bytes 73736 | tf_op jit(solution)/shard_map/ppermute | solution.py:48
  172.5 1.3 collective-permute-start.60
  176.0 7.8 %collective-permute-start.62 = (bf16[2,24,8,512]{3,2,1,0:T(8,128)(2,1)S(1)}, bf16[2,24,8,512]{3,2,1,0:T(8,128)(2,1)S(1)}, u32[]{:S(2)}, u32[]{:S(2)}) collective-permute-start(bf16[2,24,8,512]{3,2,1,0:T(8,128)(2,1)S(1)} %get-tuple-element.84), channel_id=1, source_target_pairs={{0,1},{1,0},{2,3},{3,2},{4,5},{5,4},{6,7},{7,6},{8,9},{9,8},{10,11... | collective-permute-start | bytes 1179656 | tf_op jit(solution)/shard_map/ppermute | solution.py:48
  176.2 10.5 %collective-permute-start.63 = (bf16[2,24,8,512]{3,2,1,0:T(8,128)(2,1)S(1)}, bf16[2,24,8,512]{3,2,1,0:T(8,128)(2,1)S(1)}, u32[]{:S(2)}, u32[]{:S(2)}) collective-permute-start(bf16[2,24,8,512]{3,2,1,0:T(8,128)(2,1)S(1)} %get-tuple-element.85), channel_id=1, source_target_pairs={{0,31},{1,2},{2,1},{3,4},{4,3},{5,6},{6,5},{7,8},{8,7},{9,10},{10,... | collective-permute-start | bytes 1179656 | tf_op jit(solution)/shard_map/ppermute | solution.py:48
  179.2 4.6 %collective-permute-start.61 = (f32[2,24,512]{2,1,0:T(8,128)S(1)}, f32[2,24,512]{2,1,0:T(8,128)S(1)}, u32[]{:S(2)}, u32[]{:S(2)}) collective-permute-start(f32[2,24,512]{2,1,0:T(8,128)S(1)} %get-tuple-element.83), channel_id=1, source_target_pairs={{0,32},{1,33},{2,34},{3,35},{4,36},{5,37},{6,38},{7,39},{8,40},{9,... | collective-permute-start | bytes 294920 | tf_op jit(solution)/shard_map/ppermute | solution.py:48
  (20 other events, 239.9 us)
